TPU v7x, 32 devices: a whole 2x2x4 slice. The times are simulated.
32 devices in a mesh: group: 2 (over x), det: 16 (over z, y, core).
Axes of the slice: x: 2, y: 2, z: 4, core: 2. Of those that a mesh axis runs over, the one named last changes fastest.
Arguments:
- science: float32 [2048, 4096], P(('group', 'det')), parts along dimension 0, may hold values from -6 to 6
- variance: float32 [2048, 4096], P(('group', 'det')), parts along dimension 0, may hold values from 0.5 to 18
- template_blocks: float32 [256, 2, 64, 256], P(('group', 'det')), parts along dimension 0, may hold values from -5 to 10.8, as said below
- requests: int32 [32, 16], P('group'), parts along dimension 0, may hold values from 0 to 127, as said below
- stamp_rows: int32 [32, 16], P(('group', 'det')), parts along dimension 0, may hold values from 26 to 38, as said below
- stamp_cols: int32 [32, 16], P(('group', 'det')), parts along dimension 0, may hold values from 26 to 4070, as said below
Outputs:
- decorrelated: float32 [2048, 4096], P(('group', 'det')), parts along dimension 0
- decorrelated_variance: float32 [2048, 4096], P(('group', 'det')), parts along dimension 0
There are 2 independent parts, one for each index of `group`. A program takes and returns all parts, laid end to end along the dimension named above; each array names one. Nothing has to cross between parts.
Inputs may be any that keep to these rules, and one draw needn't show every extreme that they name: `requests`: entries name template blocks as owner * 8 + block. The entries of a row that name one owner stand next to each other, 2 of them at most; one owner, drawn afresh, is named exactly 2 times in every row. `stamp_rows`: every row holds both ends of the range. `stamp_cols`: every row holds both ends of the range. `template_blocks`: plane 1 is positive.
All inputs are finite; a program needn't handle non-finite values.
Results may differ from a plain program's by a relative error of at most 0.0003.
Values sent between devices are 32-bit elements; how exact they have to be, the bound alone decides.
No kernel may reach another device: no remote copies, remote signals or barrier semaphores. Data moves between devices by JAX's collectives and lax.ppermute only.
A program may use at most 256 MiB of HBM per device.

v0:
```python
import math

import jax
import jax.numpy as jnp
import numpy as np
from jax import lax
from jax.sharding import PartitionSpec as P

CPER = 4
SS = 32
KS = 21
PD = 32


HIGHEST = lax.Precision.HIGHEST
GAUSS_WIDTHS = (0.7, 1.5, 3.0)
GAUSS_DEGREES = (4, 2, 2)


def extended(shard, sides, width):
    for axis, dim in sides:
        devices, length = (lax.axis_size(axis), shard.shape[dim])
        up = [(i, (i + 1) % devices) for i in range(devices - 1)]
        down = [(j, i) for i, j in up]
        last = lax.slice_in_dim(shard, length - width, length, axis=dim)
        initial = lax.slice_in_dim(shard, 0, width, axis=dim)
        before = lax.ppermute(last, axis, up)
        after = lax.ppermute(initial, axis, down)
        shard = jnp.concatenate([before, shard, after], axis=dim)
    return shard


def line_functions(kernel_taps):
    centre = kernel_taps // 2
    tap_grid = jnp.arange(kernel_taps).astype(jnp.float32) - centre
    raw_list = []
    for spread, degree in zip(GAUSS_WIDTHS, GAUSS_DEGREES):
        gaussian = jnp.exp(-tap_grid * tap_grid / (2.0 * spread * spread))
        for degree_power in range(degree + 1):
            raw_list.append(gaussian * tap_grid**degree_power)
    result = []
    for vector in raw_list:
        for earlier in result:
            vector = vector - jnp.sum(vector * earlier) * earlier
        result.append(vector / jnp.sqrt(jnp.sum(vector * vector)))
    return jnp.stack(result)


def pair_tables():
    first_index = []
    second_index = []
    offset_base = 0
    for degree in GAUSS_DEGREES:
        for outer in range(degree + 1):
            for inner in range(degree + 1 - outer):
                first_index.append(offset_base + outer)
                second_index.append(offset_base + inner)
        offset_base += degree + 1
    return (np.array(first_index), np.array(second_index))


def dft_tables(length):
    positions = jnp.arange(length)
    phase_steps = positions[:, None] * positions[None, :] % length
    angles = 2.0 * math.pi / length * phase_steps.astype(jnp.float32)
    return (jnp.cos(angles), jnp.sin(angles))


def sandwich(left_matrix, values_in, right_matrix):
    return jnp.einsum("ij,...jk,kl->...il", left_matrix, values_in, right_matrix, precision=HIGHEST)


def spectrum(values_in, cosine, sine):
    real_part = sandwich(cosine, values_in, cosine) - sandwich(sine, values_in, sine)
    imag_part = -(sandwich(sine, values_in, cosine) + sandwich(cosine, values_in, sine))
    return (real_part, imag_part)


def cut_squares(source, row_starts, col_starts, extent):

    def one_square(row_start, col_start):
        return lax.dynamic_slice(source, (row_start, col_start), (extent, extent))

    return jax.vmap(one_square)(row_starts, col_starts)


def stamp_system(science_strip, weight_plane, template_strip, centre_rows, centre_cols, line_basis):
    kernel_taps = line_basis.shape[1]
    margin = kernel_taps // 2
    functions = line_basis.shape[0]
    stamp_side = SS
    half_side = stamp_side // 2
    stamps_here = centre_rows.shape[0]
    row_starts = centre_rows - half_side
    col_starts = centre_cols - half_side
    science_stamp = cut_squares(science_strip, row_starts, col_starts, stamp_side)
    weight_stamp = cut_squares(weight_plane, row_starts, col_starts, stamp_side)
    extent = stamp_side + 2 * margin
    window = cut_squares(template_strip, row_starts - margin, col_starts - margin, extent)
    template_stamp = window[:, margin : margin + stamp_side, margin : margin + stamp_side]
    cosine, sine = dft_tables(stamp_side)
    science_re, science_im = spectrum(science_stamp, cosine, sine)
    template_re, template_im = spectrum(template_stamp, cosine, sine)
    cross_re = science_re * template_re + science_im * template_im
    cross_im = science_im * template_re - science_re * template_im
    magnitude = jnp.sqrt(cross_re * cross_re + cross_im * cross_im)
    floor_level = 0.25 * (jnp.mean(magnitude, axis=(1, 2), keepdims=True) + 1e-06)
    scaling = 1.0 / jnp.maximum(magnitude, floor_level)
    unit_re = cross_re * scaling
    unit_im = cross_im * scaling
    surface = (
        sandwich(cosine, unit_re, cosine)
        - sandwich(sine, unit_re, sine)
        - sandwich(cosine, unit_im, sine)
        - sandwich(sine, unit_im, cosine)
    ) / (stamp_side * stamp_side)
    quality = jnp.max(surface, axis=(1, 2))
    stamp_weight = jnp.maximum(quality, 0.1)
    offsets = jnp.arange(extent)[None, :] - jnp.arange(stamp_side)[:, None]
    selector = (offsets[None] == jnp.arange(kernel_taps)[:, None, None]).astype(jnp.float32)
    vertical = jnp.einsum("au,urp->arp", line_basis, selector, precision=HIGHEST).reshape(
        functions * stamp_side, extent
    )
    across = jnp.einsum("spq,mq->spm", window, vertical, precision=HIGHEST)
    both_ways = jnp.einsum("kp,spm->skm", vertical, across, precision=HIGHEST)
    stacked = both_ways.reshape(
        stamps_here, functions, stamp_side, functions, stamp_side
    ).transpose(1, 3, 0, 2, 4)
    first_index, second_index = pair_tables()
    images = stacked[first_index, second_index].reshape(
        len(first_index), stamps_here, stamp_side * stamp_side
    )
    target = (science_stamp - template_stamp).reshape(stamps_here, stamp_side * stamp_side)
    pixel_weight = stamp_weight[:, None] / weight_stamp.reshape(
        stamps_here, stamp_side * stamp_side
    )
    weighted = images * pixel_weight[None]
    normal = jnp.einsum("bsp,csp->bc", weighted, images, precision=HIGHEST)
    right_side = jnp.einsum("bsp,sp->b", weighted, target, precision=HIGHEST)
    return (normal, right_side)


def solve_system(normal, right_side):
    factor_lower = jnp.linalg.cholesky(normal)
    middle = lax.linalg.triangular_solve(
        factor_lower, right_side[:, None], left_side=True, lower=True
    )
    answer = lax.linalg.triangular_solve(
        factor_lower, middle, left_side=True, lower=True, transpose_a=True
    )
    return answer[:, 0]


def kernel_from(coefficients, line_basis):
    first_index, second_index = pair_tables()
    kernel_taps = line_basis.shape[1]
    margin = kernel_taps // 2
    spread_part = jnp.einsum(
        "b,bu,bv->uv",
        coefficients,
        line_basis[first_index],
        line_basis[second_index],
        precision=HIGHEST,
    )
    positions = jnp.arange(kernel_taps)
    impulse = ((positions[:, None] == margin) & (positions[None, :] == margin)).astype(jnp.float32)
    return spread_part + impulse


def decorrelation(kernel, mean_science, mean_template):
    kernel_taps = kernel.shape[0]
    margin = kernel_taps // 2
    placing = ((jnp.arange(kernel_taps)[None, :] - margin) % PD == jnp.arange(PD)[:, None]).astype(
        jnp.float32
    )
    placed = jnp.dot(jnp.dot(placing, kernel, precision=HIGHEST), placing.T, precision=HIGHEST)
    cosine, sine = dft_tables(PD)
    kernel_re, kernel_im = spectrum(placed, cosine, sine)
    response = jnp.sqrt(
        (mean_science + mean_template)
        / (mean_science + mean_template * (kernel_re * kernel_re + kernel_im * kernel_im))
    )
    spatial = (sandwich(cosine, response, cosine) - sandwich(sine, response, sine)) / (PD * PD)
    return jnp.dot(jnp.dot(placing.T, spatial, precision=HIGHEST), placing, precision=HIGHEST)


def correlate_strip(padded, kernel):
    kernel_taps = kernel.shape[0]
    margin = kernel_taps // 2
    height = padded.shape[0] - 2 * margin
    columns = padded.shape[1]
    tile_count = columns // 128
    widened = jnp.pad(padded, ((0, 0), (margin, 128 - margin)))
    leading = widened[:, :columns].reshape(-1, tile_count, 128)
    following = widened[:, 128 : columns + 128].reshape(-1, tile_count, 128)
    offsets = jnp.arange(256)[:, None] - jnp.arange(128)[None, :]
    selector = (offsets[None] == jnp.arange(kernel_taps)[:, None, None]).astype(jnp.float32)
    bands = jnp.einsum("uv,vpc->upc", kernel, selector, precision=HIGHEST)
    summed = jnp.zeros((height, tile_count, 128), jnp.float32)
    for tap_row in range(kernel_taps):
        first_part = jnp.einsum(
            "rtp,pc->rtc",
            leading[tap_row : tap_row + height],
            bands[tap_row, :128],
            precision=HIGHEST,
        )
        second_part = jnp.einsum(
            "rtp,pc->rtc",
            following[tap_row : tap_row + height],
            bands[tap_row, 128:],
            precision=HIGHEST,
        )
        summed = summed + first_part + second_part
    return summed.reshape(height, columns)


def per_device(science, variance, template_blocks, requests, stamp_rows, stamp_cols):
    height, columns = science.shape
    strips = lax.axis_size("det")
    device = lax.axis_index("det")
    detector = device // CPER
    needed = requests.shape[1]
    wanted = lax.dynamic_index_in_dim(requests, device, 0, keepdims=False)
    nothing = jnp.zeros((needed,) + template_blocks.shape[1:], jnp.float32)
    piece_rows = lax.all_gather(template_blocks, "det", axis=0, tiled=True)
    pick_number = piece_rows.shape[0]
    inside = (wanted >= 0) & (wanted < pick_number)
    chosen = jnp.take(piece_rows, jnp.clip(wanted, 0, pick_number - 1), axis=0)
    blocks = jnp.where(inside[:, None, None, None], chosen, nothing)
    template_image = jnp.concatenate([blocks[number, 0] for number in range(needed)], axis=1)
    template_variance = jnp.concatenate([blocks[number, 1] for number in range(needed)], axis=1)
    line_basis = line_functions(KS)
    margin = KS // 2
    padded_template = extended(template_image, (("det", 0),), margin)
    normal, right_side = stamp_system(
        science,
        variance + template_variance,
        template_image,
        stamp_rows[0],
        stamp_cols[0],
        line_basis,
    )
    variance_sums = jnp.stack([jnp.sum(variance), jnp.sum(template_variance)])
    detectors = strips // CPER
    ccd_slot = (jnp.arange(detectors) == detector).astype(jnp.float32)
    summed = lax.psum(
        (
            ccd_slot[:, None, None] * normal,
            ccd_slot[:, None] * right_side,
            ccd_slot[:, None] * variance_sums[None, :],
        ),
        "det",
    )
    normal = lax.dynamic_index_in_dim(summed[0], detector, 0, keepdims=False)
    right_side = lax.dynamic_index_in_dim(summed[1], detector, 0, keepdims=False)
    variance_sums = lax.dynamic_index_in_dim(summed[2], detector, 0, keepdims=False)
    pixels = CPER * height * columns
    mean_science = variance_sums[0] / pixels
    mean_template = variance_sums[1] / pixels
    coefficients = solve_system(normal, right_side)
    kernel = kernel_from(coefficients, line_basis)
    decorrelation_filter = decorrelation(kernel, mean_science, mean_template)
    difference = science - correlate_strip(padded_template, kernel)
    padded_difference = extended(difference, (("det", 0),), margin)
    decorrelated = correlate_strip(padded_difference, decorrelation_filter)
    kernel_power = jnp.sum(kernel * kernel)
    filter_power = jnp.sum(decorrelation_filter * decorrelation_filter)
    decorrelated_variance = filter_power * (variance + template_variance * kernel_power)
    return (decorrelated, decorrelated_variance)


def solution(mesh):
    placed = (
        P(("group", "det"), None),
        P(("group", "det"), None),
        P(("group", "det"), None, None, None),
        P("group", None),
        P(("group", "det"), None),
        P(("group", "det"), None),
    )
    return jax.shard_map(
        per_device,
        mesh=mesh,
        in_specs=placed,
        out_specs=(P(("group", "det"), None), P(("group", "det"), None)),
        check_vma=False,
    )
```

profile of v0, /device:TPU:1, one launch (start us, length us, event | category | flops | bytes accessed | tf_op | source)
XLA Modules:
  0.0 691.2 jit_solution(9693643947427465572)
XLA Ops:
  14.4 6.9 multiply_reduce_fusion.11
  25.6 10.0 %multiply_reduce_fusion.10 = (f32[]{:T(128)}, f32[]{:T(128)}, f32[]{:T(128)}, f32[]{:T(128)}, f32[]{:T(128)}, /*index=5*/f32[]{:T(128)}, f32[]{:T(128)}, f32[]{:...) fusion(f32[21]{0:T(128)S(1)} %get-tuple-element.164, ...), kind=kLoop, calls=%fused_computation.461 | loop fusion | flops 1273 | bytes 936 | tf_op jit(solution)/shard_map/reduce_sum | solution.py:44
  36.3 5.6 multiply_reduce_fusion.9
  46.4 7.7 %multiply_reduce_fusion.8 = (f32[]{:T(128)}, f32[]{:T(128)}, f32[]{:T(128)}, f32[]{:T(128)}, f32[]{:T(128)}, /*index=5*/f32[]{:T(128)}, f32[21]{0:T(128)S(1)}, f...) fusion(f32[21]{0:T(128)S(1)} %get-tuple-element.151, f32[21]{0:T(128)S(1)} %get-tuple-element.150, ...), kind=kLoop, calls=%fused_computation.457 | loop fusion | flops 708 | bytes 1244 | tf_op jit(solution)/shard_map/reduce_sum | solution.py:44
  54.8 4.5 multiply_reduce_fusion.7
  63.7 5.0 multiply_reduce_fusion.6
  69.3 3.0 multiply_reduce_fusion.5
  84.5 34.2 %subtract_divide_fusion = (f32[1,21]{1,0:T(1,128)S(1)}, f32[1,21]{1,0:T(1,128)S(1)}, f32[1,21]{1,0:T(1,128)S(1)}, f32[1,21]{1,0:T(1,128)S(1)}, f32[1,21]{1,0:T(1...) fusion(f32[]{:T(128)S(6)} %sqrt.49, ...), kind=kLoop, calls=%fused_computation.446 | loop fusion | flops 2919 | bytes 1104 | tf_op jit(solution)/shard_map/div | solution.py:45
  119.8 44.4 %while.4 = (s32[]{:T(128)}, f32[64,4096]{1,0:T(8,128)}, s32[16,2]{0,1:T(2,128)S(1)}, f32[16,32,32]{2,1,0:T(8,128)S(1)}, s32[]{:T(128)}) while((s32[]{:T(128)}, f32[64,4096]{1,0:T(8,128)}, s32[16,2]{0,1:T(2,128)S(1)}, f32[16,32,32]{2,1,0:T(8,128)S(1)}, s32[]{:T(128)}) %tuple.340), condition=%wide.while_cond.1, body=%wide.while_body.1.sunk | while | flops 2 | bytes 20589 | solution.py:82
  173.7 7.8 %gather_fusion = f32[16,2,64,256]{3,2,1,0:T(8,128)} fusion(f32[128,2,64,256]{3,2,1,0:T(8,128)} %all-gather.2.cloned.1.call-done, s32[1024]{0:T(1024)S(1)} %pad_clamp_fusion.2), kind=kCustom, calls=%fused_computation | custom fusion | bytes 4194368 | tf_op jit(solution)/shard_map/jit(_take)/gather | solution.py:228
  184.8 55.5 %while.3 = (s32[]{:T(128)}, f32[64,4096]{1,0:T(8,128)}, s32[16,2]{0,1:T(2,128)S(1)}, f32[16,52,52]{2,1,0:T(8,128)}, s32[]{:T(128)}) while((s32[]{:T(128)}, f32[64,4096]{1,0:T(8,128)}, s32[16,2]{0,1:T(2,128)S(1)}, f32[16,52,52]{2,1,0:T(8,128)}, s32[]{:T(128)}) %tuple.345), condition=%wide.while_cond, body=%wide.while_body.sunk | while | flops 2 | bytes 58977 | solution.py:82
  192.2 2.8 bitcast_dynamic-update-slice_fusion.6
  195.7 2.8 bitcast_dynamic-update-slice_fusion.6
  199.1 2.8 bitcast_dynamic-update-slice_fusion.6
  202.6 2.8 bitcast_dynamic-update-slice_fusion.6
  206.1 2.8 bitcast_dynamic-update-slice_fusion.6
  213.0 2.8 bitcast_dynamic-update-slice_fusion.6
  255.3 32.1 %while.5 = (s32[]{:T(128)}, f32[64,4096]{1,0:T(8,128)S(1)}, s32[16,2]{0,1:T(2,128)S(1)}, f32[16,32,32]{2,1,0:T(8,128)S(1)}, s32[]{:T(128)}) while((s32[]{:T(128)}, f32[64,4096]{1,0:T(8,128)S(1)}, s32[16,2]{0,1:T(2,128)S(1)}, f32[16,32,32]{2,1,0:T(8,128)S(1)}, s32[]{:T(128)}) %tuple.346), condition=%wide.while_cond.2, body=%wide.while_body.2.sunk | while | flops 2 | bytes 32877 | solution.py:82
  288.8 12.1 %convolution_bitcast_fusion = f32[16,352,352]{1,2,0:T(8,128)} fusion(f32[16,52,352]{2,1,0:T(8,128)S(1)} %fusion.293, f32[352,52,1]{1,0,2:T(8,128)S(1)} %bitcast.963), kind=kOutput, calls=%fused_computation.10 | convolution fusion | flops 1237057536 | bytes 9174528 | tf_op jit(solution)/shard_map/kp,spm->skm/dot_general | solution.py:125
  301.0 26.9 %reshape.1030 = f32[16,11,32,11,32]{2,1,4,3,0:T(8,128)} reshape(f32[16,352,352]{1,2,0:T(8,128)} %convolution_bitcast_fusion) | data formatting | bytes 15859712 | tf_op jit(solution)/shard_map/reshape | solution.py:126
  327.9 42.3 %copy.56 = f32[16,11,32,11,32]{4,2,0,3,1:T(8,128)} copy(f32[16,11,32,11,32]{2,1,4,3,0:T(8,128)} %reshape.1030) | data formatting | bytes 15859712 | tf_op jit(solution)/shard_map/reshape | solution.py:126
  370.2 14.0 %gather_fusion.1 = f32[27,16,32,32]{3,2,1,0:T(8,128)} fusion(f32[11,11,16,32,32]{4,3,2,1,0:T(8,128)} %bitcast.875, s32[27]{0:T(128)S(1)} %copy-done.74), kind=kCustom, calls=%fused_computation.1 | custom fusion | bytes 3539160 | tf_op jit(solution)/shard_map/gather | solution.py:130
  384.2 6.2 reshape.839
  392.1 3.9 fusion.12
  409.9 58.8 %all-reduce.2 = (f32[4,27,27]{1,2,0:T(8,128)S(1)}, f32[4,27]{1,0:T(4,128)S(1)}, f32[4,2]{1,0:T(4,128)S(1)}) all-reduce(f32[4,27,27]{1,2,0:T(8,128)S(1)} %broadcast_multiply_fusion.1, f32[4,27]{1,0:T(4,128)S(1)} %broadcast_multiply_fusion.3, f32[4,2]{1,0:T(4,128)S(1)} %broadcast_multiply_fusion.2), channel_id=1, replica_groups=mesh['group'=2,'det'=16] {'det'}, use_global_device_ids=true, to_apply=%region_68.69 | all-reduce | flops 3032 | bytes 24256 | tf_op jit(solution)/shard_map/psum | solution.py:246
  492.1 3.6 collective-permute-start
  495.7 4.7 collective-permute-start.1
  505.4 7.2 %slice_bitcast_fusion.61 = (f32[8,8,32,128]{3,1,2,0:T(8,128)}, f32[8,8,32,128]{3,1,2,0:T(8,128)}, f32[8,8,32,128]{3,1,2,0:T(8,128)}, f32[8,8,32,128]{3,1,2,0:T(8...) fusion(f32[84,4224]{1,0:T(8,128)S(1)} %select_maximum_fusion.2), kind=kLoop, calls=%fused_computation.199 | loop fusion | bytes 39845888
  512.6 6.8 slice_bitcast_fusion.42
  595.2 3.3 collective-permute-done.2
  600.6 7.2 %slice_bitcast_fusion.19 = (f32[8,8,32,128]{3,1,2,0:T(8,128)}, f32[8,8,32,128]{3,1,2,0:T(8,128)}, f32[8,8,32,128]{3,1,2,0:T(8,128)}, f32[8,8,32,128]{3,1,2,0:T(8...) fusion(f32[84,4224]{1,0:T(8,128)S(1)} %select_maximum_fusion), kind=kLoop, calls=%fused_computation.157 | loop fusion | bytes 39845888
  609.5 5.5 slice_bitcast_fusion
  (769 shorter events, 350.3 us)
Async XLA Ops:
  7.2 157.9 %copy-start.153 = (s32[27]{0:T(128)S(1)}, s32[27]{0:T(128)}, u32[]{:S(2)}) copy-start(s32[27]{0:T(128)} %constant.275) | copy-start | bytes 328
  7.2 157.9 %copy-start.154 = (s32[27]{0:T(128)S(1)}, s32[27]{0:T(128)}, u32[]{:S(2)}) copy-start(s32[27]{0:T(128)} %constant.276) | copy-start | bytes 328
  7.2 112.6 %copy-start.156 = (s32[1,16]{1,0:T(1,128)S(1)}, s32[1,16]{1,0:T(1,128)}, u32[]{:S(2)}) copy-start(s32[1,16]{1,0:T(1,128)} %param.18) | copy-start | bytes 196
  7.2 112.6 %copy-start.155 = (s32[1,16]{1,0:T(1,128)S(1)}, s32[1,16]{1,0:T(1,128)}, u32[]{:S(2)}) copy-start(s32[1,16]{1,0:T(1,128)} %param.19) | copy-start | bytes 196
  7.2 166.5 %all-gather.2.cloned.1.call-start = ((), (), s32[]{:S(2)}) async-start(), calls=%async_computation | async-start | bytes 17825792 | tf_op jit(solution)/shard_map/all_gather | solution.py:225
  242.2 6.5 copy-start.72
  242.3 6.5 copy-start.73
  251.7 2.7 copy-start.60
  254.4 33.2 %copy-start.68 = (f32[16,52,52]{2,1,0:T(8,128)S(1)}, f32[16,52,52]{2,1,0:T(8,128)}, u32[]{:S(2)}) copy-start(f32[16,52,52]{2,1,0:T(8,128)} %get-tuple-element.9) | copy-start | bytes 519172
  254.4 33.2 %copy-start.69 = (f32[11,32,52]{2,1,0:T(8,128)S(1)}, f32[11,32,52]{2,1,0:T(8,128)}, u32[]{:S(2)}) copy-start(f32[11,32,52]{2,1,0:T(8,128)} %copy.52) | copy-start | bytes 219652
  327.9 42.3 %copy-start.74 = (s32[27]{0:T(128)S(1)}, s32[27]{0:T(128)}, u32[]{:S(2)}) copy-start(s32[27]{0:T(128)} %constant.274) | copy-start | bytes 328
  384.2 6.2 copy-start.71
  396.0 78.9 %copy-start.151 = (f32[27,21]{1,0:T(8,128)S(1)}, f32[27,21]{1,0:T(8,128)}, u32[]{:S(2)}) copy-start(f32[27,21]{1,0:T(8,128)} %gather_fusion.2) | copy-start | bytes 6808
  396.0 78.9 %copy-start.152 = (f32[27,21]{1,0:T(8,128)S(1)}, f32[27,21]{1,0:T(8,128)}, u32[]{:S(2)}) copy-start(f32[27,21]{1,0:T(8,128)} %gather_fusion.3) | copy-start | bytes 6808
  396.1 78.9 %copy-start.157 = (pred[21]{0:T(512)(128)(4,1)S(1)}, pred[21]{0:T(512)(128)(4,1)}, u32[]{:S(2)}) copy-start(pred[21]{0:T(512)(128)(4,1)} %iota_compare_fusion.14) | copy-start | bytes 67
  396.1 84.1 %copy-start.67 = (f32[64,4096]{1,0:T(8,128)S(1)}, f32[64,4096]{1,0:T(8,128)}, u32[]{:S(2)}) copy-start(f32[64,4096]{1,0:T(8,128)} %get-tuple-element.537) | copy-start | bytes 3145732
  488.4 11.9 %copy-start.61 = (f32[64,4096]{1,0:T(8,128)S(1)}, f32[64,4096]{1,0:T(8,128)}, u32[]{:S(2)}) copy-start(f32[64,4096]{1,0:T(8,128)} %param.15) | copy-start | bytes 3145732
  492.1 11.5 %collective-permute-start = (f32[10,4096]{1,0:T(8,128)S(1)}, f32[10,4096]{1,0:T(8,128)S(1)}, u32[]{:S(2)}, u32[]{:S(2)}) collective-permute-start(f32[10,4096]{1,0:T(8,128)S(1)} %get-tuple-element.378), channel_id=1, source_target_pairs={{0,1},{1,2},{2,3},{3,4},{4,5},{5,6},{6,7},{7,8},{8,9},{9,10},{10,1... | collective-permute-start | bytes 491528 | tf_op jit(solution)/shard_map/ppermute | solution.py:27
  495.7 8.0 %collective-permute-start.1 = (f32[10,4096]{1,0:T(8,128)S(1)}, f32[10,4096]{1,0:T(8,128)S(1)}, u32[]{:S(2)}, u32[]{:S(2)}) collective-permute-start(f32[10,4096]{1,0:T(8,128)S(1)} %get-tuple-element.379), channel_id=1, source_target_pairs={{1,0},{2,1},{3,2},{4,3},{5,4},{6,5},{7,6},{8,7},{9,8},{10,9},{11,1... | collective-permute-start | bytes 491528 | tf_op jit(solution)/shard_map/ppermute | solution.py:28
  522.6 1.4 copy-start.58
  523.7 1.3 copy-start.57
  525.0 1.3 copy-start.55
  526.3 1.3 copy-start.51
  527.6 1.3 copy-start.47
  544.3 2.0 copy-start.147
  572.6 1.5 copy-start.120
  584.0 1.9 copy-start.109
  589.8 8.7 %collective-permute-start.2 = (f32[10,4096]{1,0:T(8,128)S(1)}, f32[10,4096]{1,0:T(8,128)S(1)}, u32[]{:S(2)}, u32[]{:S(2)}) collective-permute-start(f32[10,4096]{1,0:T(8,128)S(1)} %get-tuple-element.374), channel_id=1, source_target_pairs={{0,1},{1,2},{2,3},{3,4},{4,5},{5,6},{6,7},{7,8},{8,9},{9,10},{10,1... | collective-permute-start | bytes 491528 | tf_op jit(solution)/shard_map/ppermute | solution.py:27
  592.4 7.7 %collective-permute-start.3 = (f32[10,4096]{1,0:T(8,128)S(1)}, f32[10,4096]{1,0:T(8,128)S(1)}, u32[]{:S(2)}, u32[]{:S(2)}) collective-permute-start(f32[10,4096]{1,0:T(8,128)S(1)} %get-tuple-element.375), channel_id=1, source_target_pairs={{1,0},{2,1},{3,2},{4,3},{5,4},{6,5},{7,6},{8,7},{9,8},{10,9},{11,1... | collective-permute-start | bytes 491528 | tf_op jit(solution)/shard_map/ppermute | solution.py:28
  618.9 1.4 copy-start.52
  638.7 2.0 copy-start.148
  642.7 1.4 copy-start.107
  (131 other events, 150.1 us)
Sparse Core Ops, SparseCore 0:
  10.2 129.5 all-gather.1
where the time goes:
time: 702 us; the launch traced here: 691 us
  local copies, waits for them, and re-layouts  328 us (47%)
  matrix products  127 us (18%)
  other arithmetic  122 us (17%)
  blocking collectives  58.8 us (8%)
  between operations  36.4 us (5%)
  starting transfers between devices  12.7 us (2%)
    gather x144, local copies, waits for them, and re-layouts  132 us
    unnamed x424, local copies, waits for them, and re-layouts  83.1 us
    reshape x2, local copies, waits for them, and re-layouts, stamp_system(): both_ways.reshape(stamps_here, functions, stamp_side, functions, stamp_side)  69.2 us
    reduce_sum x19, other arithmetic, line_functions(): vector = vector - jnp.sum(vector * earlier) * earlier  59 us
    psum x1, blocking collectives, per_device(): lax.psum((ccd_slot[:, None, None] * normal, ccd_slot[:, None] * right_sid...  58.8 us
    dot_general x42, matrix products, correlate_strip(): jnp.einsum('rtp,pc->rtc', following[tap_row:tap_row + height], bands[tap_...  42.5 us
    dot_general x42, matrix products, correlate_strip(): jnp.einsum('rtp,pc->rtc', leading[tap_row:tap_row + height], bands[tap_ro...  41.8 us
    div x2, other arithmetic, line_functions(): result.append(vector / jnp.sqrt(jnp.sum(vector * vector)))  34.3 us
  transfers between devices with their start and end apart: 5, of which 2 were waited for; matrix products, arithmetic and copies ran while one was open for 23% of the time, Pallas kernels for 0%

commit v1 on v0

v1 whole, which is shorter than its diff:
```python
import functools

import jax
import jax.numpy as jnp
import numpy as np
from jax import lax
from jax.experimental import pallas as pl
from jax.experimental.pallas import tpu as pltpu
from jax.sharding import PartitionSpec as P

CPER = 4
SS = 32
KS = 21
PD = 32
MARGIN = KS // 2
HALO = 16
EXTENT = SS + 2 * MARGIN

HIGHEST = lax.Precision.HIGHEST
GAUSS_WIDTHS = (0.7, 1.5, 3.0)
GAUSS_DEGREES = (4, 2, 2)
VMEM_LIMIT = 60 * 1024 * 1024
VMEM = pltpu.MemorySpace.VMEM
SMEM = pltpu.MemorySpace.SMEM


def line_functions():
    tap_grid = np.arange(KS, dtype=np.float64) - MARGIN
    raw_list = []
    for spread, degree in zip(GAUSS_WIDTHS, GAUSS_DEGREES):
        gaussian = np.exp(-tap_grid * tap_grid / (2.0 * spread * spread))
        for degree_power in range(degree + 1):
            raw_list.append(gaussian * tap_grid**degree_power)
    result = []
    for vector in raw_list:
        for earlier in result:
            vector = vector - np.sum(vector * earlier) * earlier
        result.append(vector / np.sqrt(np.sum(vector * vector)))
    return np.stack(result)


def images_by_across():
    groups = []
    base = 0
    for degree in GAUSS_DEGREES:
        for inner in range(degree + 1):
            groups.append((base + inner, [base + outer for outer in range(degree + 1 - inner)]))
        base += degree + 1
    return groups


LINE = line_functions()
GROUPS = images_by_across()
PAIRS = [(a, b) for b, downs in GROUPS for a in downs]
NB = len(PAIRS)
NFUN = LINE.shape[0]
WROWS = 56


def block_diag(matrix, times):
    rows, cols = matrix.shape
    out = np.zeros((rows * times, cols * times))
    for k in range(times):
        out[k * rows : (k + 1) * rows, k * cols : (k + 1) * cols] = matrix
    return out


def across_table():
    table = np.zeros((256, NFUN * 128))
    for b in range(NFUN):
        for k in range(4):
            for c in range(SS):
                table[64 * k + c : 64 * k + c + KS, b * 128 + 32 * k + c] = LINE[b]
    return table.astype(np.float32)


def down_table():
    table = np.zeros((NB * SS, WROWS))
    for image, (a, _) in enumerate(PAIRS):
        for r in range(SS):
            table[image * SS + r, r : r + KS] = LINE[a]
    return table.astype(np.float32)


def dft_blocks():
    grid = np.outer(np.arange(SS), np.arange(SS)) % SS
    c, s = np.cos(2 * np.pi * grid / SS), np.sin(2 * np.pi * grid / SS)
    c, s = block_diag(c, 4), block_diag(s, 4)
    ones = block_diag(np.ones((SS, SS)), 4)
    left = np.concatenate([c, s], 0)
    right = np.block([[c, -s], [-s, -c]])
    back_left = np.block([[c, -s], [s, c]])
    back_right = np.concatenate([c, -s], 0) / (SS * SS)
    return [x.astype(np.float32) for x in (left, right, back_left, back_right, ones)]


def basis_tables():
    lv, lu = np.zeros((32, 32)), np.zeros((32, 128))
    for image, (a, b) in enumerate(PAIRS):
        lv[:KS, image] = LINE[b]
        lu[image, :KS] = LINE[a]
    return lv.astype(np.float32), lu.astype(np.float32)


def filter_tables():
    grid = np.outer(np.arange(PD), np.arange(KS) - MARGIN)
    c, s = np.zeros((PD, 32)), np.zeros((PD, 32))
    c[:, :KS], s[:, :KS] = np.cos(2 * np.pi * grid / PD), np.sin(2 * np.pi * grid / PD)
    cr, sr = np.zeros((128, 128)), np.zeros((128, 128))
    cr[:32, :PD], sr[:32, :PD] = c.T, s.T
    left = np.concatenate([c, s], 0)
    right = np.block([[cr, -sr], [-sr, -cr]])
    back_left = np.concatenate([c.T, s.T], 0) / (PD * PD)
    back_c, back_s = np.zeros((128, 128)), np.zeros((128, 128))
    back_c[:PD, :32], back_s[:PD, :32] = c, s
    back_right = np.concatenate([back_c, -back_s], 0)
    return [x.astype(np.float32) for x in (left, right, back_left, back_right)]


def pick_kernel(picks, source, out, sem):
    count = out.shape[0]

    def copy(k):
        return pltpu.make_async_copy(source.at[picks[k]], out.at[k], sem.at[k])

    def start(k, carry):
        copy(k).start()
        return carry

    def finish(k, carry):
        copy(k).wait()
        return carry

    lax.fori_loop(0, count, start, 0)
    lax.fori_loop(0, count, finish, 0)


def pick(picks, source):
    count = picks.shape[0]
    return pl.pallas_call(
        pick_kernel,
        out_shape=jax.ShapeDtypeStruct((count,) + source.shape[1:], source.dtype),
        in_specs=[pl.BlockSpec(memory_space=SMEM), pl.BlockSpec(memory_space=VMEM)],
        out_specs=pl.BlockSpec(memory_space=pl.ANY),
        scratch_shapes=[pltpu.SemaphoreType.DMA((count,))],
        compiler_params=pltpu.CompilerParams(vmem_limit_bytes=VMEM_LIMIT),
        name="pick_blocks",
    )(picks, source)


def lay_kernel(needed, width, slots, received, image, variance, sem):
    def copies(j):
        k = slots[j]
        columns = pl.ds(j * width, width)
        return [
            pltpu.make_async_copy(received.at[k, 0], image.at[:, columns], sem.at[0, j]),
            pltpu.make_async_copy(received.at[k, 1], variance.at[:, columns], sem.at[1, j]),
        ]

    for j in range(needed):
        for copy in copies(j):
            copy.start()
    for j in range(needed):
        for copy in copies(j):
            copy.wait()


def lay_strip(slots, received):
    needed = slots.shape[0]
    _, _, rows, width = received.shape
    shape = jax.ShapeDtypeStruct((rows, needed * width), received.dtype)
    return pl.pallas_call(
        functools.partial(lay_kernel, needed, width),
        out_shape=[shape, shape],
        in_specs=[pl.BlockSpec(memory_space=SMEM), pl.BlockSpec(memory_space=pl.ANY)],
        out_specs=[pl.BlockSpec(memory_space=VMEM)] * 2,
        scratch_shapes=[pltpu.SemaphoreType.DMA((2, needed))],
        compiler_params=pltpu.CompilerParams(vmem_limit_bytes=VMEM_LIMIT),
        name="lay_strip",
    )(slots, received)


def dot(a, b, contract=((1,), (0,))):
    return lax.dot_general(
        a, b, (contract, ((), ())), precision=HIGHEST, preferred_element_type=jnp.float32
    )


def split(x):
    high = x.astype(jnp.bfloat16)
    return high, (x - high.astype(jnp.float32)).astype(jnp.bfloat16)


def stamp_kernel(
    stamp_rows,
    stamp_cols,
    science,
    variance,
    template,
    template_variance,
    across_ref,
    down_ref,
    left_ref,
    right_ref,
    back_left_ref,
    back_right_ref,
    ones_ref,
    out,
    images,
    flat_x,
    flat_y,
):
    height, columns = science.shape
    stamps = stamp_rows.shape[0]
    groups = stamps // 4
    lane = lax.broadcasted_iota(jnp.int32, (1, 256), 1)

    windows, sciences, templates, weights = [], [], [], []
    for g in range(groups):
        window = sci = tmp = wgt = None
        for k in range(4):
            row = stamp_rows[g * 4 + k] - (SS // 2 + MARGIN)
            col = stamp_cols[g * 4 + k] - (SS // 2 + MARGIN)
            base = jnp.minimum(col // 128 * 128, columns - 256)
            base = pl.multiple_of(base, 128)
            off = col - base
            cols = pl.ds(base, 256)
            t = template[:, cols]
            s = science[:, cols]
            w = variance[:, cols] + template_variance[:, cols]
            up = lax.rem(height - row, height)
            up_in = height - row - MARGIN
            to64 = lax.rem(64 * k - off + 256, 256)
            to32 = lax.rem(32 * k - off - MARGIN + 512, 256)
            tw = pltpu.roll(pltpu.roll(t, to64, 1), up, 0)[:WROWS]

            def inner(x):
                return pltpu.roll(pltpu.roll(x, to32, 1)[:, :128], up_in, 0)[:SS]

            t, s, w = inner(t), inner(s), inner(w)
            if k == 0:
                window, sci, tmp, wgt = tw, s, t, w
            else:
                window = jnp.where(lane // 64 == k, tw, window)
                here = lane[:, :128] // 32 == k
                sci = jnp.where(here, s, sci)
                tmp = jnp.where(here, t, tmp)
                wgt = jnp.where(here, w, wgt)
        windows.append(window)
        sciences.append(sci)
        templates.append(tmp)
        weights.append(wgt)

    across = dot(jnp.concatenate(windows, 0), across_ref[...])
    row = 0
    for b, downs in GROUPS:
        piece = jnp.concatenate(
            [across[g * WROWS : (g + 1) * WROWS, b * 128 : (b + 1) * 128] for g in range(groups)], 1
        )
        count = len(downs) * SS
        made = dot(down_ref[row : row + count, :], piece)
        for g in range(groups):
            images[g, row : row + count, :] = made[:, g * 128 : (g + 1) * 128]
        row += count

    sci = jnp.concatenate(sciences, 0)
    tmp = jnp.concatenate(templates, 0)
    side = groups * SS
    first = dot(left_ref[...], jnp.concatenate([sci, tmp], 1))
    first = jnp.concatenate(
        [
            jnp.concatenate([first[:side, :128], first[side:, :128]], 1),
            jnp.concatenate([first[:side, 128:], first[side:, 128:]], 1),
        ],
        0,
    )
    second = dot(first, right_ref[...])
    sre, sim = second[:side, :128], second[:side, 128:]
    tre, tim = second[side:, :128], second[side:, 128:]
    cross_re = sre * tre + sim * tim
    cross_im = sim * tre - sre * tim
    magnitude = jnp.sqrt(cross_re * cross_re + cross_im * cross_im)
    mean = dot(dot(ones_ref[...], magnitude), ones_ref[...]) * (1.0 / (SS * SS))
    scaling = 1.0 / jnp.maximum(magnitude, 0.25 * (mean + 1e-06))
    unit = jnp.concatenate([cross_re * scaling, cross_im * scaling], 0)
    back = dot(back_left_ref[...], unit)
    surface = dot(jnp.concatenate([back[:side], back[side:]], 1), back_right_ref[...])
    narrow = lane[:, :128]
    target, pixel_weight = [], []
    for g in range(groups):
        best = jnp.max(surface[g * SS : (g + 1) * SS], axis=0, keepdims=True)
        best = jnp.broadcast_to(best, (8, 128))
        for step in (1, 2, 4, 8, 16):
            partner = jnp.where(
                narrow // step % 2 == 0,
                pltpu.roll(best, 128 - step, 1),
                pltpu.roll(best, step, 1),
            )
            best = jnp.maximum(best, partner)
        stamp_weight = jnp.maximum(best[:1], 0.1)
        pixel_weight.append(stamp_weight / weights[g])
        target.append(sciences[g] - templates[g])
    wide = groups * 128
    for g in range(groups):
        images[g, NB * SS : (NB + 1) * SS, :] = target[g]
        images[g, (NB + 1) * SS :, :] = jnp.zeros(((31 - NB) * SS, 128), jnp.float32)
    pixel_weight = jnp.concatenate(pixel_weight, 1)

    for r in range(SS):
        x = jnp.concatenate([images[g, pl.ds(r, 32, stride=SS), :] for g in range(groups)], 1)
        y = x * pixel_weight[r : r + 1, :]
        at = slice(r * wide, (r + 1) * wide)
        for value, ref in ((x, flat_x), (y, flat_y)):
            high = value.astype(jnp.bfloat16).astype(jnp.float32)
            ref[:, at] = jnp.concatenate([high, value - high], 0).astype(jnp.bfloat16)
    gram = lax.dot_general(
        flat_y[...], flat_x[...], (((1,), (1,)), ((), ())), preferred_element_type=jnp.float32
    )
    gram = gram[:32] + gram[32:]
    gram = gram + pltpu.roll(jnp.concatenate([gram, jnp.zeros((32, 64), jnp.float32)], 1), 96, 1)[:, :64]
    total = jnp.sum(jnp.sum(variance[...], axis=0, keepdims=True), axis=1, keepdims=True)
    total_t = jnp.sum(jnp.sum(template_variance[...], axis=0, keepdims=True), axis=1, keepdims=True)
    out[:32, :] = jnp.concatenate([gram, jnp.zeros((32, 64), jnp.float32)], 1)
    out[32:, :] = jnp.broadcast_to(jnp.where(narrow == 0, total, total_t), (8, 128))


def stamp_system(rows, cols, science, variance, template, template_variance):
    stamps = rows.shape[0]
    wide = stamps // 4 * 128
    tables = [across_table(), down_table(), *dft_blocks()]
    return pl.pallas_call(
        stamp_kernel,
        out_shape=jax.ShapeDtypeStruct((40, 128), jnp.float32),
        in_specs=[pl.BlockSpec(memory_space=SMEM)] * 2 + [pl.BlockSpec(memory_space=VMEM)] * 11,
        out_specs=pl.BlockSpec(memory_space=VMEM),
        scratch_shapes=[
            pltpu.VMEM((stamps // 4, 32 * SS, 128), jnp.float32),
            pltpu.VMEM((64, SS * wide), jnp.bfloat16),
            pltpu.VMEM((64, SS * wide), jnp.bfloat16),
        ],
        compiler_params=pltpu.CompilerParams(vmem_limit_bytes=VMEM_LIMIT),
        name="stamp_system",
    )(rows, cols, science, variance, template, template_variance, *[jnp.asarray(t) for t in tables])


def eliminate(a):
    row_index = lax.broadcasted_iota(jnp.int32, (32, 1), 0)
    for k in range(NB):
        pivot_row = a[k : k + 1, :]
        pivot_row = pivot_row / pivot_row[:, k : k + 1]
        column = a[:, k : k + 1] - (row_index == k).astype(jnp.float32)
        a = a - column * pivot_row
    return jnp.where(row_index < NB, a[:, NB : NB + 1], 0.0)


def widen(x):
    return jnp.concatenate([x, jnp.zeros((x.shape[0], 128 - x.shape[1]), jnp.float32)], 1)


def total_of(x):
    return jnp.sum(jnp.sum(x, axis=0, keepdims=True), axis=1, keepdims=True)


def correlate(kernel_t, before, own, after, stack, bands, products, out, science, column_chunk):
    height, columns = own.shape
    reach = height + 2 * MARGIN
    pad = 128
    lead = HALO - MARGIN
    for c in range(0, columns, column_chunk):
        at = slice(c, c + column_chunk)
        rows = jnp.concatenate([before[:, at], own[:, at], after[:, at]], 0)[lead : lead + reach]
        high = rows.astype(jnp.bfloat16).astype(jnp.float32)
        rest = jnp.zeros((256 - 3 * reach, column_chunk), jnp.float32)
        stack[:, at] = jnp.concatenate([high, rows - high, high, rest], 0).astype(jnp.bfloat16)
    high = kernel_t.astype(jnp.bfloat16).astype(jnp.float32)
    low = kernel_t - high
    blank = jnp.zeros_like(high)
    high, low = jnp.concatenate([high, blank], 1), jnp.concatenate([low, blank], 1)
    taps = high + pltpu.roll(high, reach, 1) + pltpu.roll(low, 2 * reach, 1)
    for v in range(KS):
        band = jnp.broadcast_to(taps[v : v + 1, :], (height, 256))
        band = pltpu.roll(band, 0, 1, stride=1, stride_axis=0)
        bands[v * height : (v + 1) * height, :] = band.astype(jnp.bfloat16)
    products[:, columns:] = jnp.zeros((KS * height, pad), jnp.float32)
    for c in range(0, columns, column_chunk):
        at = slice(c, c + column_chunk)
        products[:, at] = jnp.dot(bands[...], stack[:, at], preferred_element_type=jnp.float32)

    def finish(g, carry):
        at = pl.multiple_of(g * 8, 8)
        total = products[pl.ds((KS - 1) * height + at, 8), :]
        for v in range(KS - 2, -1, -1):
            total = pltpu.roll(total, columns + pad - 1, 1) + products[pl.ds(v * height + at, 8), :]
        total = pltpu.roll(total, MARGIN, 1)[:, :columns]
        rows = pl.ds(at, 8)
        out[rows, :] = total if science is None else science[rows, :] - total
        return carry

    lax.fori_loop(0, height // 8, finish, 0)


def first_kernel(pixels, p0, p1, p2, p3, science, before, own, after, lv, lu, left, right, back_left,
                 back_right, difference, filter_out, powers, stack, bands, products):
    sums = p0[...] + p1[...] + p2[...] + p3[...]
    coefficients = eliminate(sums[:32, :])
    mean_science = sums[32:33, 0:1] * (1.0 / pixels)
    mean_template = sums[32:33, 1:2] * (1.0 / pixels)
    kernel_t = dot(lv[...], coefficients * lu[...])
    v_index = lax.broadcasted_iota(jnp.int32, (32, 128), 0)
    u_index = lax.broadcasted_iota(jnp.int32, (32, 128), 1)
    kernel_t = kernel_t + ((v_index == MARGIN) & (u_index == MARGIN)).astype(jnp.float32)
    step = dot(left[...], kernel_t)
    both = dot(jnp.concatenate([step[:PD], step[PD:]], 1), right[...])
    re, im = both[:, :128], both[:, 128:]
    response = jnp.sqrt(
        (mean_science + mean_template) / (mean_science + mean_template * (re * re + im * im))
    )
    step = dot(back_left[...], response)
    filter_t = dot(jnp.concatenate([step[:32], step[32:]], 1), back_right[...])
    filter_out[...] = filter_t
    powers[0:1, :] = jnp.broadcast_to(total_of(kernel_t * kernel_t), (1, 128))
    powers[1:2, :] = jnp.broadcast_to(total_of(filter_t * filter_t), (1, 128))
    powers[2:, :] = jnp.zeros((6, 128), jnp.float32)
    correlate(kernel_t, before, own, after, stack, bands, products, difference, science, 512)


def second_kernel(filter_t, before, own, after, out, stack, bands, products):
    correlate(filter_t[...], before, own, after, stack, bands, products, out, None, 512)


def correlation_scratch(height, columns):
    return [
        pltpu.VMEM((256, columns), jnp.bfloat16),
        pltpu.VMEM((KS * height, 256), jnp.bfloat16),
        pltpu.VMEM((KS * height, columns + 128), jnp.float32),
    ]


def edges(strip, axis):
    devices, length = lax.axis_size(axis), strip.shape[0]
    up = [(i, i + 1) for i in range(devices - 1)]
    down = [(j, i) for i, j in up]
    before = lax.ppermute(strip[length - HALO :], axis, up)
    after = lax.ppermute(strip[:HALO], axis, down)
    return before, after


def per_device(science, variance, template_blocks, requests, stamp_rows, stamp_cols):
    height, columns = science.shape
    strips = lax.axis_size("det")
    device = lax.axis_index("det")
    held = template_blocks.shape[0]

    local = requests - device * held
    mine = (local >= 0) & (local < held)
    again = mine & jnp.pad(mine[:, :-1], ((0, 0), (1, 0)))
    first = jnp.sum(jnp.where(mine & ~again, local, 0), axis=1)
    second = jnp.sum(jnp.where(again, local, 0), axis=1)
    picks = jnp.stack([first, second], axis=1).reshape(-1).astype(jnp.int32)
    wanted = lax.dynamic_index_in_dim(requests, device, 0, keepdims=False)
    owner = wanted // held
    repeat = owner == jnp.concatenate([owner[:1] - 1, owner[:-1]])
    slots = (owner * 2 + repeat).astype(jnp.int32)

    received = lax.all_to_all(pick(picks, template_blocks), "det", 0, 0, tiled=True)
    template_image, template_variance = lay_strip(slots, received)
    before, after = edges(template_image, "det")
    partial = stamp_system(
        stamp_rows[0], stamp_cols[0], science, variance, template_image, template_variance
    )
    partials = [partial]
    for shift in range(1, CPER):
        partials.append(
            lax.ppermute(
                partial,
                "det",
                [(i, i // CPER * CPER + (i + shift) % CPER) for i in range(strips)],
            )
        )
    pixels = CPER * height * columns
    vmem = pl.BlockSpec(memory_space=VMEM)
    tables = [jnp.asarray(t) for t in (*basis_tables(), *filter_tables())]
    strip = jax.ShapeDtypeStruct((height, columns), jnp.float32)
    difference, filter_t, powers = pl.pallas_call(
        functools.partial(first_kernel, pixels),
        out_shape=[
            strip,
            jax.ShapeDtypeStruct((32, 128), jnp.float32),
            jax.ShapeDtypeStruct((8, 128), jnp.float32),
        ],
        in_specs=[vmem] * 14,
        out_specs=[vmem] * 3,
        scratch_shapes=correlation_scratch(height, columns),
        compiler_params=pltpu.CompilerParams(vmem_limit_bytes=VMEM_LIMIT),
        name="solve_and_subtract",
    )(*partials, science, before, template_image, after, *tables)
    before, after = edges(difference, "det")
    decorrelated_variance = powers[1, 0] * (variance + template_variance * powers[0, 0])
    decorrelated = pl.pallas_call(
        second_kernel,
        out_shape=strip,
        in_specs=[vmem] * 4,
        out_specs=vmem,
        scratch_shapes=correlation_scratch(height, columns),
        compiler_params=pltpu.CompilerParams(vmem_limit_bytes=VMEM_LIMIT),
        name="decorrelate",
    )(filter_t, before, difference, after)
    return (decorrelated, decorrelated_variance)


def solution(mesh):
    placed = (
        P(("group", "det"), None),
        P(("group", "det"), None),
        P(("group", "det"), None, None, None),
        P("group", None),
        P(("group", "det"), None),
        P(("group", "det"), None),
    )
    return jax.shard_map(
        per_device,
        mesh=mesh,
        in_specs=placed,
        out_specs=(P(("group", "det"), None), P(("group", "det"), None)),
        check_vma=False,
    )
```

time: 702 us -> 188 us (0.27); the launches traced: 691 us -> 186 us
  local copies, waits for them, and re-layouts: 328 us -> 6.22 us
  matrix products: 127 us -> 0 us
  other arithmetic: 122 us -> 5.84 us
  waiting for transfers between devices: 5.61 us -> 81 us
  blocking collectives: 58.8 us -> 0 us
  Pallas kernels: 0 us -> 57.4 us
  between operations: 36.4 us -> 0.81 us
  starting transfers between devices: 12.7 us -> 34.9 us
    gather x150 -> x0, local copies, waits for them, and re-layouts: 159 us -> none
    dot_general x126 -> x0, matrix products: 127 us -> none  [the longest x42 42.5 us: correlate_strip(): jnp.einsum('rtp,pc->rtc', following[tap_row:tap_row + height], bands[tap_...]
    unnamed x424 -> x18, local copies, waits for them, and re-layouts: 83.1 us -> 2.11 us
    all_to_all x0 -> x1, waiting for transfers between devices: none -> 76.1 us  [per_device(): lax.all_to_all(pick(picks, template_blocks), 'det', 0, 0, tiled=True)]
    reshape x5 -> x1, local copies, waits for them, and re-layouts: 75.8 us -> 0.61 us  [per_device(): picks = jnp.stack([first, second], axis=1).reshape(-1).astype(jnp.int32)]
    reduce_sum x27 -> x1, other arithmetic: 70.8 us -> 0.88 us  [per_device(): first = jnp.sum(jnp.where(mine & ~again, local, 0), axis=1)]
    psum x1 -> x0, blocking collectives: 58.8 us -> none  [per_device(): lax.psum((ccd_slot[:, None, None] * normal, ccd_slot[:, None] * right_sid...]
    pallas_call x0 -> x5, Pallas kernels: none -> 57.4 us  [the longest x1 21.1 us: per_device(): pl.pallas_call(functools.partial(first_kernel, pixels), out_shape=[strip,...]
  transfers between devices with their start and end apart: 5 -> 8, of which waited for: 2 -> 3; matrix products, arithmetic and copies ran while one was open for 23% -> 2% of each run, Pallas kernels for 0% -> 6%
where the time goes in v1:
time: 188 us; the launch traced here: 186 us
  waiting for transfers between devices  81 us (43%)
  Pallas kernels  57.4 us (31%)
  starting transfers between devices  34.9 us (19%)
  local copies, waits for them, and re-layouts  6.22 us (3%)
  other arithmetic  5.84 us (3%)
    all_to_all x1, waiting for transfers between devices, per_device(): lax.all_to_all(pick(picks, template_blocks), 'det', 0, 0, tiled=True)  76.1 us
    pallas_call x1, Pallas kernels, per_device(): pl.pallas_call(functools.partial(first_kernel, pixels), out_shape=[strip,...  21.1 us
    pallas_call x1, Pallas kernels, per_device(): pl.pallas_call(second_kernel, out_shape=strip, in_specs=[vmem] * 4, out_s...  17.5 us
    ppermute x3, starting transfers between devices, per_device(): lax.ppermute(partial, 'det', [(i, i // CPER * CPER + (i + shift) % CPER)...  12 us
    pallas_call x1, Pallas kernels, stamp_system(): pl.pallas_call(stamp_kernel, out_shape=jax.ShapeDtypeStruct((40, 128), jn...  11.4 us
    ppermute x2, starting transfers between devices, edges(): before = lax.ppermute(strip[length - HALO:], axis, up)  10.4 us
    all_to_all x1, starting transfers between devices, per_device(): lax.all_to_all(pick(picks, template_blocks), 'det', 0, 0, tiled=True)  7.36 us
    ppermute x2, starting transfers between devices, edges(): after = lax.ppermute(strip[:HALO], axis, down)  5.08 us
  transfers between devices with their start and end apart: 8, of which 3 were waited for; matrix products, arithmetic and copies ran while one was open for 2% of the time, Pallas kernels for 6%

profile of v1, /device:TPU:1, one launch (start us, length us, event | category | flops | bytes accessed | tf_op | source)
XLA Modules:
  0.0 186.2 jit_solution(16361470107884472668)
XLA Ops:
  0.6 0.7 compare_and_fusion
  1.3 0.9 select_reduce_fusion.1
  2.2 0.1 copy.22
  2.3 0.6 reshape.7.picks
  2.9 3.5 %pick_blocks.1 = f32[32,2,64,256]{3,2,1,0:T(8,128)} custom-call(s32[32]{0:T(128)} %reshape.7.picks, f32[8,2,64,256]{3,2,1,0:T(8,128)} %source.1), custom_call_target="tpu_custom_call" | custom-call | tf_op jit(solution)/shard_map/pick_blocks/pallas_call | solution.py:140
  6.4 7.4 %all-to-all-start = ((f32[32,2,64,256]{3,2,1,0:T(8,128)}), f32[32,2,64,256]{3,2,1,0:T(8,128)}, u32[]{:S(2)}, u32[]{:S(2)}) async-start(f32[32,2,64,256]{3,2,1,0:T(8,128)} %pick_blocks.1), calls=%async_computation | async-start | bytes 8388608 | tf_op jit(solution)/shard_map/all_to_all | solution.py:465
  13.8 0.7 and_select_fusion
  14.6 1.3 fusion.slots
  15.8 76.1 %all-to-all-done.received = f32[32,2,64,256]{3,2,1,0:T(8,128)} async-done(((f32[32,2,64,256]{3,2,1,0:T(8,128)}), f32[32,2,64,256]{3,2,1,0:T(8,128)}, u32[]{:S(2)}, u32[]{:S(2)}) %all-to-all-start) | async-done | bytes 4194336 | tf_op jit(solution)/shard_map/all_to_all | solution.py:465
  91.9 3.8 %lay_strip.1 = (f32[64,4096]{1,0:T(8,128)}, f32[64,4096]{1,0:T(8,128)}) custom-call(s32[16]{0:T(128)} %fusion.slots, f32[32,2,64,256]{3,2,1,0:T(8,128)} %all-to-all-done.received), custom_call_target="tpu_custom_call" | custom-call | tf_op jit(solution)/shard_map/lay_strip/pallas_call | solution.py:172
  95.7 1.1 fusion.2
  96.8 1.9 %collective-permute-start.4 = (f32[16,4096]{1,0:T(8,128)S(1)}, f32[16,4096]{1,0:T(8,128)S(1)}, u32[]{:S(2)}, u32[]{:S(2)}) collective-permute-start(f32[16,4096]{1,0:T(8,128)S(1)} %get-tuple-element.16), channel_id=1, source_target_pairs={{1,0},{2,1},{3,2},{4,3},{5,4},{6,5},{7,6},{8,7},{9,8},{10,9},{11,1... | collective-permute-start | bytes 786440 | tf_op jit(solution)/shard_map/ppermute | solution.py:444
  98.7 7.4 %collective-permute-start.3 = (f32[16,4096]{1,0:T(8,128)S(1)}, f32[16,4096]{1,0:T(8,128)S(1)}, u32[]{:S(2)}, u32[]{:S(2)}) collective-permute-start(f32[16,4096]{1,0:T(8,128)S(1)} %get-tuple-element.17), channel_id=1, source_target_pairs={{0,1},{1,2},{2,3},{3,4},{4,5},{5,6},{6,7},{7,8},{8,9},{9,10},{10,1... | collective-permute-start | bytes 786440 | tf_op jit(solution)/shard_map/ppermute | solution.py:443
  106.2 0.0 copy-start
  106.2 0.0 copy-start.1
  106.2 11.4 %stamp_system.1.p0 = f32[40,128]{1,0:T(8,128)} custom-call(s32[16]{0:T(128)} %bitcast.22, s32[16]{0:T(128)} %bitcast.23, f32[64,4096]{1,0:T(8,128)} %science.3, f32[64,4096]{1,0:T(8,128)} %variance.1, f32[64,4096]{1,0:T(8,128)} %get-tuple-element.7.template.own, f32[64,4096]{1,0:T(8,128)} %get-tuple-element.8.template_variance, ...), custom_call_target="tpu_custom_call" | custom-call | tf_op jit(solution)/shard_map/stamp_system/pallas_call | solution.py:331
  117.6 0.0 collective-permute-start.2
  117.6 10.0 %collective-permute-start.1 = (f32[40,128]{1,0:T(8,128)}, f32[40,128]{1,0:T(8,128)S(1)}, u32[]{:S(2)}, u32[]{:S(2)}) collective-permute-start(f32[40,128]{1,0:T(8,128)} %stamp_system.1.p0), channel_id=1, source_target_pairs={{0,2},{1,3},{2,0},{3,1},{4,6},{5,7},{6,4},{7,5},{8,10},{9,11},{10,... | collective-permute-start | bytes 61448 | tf_op jit(solution)/shard_map/ppermute | solution.py:474
  127.7 2.0 %collective-permute-start = (f32[40,128]{1,0:T(8,128)}, f32[40,128]{1,0:T(8,128)S(1)}, u32[]{:S(2)}, u32[]{:S(2)}) collective-permute-start(f32[40,128]{1,0:T(8,128)} %stamp_system.1.p0), channel_id=1, source_target_pairs={{0,1},{1,2},{2,3},{3,0},{4,5},{5,6},{6,7},{7,4},{8,9},{9,10},{10,1... | collective-permute-start | bytes 61448 | tf_op jit(solution)/shard_map/ppermute | solution.py:474
  129.7 1.1 collective-permute-done.p1
  130.8 0.6 copy-done.8
  131.4 0.1 copy-done.2
  131.5 0.7 copy-done.3
  132.2 21.1 %solve_and_subtract.1 = (f32[64,4096]{1,0:T(8,128)}, f32[32,128]{1,0:T(8,128)}, f32[8,128]{1,0:T(8,128)}) custom-call(f32[40,128]{1,0:T(8,128)} %stamp_system.1.p0, f32[40,128]{1,0:T(8,128)} %copy-done.8, f32[40,128]{1,0:T(8,128)} %copy-done.7, f32[40,128]{1,0:T(8,128)} %copy-done.6, f32[64,4096]{1,0:T(8,128)} %science.3, f32[16,4096]{1,0:T(8,128)} %copy-done.3, ...), custom_call_target="tpu_custom_call" | custom-call | tf_op jit(solution)/shard_map/solve_and_subtract/pallas_call | solution.py:484
  153.3 1.3 fusion.3
  154.6 1.1 fusion.1
  155.7 3.2 %collective-permute-start.6 = (f32[16,4096]{1,0:T(8,128)S(1)}, f32[16,4096]{1,0:T(8,128)S(1)}, u32[]{:S(2)}, u32[]{:S(2)}) collective-permute-start(f32[16,4096]{1,0:T(8,128)S(1)} %get-tuple-element.14), channel_id=1, source_target_pairs={{1,0},{2,1},{3,2},{4,3},{5,4},{6,5},{7,6},{8,7},{9,8},{10,9},{11,1... | collective-permute-start | bytes 786440 | tf_op jit(solution)/shard_map/ppermute | solution.py:444
  158.9 3.0 %collective-permute-start.5 = (f32[16,4096]{1,0:T(8,128)S(1)}, f32[16,4096]{1,0:T(8,128)S(1)}, u32[]{:S(2)}, u32[]{:S(2)}) collective-permute-start(f32[16,4096]{1,0:T(8,128)S(1)} %get-tuple-element.15), channel_id=1, source_target_pairs={{0,1},{1,2},{2,3},{3,4},{4,5},{5,6},{6,7},{7,8},{8,9},{9,10},{10,1... | collective-permute-start | bytes 786440 | tf_op jit(solution)/shard_map/ppermute | solution.py:443
  161.9 2.3 %add_multiply_fusion = f32[64,4096]{1,0:T(8,128)} fusion(f32[64,4096]{1,0:T(8,128)S(1)} %copy-done, f32[64,4096]{1,0:T(8,128)S(1)} %copy-done.1, f32[]{:T(128)} %bitcast.6, f32[]{:T(128)} %bitcast.5), kind=kLoop, calls=%fused_computation | loop fusion | flops 786432 | bytes 3145736 | tf_op jit(solution)/shard_map/mul | solution.py:498
  164.1 3.8 %collective-permute-done.5.before = f32[16,4096]{1,0:T(8,128)S(1)} collective-permute-done((f32[16,4096]{1,0:T(8,128)S(1)}, f32[16,4096]{1,0:T(8,128)S(1)}, u32[]{:S(2)}, u32[]{:S(2)}) %collective-permute-start.5) | collective-permute-done | bytes 262176 | tf_op jit(solution)/shard_map/ppermute | solution.py:443
  167.9 0.7 copy-done.5
  168.6 17.5 %decorrelate.1 = f32[64,4096]{1,0:T(8,128)} custom-call(f32[32,128]{1,0:T(8,128)} %get-tuple-element.9.filter_t, f32[16,4096]{1,0:T(8,128)} %copy-done.5, f32[64,4096]{1,0:T(8,128)} %get-tuple-element.10.own, f32[16,4096]{1,0:T(8,128)} %copy-done.4), custom_call_target="tpu_custom_call" | custom-call | tf_op jit(solution)/shard_map/decorrelate/pallas_call | solution.py:499
  (18 shorter events, 0.0 us)
Async XLA Ops:
  6.4 85.4 %all-to-all-start = ((f32[32,2,64,256]{3,2,1,0:T(8,128)}), f32[32,2,64,256]{3,2,1,0:T(8,128)}, u32[]{:S(2)}, u32[]{:S(2)}) async-start(f32[32,2,64,256]{3,2,1,0:T(8,128)} %pick_blocks.1), calls=%async_computation | async-start | bytes 8388608 | tf_op jit(solution)/shard_map/all_to_all | solution.py:465
  96.8 34.0 %collective-permute-start.4 = (f32[16,4096]{1,0:T(8,128)S(1)}, f32[16,4096]{1,0:T(8,128)S(1)}, u32[]{:S(2)}, u32[]{:S(2)}) collective-permute-start(f32[16,4096]{1,0:T(8,128)S(1)} %get-tuple-element.16), channel_id=1, source_target_pairs={{1,0},{2,1},{3,2},{4,3},{5,4},{6,5},{7,6},{8,7},{9,8},{10,9},{11,1... | collective-permute-start | bytes 786440 | tf_op jit(solution)/shard_map/ppermute | solution.py:444
  98.7 32.1 %collective-permute-start.3 = (f32[16,4096]{1,0:T(8,128)S(1)}, f32[16,4096]{1,0:T(8,128)S(1)}, u32[]{:S(2)}, u32[]{:S(2)}) collective-permute-start(f32[16,4096]{1,0:T(8,128)S(1)} %get-tuple-element.17), channel_id=1, source_target_pairs={{0,1},{1,2},{2,3},{3,4},{4,5},{5,6},{6,7},{7,8},{8,9},{9,10},{10,1... | collective-permute-start | bytes 786440 | tf_op jit(solution)/shard_map/ppermute | solution.py:443
  106.2 55.7 %copy-start = (f32[64,4096]{1,0:T(8,128)S(1)}, f32[64,4096]{1,0:T(8,128)}, u32[]{:S(2)}) copy-start(f32[64,4096]{1,0:T(8,128)} %variance.1) | copy-start | bytes 3145732
  106.2 55.7 %copy-start.1 = (f32[64,4096]{1,0:T(8,128)S(1)}, f32[64,4096]{1,0:T(8,128)}, u32[]{:S(2)}) copy-start(f32[64,4096]{1,0:T(8,128)} %get-tuple-element.8.template_variance) | copy-start | bytes 3145732
  117.6 12.0 %collective-permute-start.2 = (f32[40,128]{1,0:T(8,128)}, f32[40,128]{1,0:T(8,128)S(1)}, u32[]{:S(2)}, u32[]{:S(2)}) collective-permute-start(f32[40,128]{1,0:T(8,128)} %stamp_system.1.p0), channel_id=1, source_target_pairs={{0,3},{1,0},{2,1},{3,2},{4,7},{5,4},{6,5},{7,6},{8,11},{9,8},{10,9... | collective-permute-start | bytes 61448 | tf_op jit(solution)/shard_map/ppermute | solution.py:474
  117.6 12.0 %collective-permute-start.1 = (f32[40,128]{1,0:T(8,128)}, f32[40,128]{1,0:T(8,128)S(1)}, u32[]{:S(2)}, u32[]{:S(2)}) collective-permute-start(f32[40,128]{1,0:T(8,128)} %stamp_system.1.p0), channel_id=1, source_target_pairs={{0,2},{1,3},{2,0},{3,1},{4,6},{5,7},{6,4},{7,5},{8,10},{9,11},{10,... | collective-permute-start | bytes 61448 | tf_op jit(solution)/shard_map/ppermute | solution.py:474
  127.7 3.1 %collective-permute-start = (f32[40,128]{1,0:T(8,128)}, f32[40,128]{1,0:T(8,128)S(1)}, u32[]{:S(2)}, u32[]{:S(2)}) collective-permute-start(f32[40,128]{1,0:T(8,128)} %stamp_system.1.p0), channel_id=1, source_target_pairs={{0,1},{1,2},{2,3},{3,0},{4,5},{5,6},{6,7},{7,4},{8,9},{9,10},{10,1... | collective-permute-start | bytes 61448 | tf_op jit(solution)/shard_map/ppermute | solution.py:474
  129.7 1.1 copy-start.6
  129.7 1.1 copy-start.7
  130.8 0.6 copy-start.8
  130.8 0.7 copy-start.2
  131.5 0.7 copy-start.3
  155.7 8.5 %collective-permute-start.6 = (f32[16,4096]{1,0:T(8,128)S(1)}, f32[16,4096]{1,0:T(8,128)S(1)}, u32[]{:S(2)}, u32[]{:S(2)}) collective-permute-start(f32[16,4096]{1,0:T(8,128)S(1)} %get-tuple-element.14), channel_id=1, source_target_pairs={{1,0},{2,1},{3,2},{4,3},{5,4},{6,5},{7,6},{8,7},{9,8},{10,9},{11,1... | collective-permute-start | bytes 786440 | tf_op jit(solution)/shard_map/ppermute | solution.py:444
  158.9 9.1 %collective-permute-start.5 = (f32[16,4096]{1,0:T(8,128)S(1)}, f32[16,4096]{1,0:T(8,128)S(1)}, u32[]{:S(2)}, u32[]{:S(2)}) collective-permute-start(f32[16,4096]{1,0:T(8,128)S(1)} %get-tuple-element.15), channel_id=1, source_target_pairs={{0,1},{1,2},{2,3},{3,4},{4,5},{5,6},{6,7},{7,8},{8,9},{9,10},{10,1... | collective-permute-start | bytes 786440 | tf_op jit(solution)/shard_map/ppermute | solution.py:443
  164.1 3.8 %copy-start.4 = (f32[16,4096]{1,0:T(8,128)}, f32[16,4096]{1,0:T(8,128)S(1)}, u32[]{:S(2)}) copy-start(f32[16,4096]{1,0:T(8,128)S(1)} %collective-permute-done.6.after) | copy-start | bytes 786436
  167.9 0.7 copy-start.5

commit v2 on v1

--- a/solution.py
+++ b/solution.py
@@ -55,6 +55,7 @@
 NB = len(PAIRS)
 NFUN = LINE.shape[0]
 WROWS = 56
+FINE, COARSE = 3, 7
 
 
 def block_diag(matrix, times):
@@ -135,7 +136,7 @@
     lax.fori_loop(0, count, finish, 0)
 
 
-def pick(picks, source):
+def pick(picks, source, flops=10**6):
     count = picks.shape[0]
     return pl.pallas_call(
         pick_kernel,
@@ -144,40 +145,28 @@
         out_specs=pl.BlockSpec(memory_space=pl.ANY),
         scratch_shapes=[pltpu.SemaphoreType.DMA((count,))],
         compiler_params=pltpu.CompilerParams(vmem_limit_bytes=VMEM_LIMIT),
+        cost_estimate=pl.CostEstimate(flops=flops, bytes_accessed=10**6, transcendentals=0),
         name="pick_blocks",
     )(picks, source)
 
 
-def lay_kernel(needed, width, slots, received, image, variance, sem):
-    def copies(j):
-        k = slots[j]
+def lay_strip(slots, is_near, near, far, plane, out, sem):
+    needed = slots.shape[0]
+    width = near.shape[3]
+    for j in range(needed):
         columns = pl.ds(j * width, width)
-        return [
-            pltpu.make_async_copy(received.at[k, 0], image.at[:, columns], sem.at[0, j]),
-            pltpu.make_async_copy(received.at[k, 1], variance.at[:, columns], sem.at[1, j]),
-        ]
+
+        @pl.when(is_near[j] == 1)
+        def _():
+            pltpu.make_async_copy(near.at[slots[j], plane], out.at[:, columns], sem.at[j]).start()
+
+        @pl.when(is_near[j] == 0)
+        def _():
+            pltpu.make_async_copy(far.at[slots[j]], out.at[:, columns], sem.at[j]).start()
 
     for j in range(needed):
-        for copy in copies(j):
-            copy.start()
-    for j in range(needed):
-        for copy in copies(j):
-            copy.wait()
-
-
-def lay_strip(slots, received):
-    needed = slots.shape[0]
-    _, _, rows, width = received.shape
-    shape = jax.ShapeDtypeStruct((rows, needed * width), received.dtype)
-    return pl.pallas_call(
-        functools.partial(lay_kernel, needed, width),
-        out_shape=[shape, shape],
-        in_specs=[pl.BlockSpec(memory_space=SMEM), pl.BlockSpec(memory_space=pl.ANY)],
-        out_specs=[pl.BlockSpec(memory_space=VMEM)] * 2,
-        scratch_shapes=[pltpu.SemaphoreType.DMA((2, needed))],
-        compiler_params=pltpu.CompilerParams(vmem_limit_bytes=VMEM_LIMIT),
-        name="lay_strip",
-    )(slots, received)
+        columns = pl.ds(j * width, width)
+        pltpu.make_async_copy(far.at[slots[j]], out.at[:, columns], sem.at[j]).wait()
 
 
 def dot(a, b, contract=((1,), (0,))):
@@ -191,65 +180,50 @@
     return high, (x - high.astype(jnp.float32)).astype(jnp.bfloat16)
 
 
-def stamp_kernel(
-    stamp_rows,
-    stamp_cols,
-    science,
-    variance,
-    template,
-    template_variance,
-    across_ref,
-    down_ref,
-    left_ref,
-    right_ref,
-    back_left_ref,
-    back_right_ref,
-    ones_ref,
-    out,
-    images,
-    flat_x,
-    flat_y,
-):
+def stamp_place(stamp_rows, stamp_cols, stamp, columns):
+    row = stamp_rows[stamp] - (SS // 2 + MARGIN)
+    col = stamp_cols[stamp] - (SS // 2 + MARGIN)
+    base = pl.multiple_of(jnp.minimum(col // 128 * 128, columns - 256), 128)
+    return row, col - base, pl.ds(base, 256)
+
+
+def inner_stamp(x, row, off, k):
+    moved = pltpu.roll(x, lax.rem(32 * k - off - MARGIN + 512, 256), 1)[:, :128]
+    return pltpu.roll(moved, x.shape[0] - row - MARGIN, 0)[:SS]
+
+
+def image_kernel(stamp_rows, stamp_cols, slots, is_near, near, far, science, variance, across_ref,
+                 down_ref, left_ref, right_ref, back_left_ref, back_right_ref, ones_ref,
+                 template, flat_x, variance_stamps, stamp_weights, variance_sum, images, sem):
+    lay_strip(slots, is_near, near, far, 0, template, sem)
     height, columns = science.shape
     stamps = stamp_rows.shape[0]
     groups = stamps // 4
     lane = lax.broadcasted_iota(jnp.int32, (1, 256), 1)
 
-    windows, sciences, templates, weights = [], [], [], []
+    windows, sciences, templates = [], [], []
     for g in range(groups):
-        window = sci = tmp = wgt = None
+        window = sci = tmp = var = None
         for k in range(4):
-            row = stamp_rows[g * 4 + k] - (SS // 2 + MARGIN)
-            col = stamp_cols[g * 4 + k] - (SS // 2 + MARGIN)
-            base = jnp.minimum(col // 128 * 128, columns - 256)
-            base = pl.multiple_of(base, 128)
-            off = col - base
-            cols = pl.ds(base, 256)
+            row, off, cols = stamp_place(stamp_rows, stamp_cols, g * 4 + k, columns)
             t = template[:, cols]
-            s = science[:, cols]
-            w = variance[:, cols] + template_variance[:, cols]
-            up = lax.rem(height - row, height)
-            up_in = height - row - MARGIN
             to64 = lax.rem(64 * k - off + 256, 256)
-            to32 = lax.rem(32 * k - off - MARGIN + 512, 256)
-            tw = pltpu.roll(pltpu.roll(t, to64, 1), up, 0)[:WROWS]
-
-            def inner(x):
-                return pltpu.roll(pltpu.roll(x, to32, 1)[:, :128], up_in, 0)[:SS]
-
-            t, s, w = inner(t), inner(s), inner(w)
+            tw = pltpu.roll(pltpu.roll(t, to64, 1), lax.rem(height - row, height), 0)[:WROWS]
+            t = inner_stamp(t, row, off, k)
+            s = inner_stamp(science[:, cols], row, off, k)
+            v = inner_stamp(variance[:, cols], row, off, k)
             if k == 0:
-                window, sci, tmp, wgt = tw, s, t, w
+                window, sci, tmp, var = tw, s, t, v
             else:
                 window = jnp.where(lane // 64 == k, tw, window)
                 here = lane[:, :128] // 32 == k
                 sci = jnp.where(here, s, sci)
                 tmp = jnp.where(here, t, tmp)
-                wgt = jnp.where(here, w, wgt)
+                var = jnp.where(here, v, var)
         windows.append(window)
         sciences.append(sci)
         templates.append(tmp)
-        weights.append(wgt)
+        variance_stamps[g * SS : (g + 1) * SS, :] = var
 
     across = dot(jnp.concatenate(windows, 0), across_ref[...])
     row = 0
@@ -262,6 +236,15 @@
         for g in range(groups):
             images[g, row : row + count, :] = made[:, g * 128 : (g + 1) * 128]
         row += count
+    for g in range(groups):
+        images[g, NB * SS : (NB + 1) * SS, :] = sciences[g] - templates[g]
+        images[g, (NB + 1) * SS :, :] = jnp.zeros(((31 - NB) * SS, 128), jnp.float32)
+    wide = groups * 128
+    for r in range(SS):
+        x = jnp.concatenate([images[g, pl.ds(r, 32, stride=SS), :] for g in range(groups)], 1)
+        high = x.astype(jnp.bfloat16).astype(jnp.float32)
+        pair = jnp.concatenate([high, x - high], 0).astype(jnp.bfloat16)
+        flat_x[:, r * wide : (r + 1) * wide] = pair
 
     sci = jnp.concatenate(sciences, 0)
     tmp = jnp.concatenate(templates, 0)
@@ -286,7 +269,6 @@
     back = dot(back_left_ref[...], unit)
     surface = dot(jnp.concatenate([back[:side], back[side:]], 1), back_right_ref[...])
     narrow = lane[:, :128]
-    target, pixel_weight = [], []
     for g in range(groups):
         best = jnp.max(surface[g * SS : (g + 1) * SS], axis=0, keepdims=True)
         best = jnp.broadcast_to(best, (8, 128))
@@ -297,50 +279,41 @@
                 pltpu.roll(best, step, 1),
             )
             best = jnp.maximum(best, partner)
-        stamp_weight = jnp.maximum(best[:1], 0.1)
-        pixel_weight.append(stamp_weight / weights[g])
-        target.append(sciences[g] - templates[g])
+        stamp_weights[g * 8 : (g + 1) * 8, :] = jnp.maximum(best, 0.1)
+    variance_sum[...] = jnp.broadcast_to(total_of(variance[...]), (8, 128))
+
+
+def normal_kernel(stamp_rows, stamp_cols, slots, is_near, near, far, flat_x, variance_stamps,
+                  stamp_weights, variance_sum, template_variance, out, flat_y, sem):
+    lay_strip(slots, is_near, near, far, 1, template_variance, sem)
+    _, columns = template_variance.shape
+    stamps = stamp_rows.shape[0]
+    groups = stamps // 4
+    narrow = lax.broadcasted_iota(jnp.int32, (1, 128), 1)
+    pixel_weight = []
+    for g in range(groups):
+        weight = None
+        for k in range(4):
+            row, off, cols = stamp_place(stamp_rows, stamp_cols, g * 4 + k, columns)
+            w = inner_stamp(template_variance[:, cols], row, off, k)
+            weight = w if k == 0 else jnp.where(narrow // 32 == k, w, weight)
+        weight = variance_stamps[g * SS : (g + 1) * SS, :] + weight
+        pixel_weight.append(stamp_weights[g * 8 : g * 8 + 1, :] / weight)
+    pixel_weight = jnp.concatenate(pixel_weight, 1)
     wide = groups * 128
-    for g in range(groups):
-        images[g, NB * SS : (NB + 1) * SS, :] = target[g]
-        images[g, (NB + 1) * SS :, :] = jnp.zeros(((31 - NB) * SS, 128), jnp.float32)
-    pixel_weight = jnp.concatenate(pixel_weight, 1)
-
     for r in range(SS):
-        x = jnp.concatenate([images[g, pl.ds(r, 32, stride=SS), :] for g in range(groups)], 1)
-        y = x * pixel_weight[r : r + 1, :]
         at = slice(r * wide, (r + 1) * wide)
-        for value, ref in ((x, flat_x), (y, flat_y)):
-            high = value.astype(jnp.bfloat16).astype(jnp.float32)
-            ref[:, at] = jnp.concatenate([high, value - high], 0).astype(jnp.bfloat16)
+        pair = flat_x[:, at].astype(jnp.float32)
+        y = (pair[:32] + pair[32:]) * pixel_weight[r : r + 1, :]
+        high = y.astype(jnp.bfloat16).astype(jnp.float32)
+        flat_y[:, at] = jnp.concatenate([high, y - high], 0).astype(jnp.bfloat16)
     gram = lax.dot_general(
         flat_y[...], flat_x[...], (((1,), (1,)), ((), ())), preferred_element_type=jnp.float32
     )
-    gram = gram[:32] + gram[32:]
-    gram = gram + pltpu.roll(jnp.concatenate([gram, jnp.zeros((32, 64), jnp.float32)], 1), 96, 1)[:, :64]
-    total = jnp.sum(jnp.sum(variance[...], axis=0, keepdims=True), axis=1, keepdims=True)
-    total_t = jnp.sum(jnp.sum(template_variance[...], axis=0, keepdims=True), axis=1, keepdims=True)
-    out[:32, :] = jnp.concatenate([gram, jnp.zeros((32, 64), jnp.float32)], 1)
-    out[32:, :] = jnp.broadcast_to(jnp.where(narrow == 0, total, total_t), (8, 128))
-
-
-def stamp_system(rows, cols, science, variance, template, template_variance):
-    stamps = rows.shape[0]
-    wide = stamps // 4 * 128
-    tables = [across_table(), down_table(), *dft_blocks()]
-    return pl.pallas_call(
-        stamp_kernel,
-        out_shape=jax.ShapeDtypeStruct((40, 128), jnp.float32),
-        in_specs=[pl.BlockSpec(memory_space=SMEM)] * 2 + [pl.BlockSpec(memory_space=VMEM)] * 11,
-        out_specs=pl.BlockSpec(memory_space=VMEM),
-        scratch_shapes=[
-            pltpu.VMEM((stamps // 4, 32 * SS, 128), jnp.float32),
-            pltpu.VMEM((64, SS * wide), jnp.bfloat16),
-            pltpu.VMEM((64, SS * wide), jnp.bfloat16),
-        ],
-        compiler_params=pltpu.CompilerParams(vmem_limit_bytes=VMEM_LIMIT),
-        name="stamp_system",
-    )(rows, cols, science, variance, template, template_variance, *[jnp.asarray(t) for t in tables])
+    gram = widen(gram[:32] + gram[32:])
+    out[:32, :] = gram + pltpu.roll(gram, 96, 1)
+    total_t = total_of(template_variance[...])
+    out[32:, :] = jnp.where(narrow == 0, variance_sum[...], jnp.broadcast_to(total_t, (8, 128)))
 
 
 def eliminate(a):
@@ -361,37 +334,68 @@
     return jnp.sum(jnp.sum(x, axis=0, keepdims=True), axis=1, keepdims=True)
 
 
-def correlate(kernel_t, before, own, after, stack, bands, products, out, science, column_chunk):
+def correlate(kernel_t, before, own, after, stack, bands, products, out, science):
     height, columns = own.shape
     reach = height + 2 * MARGIN
-    pad = 128
     lead = HALO - MARGIN
-    for c in range(0, columns, column_chunk):
-        at = slice(c, c + column_chunk)
-        rows = jnp.concatenate([before[:, at], own[:, at], after[:, at]], 0)[lead : lead + reach]
-        high = rows.astype(jnp.bfloat16).astype(jnp.float32)
-        rest = jnp.zeros((256 - 3 * reach, column_chunk), jnp.float32)
-        stack[:, at] = jnp.concatenate([high, rows - high, high, rest], 0).astype(jnp.bfloat16)
+    tiles = columns // 128 + 1
     high = kernel_t.astype(jnp.bfloat16).astype(jnp.float32)
     low = kernel_t - high
     blank = jnp.zeros_like(high)
     high, low = jnp.concatenate([high, blank], 1), jnp.concatenate([low, blank], 1)
     taps = high + pltpu.roll(high, reach, 1) + pltpu.roll(low, 2 * reach, 1)
     for v in range(KS):
+        w, j = v // FINE, v % FINE
         band = jnp.broadcast_to(taps[v : v + 1, :], (height, 256))
         band = pltpu.roll(band, 0, 1, stride=1, stride_axis=0)
-        bands[v * height : (v + 1) * height, :] = band.astype(jnp.bfloat16)
-    products[:, columns:] = jnp.zeros((KS * height, pad), jnp.float32)
-    for c in range(0, columns, column_chunk):
-        at = slice(c, c + column_chunk)
+        bands[w * height : (w + 1) * height, j * 256 : (j + 1) * 256] = band.astype(jnp.bfloat16)
+
+    lane = lax.broadcasted_iota(jnp.int32, (1, 128), 1)
+    rest = jnp.zeros((256 - 3 * reach, 128), jnp.float32)
+    empty = jnp.zeros((reach, 128), jnp.float32)
+
+    def tile(t):
+        if t % tiles == tiles - 1:
+            return empty
+        at = slice(t % tiles * 128, (t % tiles + 1) * 128)
+        return jnp.concatenate([before[:, at], own[:, at], after[:, at]], 0)[lead : lead + reach]
+
+    left, here = tile(-1), tile(0)
+    left_last = pltpu.roll(left, 1, 1)
+    here_last = pltpu.roll(here, 1, 1)
+    here_next = pltpu.roll(here, 127, 1)
+    for t in range(tiles):
+        right = tile(t + 1)
+        right_last, right_next = pltpu.roll(right, 1, 1), pltpu.roll(right, 127, 1)
+        moved = (
+            jnp.where(lane < 1, left_last, here_last),
+            here,
+            jnp.where(lane < 127, here_next, right_next),
+        )
+        for j, x in enumerate(moved):
+            high = x.astype(jnp.bfloat16).astype(jnp.float32)
+            stack[j * 256 : (j + 1) * 256, t * 128 : (t + 1) * 128] = jnp.concatenate(
+                [high, x - high, high, rest], 0
+            ).astype(jnp.bfloat16)
+        left_last, here, here_last, here_next = here_last, right, right_last, right_next
+    chunk = 384 if tiles % 3 == 0 else 128
+    for c in range(0, tiles * 128, chunk):
+        at = slice(c, c + chunk)
         products[:, at] = jnp.dot(bands[...], stack[:, at], preferred_element_type=jnp.float32)
 
     def finish(g, carry):
         at = pl.multiple_of(g * 8, 8)
-        total = products[pl.ds((KS - 1) * height + at, 8), :]
-        for v in range(KS - 2, -1, -1):
-            total = pltpu.roll(total, columns + pad - 1, 1) + products[pl.ds(v * height + at, 8), :]
-        total = pltpu.roll(total, MARGIN, 1)[:, :columns]
+
+        def product(w):
+            return products[pl.ds(w * height + at, 8), :]
+
+        half = COARSE // 2
+        ahead, behind = product(COARSE - 1), product(0)
+        for w in range(half - 1):
+            ahead = pltpu.roll(ahead, tiles * 128 - FINE, 1) + product(COARSE - 2 - w)
+            behind = pltpu.roll(behind, FINE, 1) + product(w + 1)
+        total = product(half) + pltpu.roll(ahead, tiles * 128 - FINE, 1) + pltpu.roll(behind, FINE, 1)
+        total = total[:, :columns]
         rows = pl.ds(at, 8)
         out[rows, :] = total if science is None else science[rows, :] - total
         return carry
@@ -421,18 +425,18 @@
     powers[0:1, :] = jnp.broadcast_to(total_of(kernel_t * kernel_t), (1, 128))
     powers[1:2, :] = jnp.broadcast_to(total_of(filter_t * filter_t), (1, 128))
     powers[2:, :] = jnp.zeros((6, 128), jnp.float32)
-    correlate(kernel_t, before, own, after, stack, bands, products, difference, science, 512)
+    correlate(kernel_t, before, own, after, stack, bands, products, difference, science)
 
 
 def second_kernel(filter_t, before, own, after, out, stack, bands, products):
-    correlate(filter_t[...], before, own, after, stack, bands, products, out, None, 512)
+    correlate(filter_t[...], before, own, after, stack, bands, products, out, None)
 
 
 def correlation_scratch(height, columns):
     return [
-        pltpu.VMEM((256, columns), jnp.bfloat16),
-        pltpu.VMEM((KS * height, 256), jnp.bfloat16),
-        pltpu.VMEM((KS * height, columns + 128), jnp.float32),
+        pltpu.VMEM((FINE * 256, columns + 128), jnp.bfloat16),
+        pltpu.VMEM((COARSE * height, FINE * 256), jnp.bfloat16),
+        pltpu.VMEM((COARSE * height, columns + 128), jnp.float32),
     ]
 
 
@@ -451,23 +455,80 @@
     device = lax.axis_index("det")
     held = template_blocks.shape[0]
 
-    local = requests - device * held
-    mine = (local >= 0) & (local < held)
-    again = mine & jnp.pad(mine[:, :-1], ((0, 0), (1, 0)))
-    first = jnp.sum(jnp.where(mine & ~again, local, 0), axis=1)
-    second = jnp.sum(jnp.where(again, local, 0), axis=1)
-    picks = jnp.stack([first, second], axis=1).reshape(-1).astype(jnp.int32)
+    half = strips // 2
+    here = device // half
+    partner = lax.rem(device + half, strips)
+    served = lax.dynamic_slice_in_dim(requests, here * half, half, 0)
+
+    def picks_of(owner):
+        local = served - owner * held
+        mine = (local >= 0) & (local < held)
+        again = mine & jnp.pad(mine[:, :-1], ((0, 0), (1, 0)))
+        first = jnp.sum(jnp.where(mine & ~again, local, 0), axis=1)
+        second = jnp.sum(jnp.where(again, local, 0), axis=1)
+        return jnp.stack([first, second], axis=1).reshape(-1).astype(jnp.int32)
+
     wanted = lax.dynamic_index_in_dim(requests, device, 0, keepdims=False)
     owner = wanted // held
     repeat = owner == jnp.concatenate([owner[:1] - 1, owner[:-1]])
-    slots = (owner * 2 + repeat).astype(jnp.int32)
-
-    received = lax.all_to_all(pick(picks, template_blocks), "det", 0, 0, tiled=True)
-    template_image, template_variance = lay_strip(slots, received)
+    slots = (owner % half * 2 + repeat).astype(jnp.int32)
+    is_near = (owner // half == here).astype(jnp.int32)
+
+    across_halves = [(i, (i + half) % strips) for i in range(strips)]
+    halves = [list(range(half)), list(range(half, strips))]
+
+    def serve(x):
+        return lax.all_to_all(x, "det", 0, 0, axis_index_groups=halves, tiled=True)
+
+    partner_image = lax.ppermute(template_blocks[:, 0], "det", across_halves)
+    near = serve(pick(picks_of(device), template_blocks, 10**11))
+    partner_planes, partner_image = lax.optimization_barrier((template_blocks[:, 1], partner_image))
+    partner_variance = lax.ppermute(partner_planes, "det", across_halves)
+    far_picks = picks_of(partner)
+    partner_image, near = lax.optimization_barrier((partner_image, near))
+    far_image = serve(pick(far_picks, partner_image))
+    far_variance = serve(pick(far_picks, partner_variance))
+
+    vmem, smem, anywhere = (pl.BlockSpec(memory_space=m) for m in (VMEM, SMEM, pl.ANY))
+    rows, cols = stamp_rows[0], stamp_cols[0]
+    stamps = rows.shape[0]
+    flat = SS * SS * stamps
+    strip = jax.ShapeDtypeStruct((height, columns), jnp.float32)
+    row = jax.ShapeDtypeStruct((8, 128), jnp.float32)
+    tables = [jnp.asarray(t) for t in (across_table(), down_table(), *dft_blocks())]
+    params = pltpu.CompilerParams(vmem_limit_bytes=VMEM_LIMIT)
+    template_image, flat_x, variance_stamps, stamp_weights, variance_sum = pl.pallas_call(
+        image_kernel,
+        out_shape=[
+            strip,
+            jax.ShapeDtypeStruct((64, flat), jnp.bfloat16),
+            jax.ShapeDtypeStruct((stamps // 4 * SS, 128), jnp.float32),
+            jax.ShapeDtypeStruct((stamps // 4 * 8, 128), jnp.float32),
+            row,
+        ],
+        in_specs=[smem] * 4 + [anywhere] * 2 + [vmem] * 9,
+        out_specs=[vmem] * 5,
+        scratch_shapes=[
+            pltpu.VMEM((stamps // 4, 32 * SS, 128), jnp.float32),
+            pltpu.SemaphoreType.DMA((wanted.shape[0],)),
+        ],
+        compiler_params=params,
+        cost_estimate=pl.CostEstimate(flops=10**10, bytes_accessed=10**7, transcendentals=0),
+        name="stamp_images",
+    )(rows, cols, slots, is_near, near, far_image, science, variance, *tables)
     before, after = edges(template_image, "det")
-    partial = stamp_system(
-        stamp_rows[0], stamp_cols[0], science, variance, template_image, template_variance
-    )
+    template_variance, partial = pl.pallas_call(
+        normal_kernel,
+        out_shape=[strip, jax.ShapeDtypeStruct((40, 128), jnp.float32)],
+        in_specs=[smem] * 4 + [anywhere] * 2 + [vmem] * 4,
+        out_specs=[vmem] * 2,
+        scratch_shapes=[
+            pltpu.VMEM((64, flat), jnp.bfloat16),
+            pltpu.SemaphoreType.DMA((wanted.shape[0],)),
+        ],
+        compiler_params=params,
+        name="normal_equations",
+    )(rows, cols, slots, is_near, near, far_variance, flat_x, variance_stamps, stamp_weights, variance_sum)
     partials = [partial]
     for shift in range(1, CPER):
         partials.append(
@@ -478,15 +539,13 @@
             )
         )
     pixels = CPER * height * columns
-    vmem = pl.BlockSpec(memory_space=VMEM)
     tables = [jnp.asarray(t) for t in (*basis_tables(), *filter_tables())]
-    strip = jax.ShapeDtypeStruct((height, columns), jnp.float32)
     difference, filter_t, powers = pl.pallas_call(
         functools.partial(first_kernel, pixels),
         out_shape=[
             strip,
             jax.ShapeDtypeStruct((32, 128), jnp.float32),
-            jax.ShapeDtypeStruct((8, 128), jnp.float32),
+            row,
         ],
         in_specs=[vmem] * 14,
         out_specs=[vmem] * 3,

time: 188 us -> 157 us (0.84)
  waiting for transfers between devices: 81 us -> 59.2 us
  Pallas kernels: 57.4 us -> 47.2 us
  local copies, waits for them, and re-layouts: 6.22 us -> 8.92 us
    all_to_all x1 -> x3, waiting for transfers between devices: 76.1 us -> 1.68 us  [serve(): return lax.all_to_all(x, 'det', 0, 0, axis_index_groups=halves, tiled=True)]
    ppermute x0 -> x2, waiting for transfers between devices: none -> 54.4 us  [the longest x1 30.3 us: per_device(): partner_image = lax.ppermute(template_blocks[:, 0], 'det', across_halves)]
    all_to_all x1 -> x3, starting transfers between devices: 7.36 us -> 16.1 us  [serve(): return lax.all_to_all(x, 'det', 0, 0, axis_index_groups=halves, tiled=True)]
    pallas_call x1, Pallas kernels: 21.1 us -> 13.4 us  [per_device(): pl.pallas_call(functools.partial(first_kernel, pixels), out_shape=[strip,...]
    ppermute x3, starting transfers between devices: 12 us -> 4.36 us  [per_device(): lax.ppermute(partial, 'det', [(i, i // CPER * CPER + (i + shift) % CPER)...]
    pallas_call x1, Pallas kernels: 17.5 us -> 9.89 us  [per_device(): pl.pallas_call(second_kernel, out_shape=strip, in_specs=[vmem] * 4, out_s...]
    ppermute x2, starting transfers between devices: 10.4 us -> 6.49 us  [edges(): before = lax.ppermute(strip[length - HALO:], axis, up)]
    pallas_call x1 -> x3, Pallas kernels: 3.51 us -> 7.35 us  [pick(): pl.pallas_call(pick_kernel, out_shape=jax.ShapeDtypeStruct((count,) + sou...]
  transfers between devices with their start and end apart: 8 -> 12, of which waited for: 3 -> 5; matrix products, arithmetic and copies ran while one was open for 2% -> 4% of each run, Pallas kernels for 6% -> 12%
where the time goes in v2:
time: 157 us; the launch traced here: 156 us
  waiting for transfers between devices  59.2 us (38%)
  Pallas kernels  47.2 us (30%)
  starting transfers between devices  34.5 us (22%)
  local copies, waits for them, and re-layouts  8.92 us (6%)
  other arithmetic  5.75 us (4%)
    ppermute x1, waiting for transfers between devices, per_device(): partner_image = lax.ppermute(template_blocks[:, 0], 'det', across_halves)  30.3 us
    ppermute x1, waiting for transfers between devices, per_device(): partner_variance = lax.ppermute(partner_planes, 'det', across_halves)  24.1 us
    all_to_all x3, starting transfers between devices, serve(): return lax.all_to_all(x, 'det', 0, 0, axis_index_groups=halves, tiled=True)  16.1 us
    pallas_call x1, Pallas kernels, per_device(): pl.pallas_call(functools.partial(first_kernel, pixels), out_shape=[strip,...  13.4 us
    pallas_call x1, Pallas kernels, per_device(): pl.pallas_call(image_kernel, out_shape=[strip, jax.ShapeDtypeStruct((64,...  11.8 us
    pallas_call x1, Pallas kernels, per_device(): pl.pallas_call(second_kernel, out_shape=strip, in_specs=[vmem] * 4, out_s...  9.89 us
    pallas_call x3, Pallas kernels, pick(): pl.pallas_call(pick_kernel, out_shape=jax.ShapeDtypeStruct((count,) + sou...  7.35 us
    ppermute x2, starting transfers between devices, edges(): before = lax.ppermute(strip[length - HALO:], axis, up)  6.49 us
  transfers between devices with their start and end apart: 12, of which 5 were waited for; matrix products, arithmetic and copies ran while one was open for 4% of the time, Pallas kernels for 12%

profile of v2, /device:TPU:1, one launch (start us, length us, event | category | flops | bytes accessed | tf_op | source)
XLA Modules:
  0.0 156.5 jit_solution(10995992251121554689)
XLA Ops:
  0.7 0.7 compare_and_fusion.1
  1.4 0.9 select_reduce_fusion.1
  3.0 2.7 %pick_blocks.3 = f32[16,2,64,256]{3,2,1,0:T(8,128)} custom-call(s32[16]{0:T(128)} %reshape.10.picks, f32[8,2,64,256]{3,2,1,0:T(8,128)} %source.1), custom_call_target="tpu_custom_call" | custom-call | flops 99999997952 | bytes 1000000 | tf_op jit(solution)/shard_map/pick_blocks/pallas_call | solution.py:141
  5.7 5.5 %all-to-all-start = ((f32[16,2,64,256]{3,2,1,0:T(8,128)}), f32[16,2,64,256]{3,2,1,0:T(8,128)S(1)}, u32[]{:S(2)}, u32[]{:S(2)}) async-start(f32[16,2,64,256]{3,2,1,0:T(8,128)} %pick_blocks.3), calls=%async_computation | async-start | bytes 4194304 | tf_op jit(solution)/shard_map/all_to_all | solution.py:481
  11.1 1.1 slice_bitcast_fusion
  12.2 2.3 %collective-permute-start = (f32[8,64,256]{2,1,0:T(8,128)}, f32[8,64,256]{2,1,0:T(8,128)S(1)}, u32[]{:S(2)}, u32[]{:S(2)}) collective-permute-start(f32[8,64,256]{2,1,0:T(8,128)} %get-tuple-element.42), channel_id=1, source_target_pairs={{0,8},{1,9},{2,10},{3,11},{4,12},{5,13},{6,14},{7,15},{8,0},{9,1},... | collective-permute-start | bytes 1572872 | tf_op jit(solution)/shard_map/ppermute | solution.py:483
  15.2 30.3 %collective-permute-done.source = f32[8,64,256]{2,1,0:T(8,128)S(1)} collective-permute-done((f32[8,64,256]{2,1,0:T(8,128)}, f32[8,64,256]{2,1,0:T(8,128)S(1)}, u32[]{:S(2)}, u32[]{:S(2)}) %collective-permute-start) | collective-permute-done | bytes 524320 | tf_op jit(solution)/shard_map/ppermute | solution.py:483
  45.5 1.7 %all-to-all-done.near = f32[16,2,64,256]{3,2,1,0:T(8,128)S(1)} async-done(((f32[16,2,64,256]{3,2,1,0:T(8,128)}), f32[16,2,64,256]{3,2,1,0:T(8,128)S(1)}, u32[]{:S(2)}, u32[]{:S(2)}) %all-to-all-start) | async-done | bytes 2097184 | tf_op jit(solution)/shard_map/all_to_all | solution.py:481
  47.2 2.5 %pick_blocks.5 = f32[16,64,256]{2,1,0:T(8,128)} custom-call(s32[16]{0:T(128)} %reshape.11.picks, f32[8,64,256]{2,1,0:T(8,128)} %copy-done.6), custom_call_target="tpu_custom_call" | custom-call | flops 1000000 | bytes 1000000 | tf_op jit(solution)/shard_map/pick_blocks/pallas_call | solution.py:141
  49.7 6.4 %all-to-all-start.2 = ((f32[16,64,256]{2,1,0:T(8,128)}), f32[16,64,256]{2,1,0:T(8,128)S(1)}, u32[]{:S(2)}, u32[]{:S(2)}) async-start(f32[16,64,256]{2,1,0:T(8,128)} %pick_blocks.5), calls=%async_computation.2 | async-start | bytes 2097152 | tf_op jit(solution)/shard_map/all_to_all | solution.py:481
  56.2 1.3 compare_convert_fusion
  58.1 24.1 %collective-permute-done.1.source = f32[8,64,256]{2,1,0:T(8,128)} collective-permute-done((f32[8,64,256]{2,1,0:T(8,128)}, f32[8,64,256]{2,1,0:T(8,128)}, u32[]{:S(2)}, u32[]{:S(2)}) %collective-permute-start.1) | collective-permute-done | bytes 524320 | tf_op jit(solution)/shard_map/ppermute | solution.py:486
  82.2 2.1 %pick_blocks.4 = f32[16,64,256]{2,1,0:T(8,128)} custom-call(s32[16]{0:T(128)} %reshape.11.picks, f32[8,64,256]{2,1,0:T(8,128)} %collective-permute-done.1.source), custom_call_target="tpu_custom_call" | custom-call | flops 1000000 | bytes 1000000 | tf_op jit(solution)/shard_map/pick_blocks/pallas_call | solution.py:141
  84.4 4.3 %all-to-all-start.1 = ((f32[16,64,256]{2,1,0:T(8,128)}), f32[16,64,256]{2,1,0:T(8,128)S(1)}, u32[]{:S(2)}, u32[]{:S(2)}) async-start(f32[16,64,256]{2,1,0:T(8,128)} %pick_blocks.4), calls=%async_computation.1 | async-start | bytes 2097152 | tf_op jit(solution)/shard_map/all_to_all | solution.py:481
  88.6 11.8 %stamp_images.1 = (f32[64,4096]{1,0:T(8,128)}, bf16[64,16384]{1,0:T(8,128)(2,1)}, f32[128,128]{1,0:T(8,128)}, f32[32,128]{1,0:T(8,128)}, f32[8,128]{1,0:T(8,128)}) custom-call(s32[16]{0:T(128)} %bitcast.37, s32[16]{0:T(128)} %bitcast.39, s32[16]{0:T(128)} %fusion.1.slots, s32[16]{0:T(128)} %get-tuple-element.36.is_near, f32[16,2,64,256]{3,2,1,0:T(8,128)} %copy-done, ...), custom_call_target="tpu_custom_call" | custom-call | flops 10000000000 | bytes 10000000 | tf_op jit(solution)/shard_map/stamp_images/pallas_call | solution.py:500
  100.4 1.1 fusion.3
  101.5 2.0 %collective-permute-start.6 = (f32[16,4096]{1,0:T(8,128)S(1)}, f32[16,4096]{1,0:T(8,128)S(1)}, u32[]{:S(2)}, u32[]{:S(2)}) collective-permute-start(f32[16,4096]{1,0:T(8,128)S(1)} %get-tuple-element.40), channel_id=1, source_target_pairs={{1,0},{2,1},{3,2},{4,3},{5,4},{6,5},{7,6},{8,7},{9,8},{10,9},{11,1... | collective-permute-start | bytes 786440 | tf_op jit(solution)/shard_map/ppermute | solution.py:448
  103.5 3.5 %collective-permute-start.5 = (f32[16,4096]{1,0:T(8,128)S(1)}, f32[16,4096]{1,0:T(8,128)S(1)}, u32[]{:S(2)}, u32[]{:S(2)}) collective-permute-start(f32[16,4096]{1,0:T(8,128)S(1)} %get-tuple-element.41), channel_id=1, source_target_pairs={{0,1},{1,2},{2,3},{3,4},{4,5},{5,6},{6,7},{7,8},{8,9},{9,10},{10,1... | collective-permute-start | bytes 786440 | tf_op jit(solution)/shard_map/ppermute | solution.py:447
  107.1 1.0 copy-done.1
  108.1 4.8 %normal_equations.1 = (f32[64,4096]{1,0:T(8,128)}, f32[40,128]{1,0:T(8,128)}) custom-call(s32[16]{0:T(128)} %bitcast.38, s32[16]{0:T(128)} %bitcast.40, s32[16]{0:T(128)} %fusion.1.slots, s32[16]{0:T(128)} %get-tuple-element.36.is_near, f32[16,2,64,256]{3,2,1,0:T(8,128)} %copy-done, f32[16,64,256]{2,1,0:T(8,128)} %copy-done.1, ...), custom_call_target="tpu_custom_call" | custom-call | tf_op jit(solution)/shard_map/normal_equations/pallas_call | solution.py:520
  112.9 2.4 %collective-permute-start.3 = (f32[40,128]{1,0:T(8,128)}, f32[40,128]{1,0:T(8,128)S(1)}, u32[]{:S(2)}, u32[]{:S(2)}) collective-permute-start(f32[40,128]{1,0:T(8,128)} %get-tuple-element.24.p0), channel_id=1, source_target_pairs={{0,2},{1,3},{2,0},{3,1},{4,6},{5,7},{6,4},{7,5},{8,10},{9,11},{10,... | collective-permute-start | bytes 61448 | tf_op jit(solution)/shard_map/ppermute | solution.py:535
  115.3 1.9 %collective-permute-start.2 = (f32[40,128]{1,0:T(8,128)}, f32[40,128]{1,0:T(8,128)S(1)}, u32[]{:S(2)}, u32[]{:S(2)}) collective-permute-start(f32[40,128]{1,0:T(8,128)} %get-tuple-element.24.p0), channel_id=1, source_target_pairs={{0,1},{1,2},{2,3},{3,0},{4,5},{5,6},{6,7},{7,4},{8,9},{9,10},{10,1... | collective-permute-start | bytes 61448 | tf_op jit(solution)/shard_map/ppermute | solution.py:535
  117.3 1.1 collective-permute-done.2.p1
  119.1 0.7 copy-done.8
  119.8 13.4 %solve_and_subtract.1 = (f32[64,4096]{1,0:T(8,128)}, f32[32,128]{1,0:T(8,128)}, f32[8,128]{1,0:T(8,128)}) custom-call(f32[40,128]{1,0:T(8,128)} %get-tuple-element.24.p0, f32[40,128]{1,0:T(8,128)} %copy-done.13, f32[40,128]{1,0:T(8,128)} %copy-done.12, f32[40,128]{1,0:T(8,128)} %copy-done.11, f32[64,4096]{1,0:T(8,128)} %science.3, f32[16,4096]{1,0:T(8,128)} %copy-done.8, ...), custom_call_target="tpu_custom_call" | custom-call | tf_op jit(solution)/shard_map/solve_and_subtract/pallas_call | solution.py:543
  133.2 1.3 fusion.4
  134.4 1.1 fusion.2
  135.5 3.2 %collective-permute-start.8 = (f32[16,4096]{1,0:T(8,128)S(1)}, f32[16,4096]{1,0:T(8,128)S(1)}, u32[]{:S(2)}, u32[]{:S(2)}) collective-permute-start(f32[16,4096]{1,0:T(8,128)S(1)} %get-tuple-element.38), channel_id=1, source_target_pairs={{1,0},{2,1},{3,2},{4,3},{5,4},{6,5},{7,6},{8,7},{9,8},{10,9},{11,1... | collective-permute-start | bytes 786440 | tf_op jit(solution)/shard_map/ppermute | solution.py:448
  138.7 3.0 %collective-permute-start.7 = (f32[16,4096]{1,0:T(8,128)S(1)}, f32[16,4096]{1,0:T(8,128)S(1)}, u32[]{:S(2)}, u32[]{:S(2)}) collective-permute-start(f32[16,4096]{1,0:T(8,128)S(1)} %get-tuple-element.39), channel_id=1, source_target_pairs={{0,1},{1,2},{2,3},{3,4},{4,5},{5,6},{6,7},{7,8},{8,9},{9,10},{10,1... | collective-permute-start | bytes 786440 | tf_op jit(solution)/shard_map/ppermute | solution.py:447
  141.7 2.2 %add_multiply_fusion = f32[64,4096]{1,0:T(8,128)} fusion(f32[64,4096]{1,0:T(8,128)S(1)} %copy-done.3, f32[64,4096]{1,0:T(8,128)S(1)} %copy-done.4, f32[]{:T(128)} %bitcast.10, f32[]{:T(128)} %bitcast.9), kind=kLoop, calls=%fused_computation | loop fusion | flops 786432 | bytes 3145736 | tf_op jit(solution)/shard_map/mul | solution.py:557
  143.9 2.0 %collective-permute-done.7.before = f32[16,4096]{1,0:T(8,128)S(1)} collective-permute-done((f32[16,4096]{1,0:T(8,128)S(1)}, f32[16,4096]{1,0:T(8,128)S(1)}, u32[]{:S(2)}, u32[]{:S(2)}) %collective-permute-start.7) | collective-permute-done | bytes 262176 | tf_op jit(solution)/shard_map/ppermute | solution.py:447
  146.6 9.9 %decorrelate.1 = f32[64,4096]{1,0:T(8,128)} custom-call(f32[32,128]{1,0:T(8,128)} %get-tuple-element.26.filter_t, f32[16,4096]{1,0:T(8,128)} %copy-done.10, f32[64,4096]{1,0:T(8,128)} %get-tuple-element.27.own, f32[16,4096]{1,0:T(8,128)} %copy-done.9), custom_call_target="tpu_custom_call" | custom-call | tf_op jit(solution)/shard_map/decorrelate/pallas_call | solution.py:558
  (42 shorter events, 3.5 us)
Async XLA Ops:
  5.7 5.5 %copy-start.2 = (f32[8,2,64,256]{3,2,1,0:T(8,128)S(1)}, f32[8,2,64,256]{3,2,1,0:T(8,128)}, u32[]{:S(2)}) copy-start(f32[8,2,64,256]{3,2,1,0:T(8,128)} %source.1) | copy-start | bytes 3145732
  5.7 41.5 %all-to-all-start = ((f32[16,2,64,256]{3,2,1,0:T(8,128)}), f32[16,2,64,256]{3,2,1,0:T(8,128)S(1)}, u32[]{:S(2)}, u32[]{:S(2)}) async-start(f32[16,2,64,256]{3,2,1,0:T(8,128)} %pick_blocks.3), calls=%async_computation | async-start | bytes 4194304 | tf_op jit(solution)/shard_map/all_to_all | solution.py:481
  12.2 33.3 %collective-permute-start = (f32[8,64,256]{2,1,0:T(8,128)}, f32[8,64,256]{2,1,0:T(8,128)S(1)}, u32[]{:S(2)}, u32[]{:S(2)}) collective-permute-start(f32[8,64,256]{2,1,0:T(8,128)} %get-tuple-element.42), channel_id=1, source_target_pairs={{0,8},{1,9},{2,10},{3,11},{4,12},{5,13},{6,14},{7,15},{8,0},{9,1},... | collective-permute-start | bytes 1572872 | tf_op jit(solution)/shard_map/ppermute | solution.py:483
  45.5 1.7 %copy-start.6 = (f32[8,64,256]{2,1,0:T(8,128)}, f32[8,64,256]{2,1,0:T(8,128)S(1)}, u32[]{:S(2)}) copy-start(f32[8,64,256]{2,1,0:T(8,128)S(1)} %collective-permute-done.source) | copy-start | bytes 1572868
  47.2 37.1 %copy-start = (f32[16,2,64,256]{3,2,1,0:T(8,128)}, f32[16,2,64,256]{3,2,1,0:T(8,128)S(1)}, u32[]{:S(2)}) copy-start(f32[16,2,64,256]{3,2,1,0:T(8,128)S(1)} %all-to-all-done.near) | copy-start | bytes 6291460
  49.7 34.6 %all-to-all-start.2 = ((f32[16,64,256]{2,1,0:T(8,128)}), f32[16,64,256]{2,1,0:T(8,128)S(1)}, u32[]{:S(2)}, u32[]{:S(2)}) async-start(f32[16,64,256]{2,1,0:T(8,128)} %pick_blocks.5), calls=%async_computation.2 | async-start | bytes 2097152 | tf_op jit(solution)/shard_map/all_to_all | solution.py:481
  56.2 26.0 %collective-permute-start.1 = (f32[8,64,256]{2,1,0:T(8,128)}, f32[8,64,256]{2,1,0:T(8,128)}, u32[]{:S(2)}, u32[]{:S(2)}) collective-permute-start(f32[8,64,256]{2,1,0:T(8,128)} %get-tuple-element.18), channel_id=1, source_target_pairs={{0,8},{1,9},{2,10},{3,11},{4,12},{5,13},{6,14},{7,15},{8,0},{9,1},... | collective-permute-start | bytes 1572872 | tf_op jit(solution)/shard_map/ppermute | solution.py:486
  84.4 4.3 %copy-start.5 = (f32[16,64,256]{2,1,0:T(8,128)}, f32[16,64,256]{2,1,0:T(8,128)S(1)}, u32[]{:S(2)}) copy-start(f32[16,64,256]{2,1,0:T(8,128)S(1)} %all-to-all-done.2.far) | copy-start | bytes 3145732
  84.4 22.7 %all-to-all-start.1 = ((f32[16,64,256]{2,1,0:T(8,128)}), f32[16,64,256]{2,1,0:T(8,128)S(1)}, u32[]{:S(2)}, u32[]{:S(2)}) async-start(f32[16,64,256]{2,1,0:T(8,128)} %pick_blocks.4), calls=%async_computation.1 | async-start | bytes 2097152 | tf_op jit(solution)/shard_map/all_to_all | solution.py:481
  101.5 16.9 %collective-permute-start.6 = (f32[16,4096]{1,0:T(8,128)S(1)}, f32[16,4096]{1,0:T(8,128)S(1)}, u32[]{:S(2)}, u32[]{:S(2)}) collective-permute-start(f32[16,4096]{1,0:T(8,128)S(1)} %get-tuple-element.40), channel_id=1, source_target_pairs={{1,0},{2,1},{3,2},{4,3},{5,4},{6,5},{7,6},{8,7},{9,8},{10,9},{11,1... | collective-permute-start | bytes 786440 | tf_op jit(solution)/shard_map/ppermute | solution.py:448
  103.5 14.8 %collective-permute-start.5 = (f32[16,4096]{1,0:T(8,128)S(1)}, f32[16,4096]{1,0:T(8,128)S(1)}, u32[]{:S(2)}, u32[]{:S(2)}) collective-permute-start(f32[16,4096]{1,0:T(8,128)S(1)} %get-tuple-element.41), channel_id=1, source_target_pairs={{0,1},{1,2},{2,3},{3,4},{4,5},{5,6},{6,7},{7,8},{8,9},{9,10},{10,1... | collective-permute-start | bytes 786440 | tf_op jit(solution)/shard_map/ppermute | solution.py:447
  107.1 1.0 copy-start.1
  112.8 28.8 %copy-start.3 = (f32[64,4096]{1,0:T(8,128)S(1)}, f32[64,4096]{1,0:T(8,128)}, u32[]{:S(2)}) copy-start(f32[64,4096]{1,0:T(8,128)} %variance.1) | copy-start | bytes 3145732
  112.9 28.8 %copy-start.4 = (f32[64,4096]{1,0:T(8,128)S(1)}, f32[64,4096]{1,0:T(8,128)}, u32[]{:S(2)}) copy-start(f32[64,4096]{1,0:T(8,128)} %get-tuple-element.29) | copy-start | bytes 3145732
  112.9 4.4 %collective-permute-start.4 = (f32[40,128]{1,0:T(8,128)}, f32[40,128]{1,0:T(8,128)S(1)}, u32[]{:S(2)}, u32[]{:S(2)}) collective-permute-start(f32[40,128]{1,0:T(8,128)} %get-tuple-element.24.p0), channel_id=1, source_target_pairs={{0,3},{1,0},{2,1},{3,2},{4,7},{5,4},{6,5},{7,6},{8,11},{9,8},{10,9... | collective-permute-start | bytes 61448 | tf_op jit(solution)/shard_map/ppermute | solution.py:535
  112.9 4.3 %collective-permute-start.3 = (f32[40,128]{1,0:T(8,128)}, f32[40,128]{1,0:T(8,128)S(1)}, u32[]{:S(2)}, u32[]{:S(2)}) collective-permute-start(f32[40,128]{1,0:T(8,128)} %get-tuple-element.24.p0), channel_id=1, source_target_pairs={{0,2},{1,3},{2,0},{3,1},{4,6},{5,7},{6,4},{7,5},{8,10},{9,11},{10,... | collective-permute-start | bytes 61448 | tf_op jit(solution)/shard_map/ppermute | solution.py:535
  115.3 3.1 %collective-permute-start.2 = (f32[40,128]{1,0:T(8,128)}, f32[40,128]{1,0:T(8,128)S(1)}, u32[]{:S(2)}, u32[]{:S(2)}) collective-permute-start(f32[40,128]{1,0:T(8,128)} %get-tuple-element.24.p0), channel_id=1, source_target_pairs={{0,1},{1,2},{2,3},{3,0},{4,5},{5,6},{6,7},{7,4},{8,9},{9,10},{10,1... | collective-permute-start | bytes 61448 | tf_op jit(solution)/shard_map/ppermute | solution.py:535
  117.2 1.1 copy-start.11
  117.2 1.1 copy-start.12
  118.4 0.6 copy-start.13
  118.4 0.7 copy-start.7
  119.1 0.7 copy-start.8
  135.5 8.4 %collective-permute-start.8 = (f32[16,4096]{1,0:T(8,128)S(1)}, f32[16,4096]{1,0:T(8,128)S(1)}, u32[]{:S(2)}, u32[]{:S(2)}) collective-permute-start(f32[16,4096]{1,0:T(8,128)S(1)} %get-tuple-element.38), channel_id=1, source_target_pairs={{1,0},{2,1},{3,2},{4,3},{5,4},{6,5},{7,6},{8,7},{9,8},{10,9},{11,1... | collective-permute-start | bytes 786440 | tf_op jit(solution)/shard_map/ppermute | solution.py:448
  138.7 7.2 %collective-permute-start.7 = (f32[16,4096]{1,0:T(8,128)S(1)}, f32[16,4096]{1,0:T(8,128)S(1)}, u32[]{:S(2)}, u32[]{:S(2)}) collective-permute-start(f32[16,4096]{1,0:T(8,128)S(1)} %get-tuple-element.39), channel_id=1, source_target_pairs={{0,1},{1,2},{2,3},{3,4},{4,5},{5,6},{6,7},{7,8},{8,9},{9,10},{10,1... | collective-permute-start | bytes 786440 | tf_op jit(solution)/shard_map/ppermute | solution.py:447
  143.9 2.0 %copy-start.9 = (f32[16,4096]{1,0:T(8,128)}, f32[16,4096]{1,0:T(8,128)S(1)}, u32[]{:S(2)}) copy-start(f32[16,4096]{1,0:T(8,128)S(1)} %collective-permute-done.8.after) | copy-start | bytes 786436
  145.9 0.7 copy-start.10

commit v3 on v2

--- a/solution.py
+++ b/solution.py
@@ -20,6 +20,7 @@
 GAUSS_WIDTHS = (0.7, 1.5, 3.0)
 GAUSS_DEGREES = (4, 2, 2)
 VMEM_LIMIT = 60 * 1024 * 1024
+VMEM_SMALL = 32 * 1024 * 1024
 VMEM = pltpu.MemorySpace.VMEM
 SMEM = pltpu.MemorySpace.SMEM
 
@@ -118,11 +119,12 @@
     return [x.astype(np.float32) for x in (left, right, back_left, back_right)]
 
 
-def pick_kernel(picks, source, out, sem):
+def pick_kernel(plane, picks, source, out, sem):
     count = out.shape[0]
 
     def copy(k):
-        return pltpu.make_async_copy(source.at[picks[k]], out.at[k], sem.at[k])
+        block = source.at[picks[k]] if plane is None else source.at[picks[k], plane]
+        return pltpu.make_async_copy(block, out.at[k], sem.at[k])
 
     def start(k, carry):
         copy(k).start()
@@ -136,16 +138,16 @@
     lax.fori_loop(0, count, finish, 0)
 
 
-def pick(picks, source, flops=10**6):
+def pick(picks, source, plane=None):
     count = picks.shape[0]
+    shape = source.shape[1:] if plane is None else source.shape[2:]
     return pl.pallas_call(
-        pick_kernel,
-        out_shape=jax.ShapeDtypeStruct((count,) + source.shape[1:], source.dtype),
+        functools.partial(pick_kernel, plane),
+        out_shape=jax.ShapeDtypeStruct((count,) + shape, source.dtype),
         in_specs=[pl.BlockSpec(memory_space=SMEM), pl.BlockSpec(memory_space=VMEM)],
         out_specs=pl.BlockSpec(memory_space=pl.ANY),
         scratch_shapes=[pltpu.SemaphoreType.DMA((count,))],
         compiler_params=pltpu.CompilerParams(vmem_limit_bytes=VMEM_LIMIT),
-        cost_estimate=pl.CostEstimate(flops=flops, bytes_accessed=10**6, transcendentals=0),
         name="pick_blocks",
     )(picks, source)
 
@@ -194,8 +196,10 @@
 
 def image_kernel(stamp_rows, stamp_cols, slots, is_near, near, far, science, variance, across_ref,
                  down_ref, left_ref, right_ref, back_left_ref, back_right_ref, ones_ref,
-                 template, flat_x, variance_stamps, stamp_weights, variance_sum, images, sem):
+                 template, top, bottom, flat_x, variance_stamps, stamp_weights, variance_sum, images, sem):
     lay_strip(slots, is_near, near, far, 0, template, sem)
+    top[...] = template[:HALO, :]
+    bottom[...] = template[template.shape[0] - HALO :, :]
     height, columns = science.shape
     stamps = stamp_rows.shape[0]
     groups = stamps // 4
@@ -390,21 +394,20 @@
             return products[pl.ds(w * height + at, 8), :]
 
         half = COARSE // 2
-        ahead, behind = product(COARSE - 1), product(0)
-        for w in range(half - 1):
-            ahead = pltpu.roll(ahead, tiles * 128 - FINE, 1) + product(COARSE - 2 - w)
-            behind = pltpu.roll(behind, FINE, 1) + product(w + 1)
-        total = product(half) + pltpu.roll(ahead, tiles * 128 - FINE, 1) + pltpu.roll(behind, FINE, 1)
+        total = product(half)
+        for w in range(COARSE):
+            if w != half:
+                total = total + pltpu.roll(product(w), FINE * (half - w) % (tiles * 128), 1)
         total = total[:, :columns]
         rows = pl.ds(at, 8)
         out[rows, :] = total if science is None else science[rows, :] - total
         return carry
 
-    lax.fori_loop(0, height // 8, finish, 0)
+    lax.fori_loop(0, height // 8, finish, 0, unroll=True)
 
 
 def first_kernel(pixels, p0, p1, p2, p3, science, before, own, after, lv, lu, left, right, back_left,
-                 back_right, difference, filter_out, powers, stack, bands, products):
+                 back_right, difference, top, bottom, filter_out, powers, stack, bands, products):
     sums = p0[...] + p1[...] + p2[...] + p3[...]
     coefficients = eliminate(sums[:32, :])
     mean_science = sums[32:33, 0:1] * (1.0 / pixels)
@@ -426,6 +429,8 @@
     powers[1:2, :] = jnp.broadcast_to(total_of(filter_t * filter_t), (1, 128))
     powers[2:, :] = jnp.zeros((6, 128), jnp.float32)
     correlate(kernel_t, before, own, after, stack, bands, products, difference, science)
+    top[...] = difference[:HALO, :]
+    bottom[...] = difference[difference.shape[0] - HALO :, :]
 
 
 def second_kernel(filter_t, before, own, after, out, stack, bands, products):
@@ -440,12 +445,12 @@
     ]
 
 
-def edges(strip, axis):
-    devices, length = lax.axis_size(axis), strip.shape[0]
+def edges(top, bottom, axis):
+    devices = lax.axis_size(axis)
     up = [(i, i + 1) for i in range(devices - 1)]
     down = [(j, i) for i, j in up]
-    before = lax.ppermute(strip[length - HALO :], axis, up)
-    after = lax.ppermute(strip[:HALO], axis, down)
+    before = lax.ppermute(bottom, axis, up)
+    after = lax.ppermute(top, axis, down)
     return before, after
 
 
@@ -480,14 +485,13 @@
     def serve(x):
         return lax.all_to_all(x, "det", 0, 0, axis_index_groups=halves, tiled=True)
 
-    partner_image = lax.ppermute(template_blocks[:, 0], "det", across_halves)
-    near = serve(pick(picks_of(device), template_blocks, 10**11))
-    partner_planes, partner_image = lax.optimization_barrier((template_blocks[:, 1], partner_image))
-    partner_variance = lax.ppermute(partner_planes, "det", across_halves)
+    partner_blocks = lax.ppermute(template_blocks, "det", across_halves)
+    near = serve(pick(picks_of(device), template_blocks))
     far_picks = picks_of(partner)
-    partner_image, near = lax.optimization_barrier((partner_image, near))
-    far_image = serve(pick(far_picks, partner_image))
-    far_variance = serve(pick(far_picks, partner_variance))
+    partner_blocks, near = lax.optimization_barrier((partner_blocks, near))
+    far_image = serve(pick(far_picks, partner_blocks, 0))
+    partner_blocks, far_image = lax.optimization_barrier((partner_blocks, far_image))
+    far_variance = serve(pick(far_picks, partner_blocks, 1))
 
     vmem, smem, anywhere = (pl.BlockSpec(memory_space=m) for m in (VMEM, SMEM, pl.ANY))
     rows, cols = stamp_rows[0], stamp_cols[0]
@@ -495,19 +499,23 @@
     flat = SS * SS * stamps
     strip = jax.ShapeDtypeStruct((height, columns), jnp.float32)
     row = jax.ShapeDtypeStruct((8, 128), jnp.float32)
+    edge = jax.ShapeDtypeStruct((HALO, columns), jnp.float32)
     tables = [jnp.asarray(t) for t in (across_table(), down_table(), *dft_blocks())]
     params = pltpu.CompilerParams(vmem_limit_bytes=VMEM_LIMIT)
-    template_image, flat_x, variance_stamps, stamp_weights, variance_sum = pl.pallas_call(
+    small = pltpu.CompilerParams(vmem_limit_bytes=VMEM_SMALL)
+    template_image, template_top, template_bottom, flat_x, variance_stamps, stamp_weights, variance_sum = pl.pallas_call(
         image_kernel,
         out_shape=[
             strip,
+            edge,
+            edge,
             jax.ShapeDtypeStruct((64, flat), jnp.bfloat16),
             jax.ShapeDtypeStruct((stamps // 4 * SS, 128), jnp.float32),
             jax.ShapeDtypeStruct((stamps // 4 * 8, 128), jnp.float32),
             row,
         ],
         in_specs=[smem] * 4 + [anywhere] * 2 + [vmem] * 9,
-        out_specs=[vmem] * 5,
+        out_specs=[vmem] * 7,
         scratch_shapes=[
             pltpu.VMEM((stamps // 4, 32 * SS, 128), jnp.float32),
             pltpu.SemaphoreType.DMA((wanted.shape[0],)),
@@ -516,7 +524,7 @@
         cost_estimate=pl.CostEstimate(flops=10**10, bytes_accessed=10**7, transcendentals=0),
         name="stamp_images",
     )(rows, cols, slots, is_near, near, far_image, science, variance, *tables)
-    before, after = edges(template_image, "det")
+    before, after = edges(template_top, template_bottom, "det")
     template_variance, partial = pl.pallas_call(
         normal_kernel,
         out_shape=[strip, jax.ShapeDtypeStruct((40, 128), jnp.float32)],
@@ -526,7 +534,7 @@
             pltpu.VMEM((64, flat), jnp.bfloat16),
             pltpu.SemaphoreType.DMA((wanted.shape[0],)),
         ],
-        compiler_params=params,
+        compiler_params=small,
         name="normal_equations",
     )(rows, cols, slots, is_near, near, far_variance, flat_x, variance_stamps, stamp_weights, variance_sum)
     partials = [partial]
@@ -540,20 +548,22 @@
         )
     pixels = CPER * height * columns
     tables = [jnp.asarray(t) for t in (*basis_tables(), *filter_tables())]
-    difference, filter_t, powers = pl.pallas_call(
+    difference, top, bottom, filter_t, powers = pl.pallas_call(
         functools.partial(first_kernel, pixels),
         out_shape=[
             strip,
+            edge,
+            edge,
             jax.ShapeDtypeStruct((32, 128), jnp.float32),
             row,
         ],
         in_specs=[vmem] * 14,
-        out_specs=[vmem] * 3,
+        out_specs=[vmem] * 5,
         scratch_shapes=correlation_scratch(height, columns),
-        compiler_params=pltpu.CompilerParams(vmem_limit_bytes=VMEM_LIMIT),
+        compiler_params=small,
         name="solve_and_subtract",
     )(*partials, science, before, template_image, after, *tables)
-    before, after = edges(difference, "det")
+    before, after = edges(top, bottom, "det")
     decorrelated_variance = powers[1, 0] * (variance + template_variance * powers[0, 0])
     decorrelated = pl.pallas_call(
         second_kernel,
@@ -561,7 +571,7 @@
         in_specs=[vmem] * 4,
         out_specs=vmem,
         scratch_shapes=correlation_scratch(height, columns),
-        compiler_params=pltpu.CompilerParams(vmem_limit_bytes=VMEM_LIMIT),
+        compiler_params=small,
         name="decorrelate",
     )(filter_t, before, difference, after)
     return (decorrelated, decorrelated_variance)

time: 157 us -> 147 us (0.936)
  blocking collectives: 0 us -> 20.6 us
  waiting for transfers between devices: 59.2 us -> 48.5 us
  Pallas kernels: 47.2 us -> 37.5 us
  starting transfers between devices: 34.5 us -> 26.7 us
  local copies, waits for them, and re-layouts: 8.92 us -> 5.86 us
    all_to_all x0 -> x1, blocking collectives: none -> 20.6 us  [serve(): return lax.all_to_all(x, 'det', 0, 0, axis_index_groups=halves, tiled=True)]
    ppermute x6 -> x5, waiting for transfers between devices: 56.4 us -> 45.9 us  [the longest x1 42.6 us: per_device(): partner_blocks = lax.ppermute(template_blocks, 'det', across_halves)]
    all_to_all x3 -> x2, starting transfers between devices: 16.1 us -> 9.54 us  [serve(): return lax.all_to_all(x, 'det', 0, 0, axis_index_groups=halves, tiled=True)]
    pallas_call x1, Pallas kernels: 13.4 us -> 8.96 us  [per_device(): pl.pallas_call(functools.partial(first_kernel, pixels), out_shape=[strip,...]
    pallas_call x1, Pallas kernels: 9.89 us -> 5.97 us  [per_device(): pl.pallas_call(second_kernel, out_shape=strip, in_specs=[vmem] * 4, out_s...]
    pallas_call x1, Pallas kernels: 4.77 us -> 2.34 us  [per_device(): pl.pallas_call(normal_kernel, out_shape=[strip, jax.ShapeDtypeStruct((40,...]
    slice x2 -> x0, local copies, waits for them, and re-layouts: 2.13 us -> none  [edges(): after = lax.ppermute(strip[:HALO], axis, down)]
    unnamed x28 -> x40, local copies, waits for them, and re-layouts: 3.07 us -> 3.89 us
  transfers between devices with their start and end apart: 12 -> 10, of which waited for: 5 -> 4; matrix products, arithmetic and copies ran while one was open for 4% -> 3% of each run, Pallas kernels for 12% -> 10%
where the time goes in v3:
time: 147 us; the launch traced here: 146 us
  waiting for transfers between devices  48.5 us (33%)
  Pallas kernels  37.5 us (26%)
  starting transfers between devices  26.7 us (18%)
  blocking collectives  20.6 us (14%)
  other arithmetic  5.98 us (4%)
  local copies, waits for them, and re-layouts  5.86 us (4%)
    ppermute x1, waiting for transfers between devices, per_device(): partner_blocks = lax.ppermute(template_blocks, 'det', across_halves)  42.6 us
    all_to_all x1, blocking collectives, serve(): return lax.all_to_all(x, 'det', 0, 0, axis_index_groups=halves, tiled=True)  20.6 us
    pallas_call x1, Pallas kernels, per_device(): pl.pallas_call(image_kernel, out_shape=[strip, edge, edge, jax.ShapeDtype...  12.1 us
    all_to_all x2, starting transfers between devices, serve(): return lax.all_to_all(x, 'det', 0, 0, axis_index_groups=halves, tiled=True)  9.54 us
    pallas_call x1, Pallas kernels, per_device(): pl.pallas_call(functools.partial(first_kernel, pixels), out_shape=[strip,...  8.96 us
    pallas_call x3, Pallas kernels, pick(): pl.pallas_call(functools.partial(pick_kernel, plane), out_shape=jax.Shape...  8.12 us
    ppermute x2, starting transfers between devices, edges(): before = lax.ppermute(bottom, axis, up)  7.76 us
    pallas_call x1, Pallas kernels, per_device(): pl.pallas_call(second_kernel, out_shape=strip, in_specs=[vmem] * 4, out_s...  5.97 us
  transfers between devices with their start and end apart: 10, of which 4 were waited for; matrix products, arithmetic and copies ran while one was open for 3% of the time, Pallas kernels for 10%

profile of v3, /device:TPU:1, one launch (start us, length us, event | category | flops | bytes accessed | tf_op | source)
XLA Modules:
  0.0 146.1 jit_solution(1905116150689661213)
XLA Ops:
  0.7 0.7 compare_and_fusion.1
  1.4 0.9 select_reduce_fusion.1
  2.4 0.6 reshape.10.picks
  3.0 2.7 %pick_blocks.3 = f32[16,2,64,256]{3,2,1,0:T(8,128)} custom-call(s32[16]{0:T(128)} %reshape.10.picks, f32[8,2,64,256]{3,2,1,0:T(8,128)} %source.1), custom_call_target="tpu_custom_call" | custom-call | tf_op jit(solution)/shard_map/pick_blocks/pallas_call | solution.py:144
  5.7 5.3 %all-to-all-start = ((f32[16,2,64,256]{3,2,1,0:T(8,128)}), f32[16,2,64,256]{3,2,1,0:T(8,128)S(1)}, u32[]{:S(2)}, u32[]{:S(2)}) async-start(f32[16,2,64,256]{3,2,1,0:T(8,128)} %pick_blocks.3), calls=%async_computation | async-start | bytes 4194304 | tf_op jit(solution)/shard_map/all_to_all | solution.py:486
  11.0 2.3 %collective-permute-start = (f32[8,2,64,256]{3,2,1,0:T(8,128)}, f32[8,2,64,256]{3,2,1,0:T(8,128)S(1)}, u32[]{:S(2)}, u32[]{:S(2)}) collective-permute-start(f32[8,2,64,256]{3,2,1,0:T(8,128)} %source.1), channel_id=1, source_target_pairs={{0,8},{1,9},{2,10},{3,11},{4,12},{5,13},{6,14},{7,15},{8,0},{9,1},... | collective-permute-start | bytes 3145736 | tf_op jit(solution)/shard_map/ppermute | solution.py:488
  13.4 0.6 reshape.11.picks
  14.0 42.6 %collective-permute-done.source = f32[8,2,64,256]{3,2,1,0:T(8,128)S(1)} collective-permute-done((f32[8,2,64,256]{3,2,1,0:T(8,128)}, f32[8,2,64,256]{3,2,1,0:T(8,128)S(1)}, u32[]{:S(2)}, u32[]{:S(2)}) %collective-permute-start) | collective-permute-done | bytes 1048608 | tf_op jit(solution)/shard_map/ppermute | solution.py:488
  56.7 1.6 %all-to-all-done.near = f32[16,2,64,256]{3,2,1,0:T(8,128)S(1)} async-done(((f32[16,2,64,256]{3,2,1,0:T(8,128)}), f32[16,2,64,256]{3,2,1,0:T(8,128)S(1)}, u32[]{:S(2)}, u32[]{:S(2)}) %all-to-all-start) | async-done | bytes 2097184 | tf_op jit(solution)/shard_map/all_to_all | solution.py:486
  58.3 3.1 %pick_blocks.4 = f32[16,64,256]{2,1,0:T(8,128)} custom-call(s32[16]{0:T(128)} %reshape.11.picks, f32[8,2,64,256]{3,2,1,0:T(8,128)} %copy-done.18), custom_call_target="tpu_custom_call" | custom-call | tf_op jit(solution)/shard_map/pick_blocks/pallas_call | solution.py:144
  61.4 20.6 %all_to_all.15.far = f32[16,64,256]{2,1,0:T(8,128)} all-to-all(f32[16,64,256]{2,1,0:T(8,128)} %pick_blocks.4), channel_id=1, replica_groups={{0,1,2,3,4,5,6,7},{8,9,10,11,12,13,14,15},{16,17,18,19,20,21,22,23},{24..., dimensions={0} | all-to-all | bytes 2097152 | tf_op jit(solution)/shard_map/all_to_all | solution.py:486
  82.0 2.3 %pick_blocks.5 = f32[16,64,256]{2,1,0:T(8,128)} custom-call(s32[16]{0:T(128)} %reshape.11.picks, f32[8,2,64,256]{3,2,1,0:T(8,128)} %copy-done.18), custom_call_target="tpu_custom_call" | custom-call | tf_op jit(solution)/shard_map/pick_blocks/pallas_call | solution.py:144
  84.3 4.2 %all-to-all-start.2 = ((f32[16,64,256]{2,1,0:T(8,128)}), f32[16,64,256]{2,1,0:T(8,128)S(1)}, u32[]{:S(2)}, u32[]{:S(2)}) async-start(f32[16,64,256]{2,1,0:T(8,128)} %pick_blocks.5), calls=%async_computation.2 | async-start | bytes 2097152 | tf_op jit(solution)/shard_map/all_to_all | solution.py:486
  88.5 1.3 compare_convert_fusion
  89.8 0.6 fusion.1.slots
  90.5 12.1 %stamp_images.1 = (f32[64,4096]{1,0:T(8,128)}, f32[16,4096]{1,0:T(8,128)}, f32[16,4096]{1,0:T(8,128)}, bf16[64,16384]{1,0:T(8,128)(2,1)}, f32[128,128]{1,0:T(8,1...) custom-call(s32[16]{0:T(128)} %bitcast.21, s32[16]{0:T(128)} %bitcast.23, s32[16]{0:T(128)} %fusion.1.slots, ...), custom_call_target="tpu_custom_call" | custom-call | flops 10000000000 | bytes 10000000 | tf_op jit(solution)/shard_map/stamp_images/pallas_call | solution.py:506
  102.6 3.6 %collective-permute-start.4 = (f32[16,4096]{1,0:T(8,128)}, f32[16,4096]{1,0:T(8,128)S(1)}, u32[]{:S(2)}, u32[]{:S(2)}) collective-permute-start(f32[16,4096]{1,0:T(8,128)} %get-tuple-element.29), channel_id=1, source_target_pairs={{0,1},{1,2},{2,3},{3,4},{4,5},{5,6},{6,7},{7,8},{8,9},{9,10},{10,1... | collective-permute-start | bytes 786440 | tf_op jit(solution)/shard_map/ppermute | solution.py:452
  106.2 1.9 %collective-permute-start.5 = (f32[16,4096]{1,0:T(8,128)}, f32[16,4096]{1,0:T(8,128)}, u32[]{:S(2)}, u32[]{:S(2)}) collective-permute-start(f32[16,4096]{1,0:T(8,128)} %get-tuple-element.31), channel_id=1, source_target_pairs={{1,0},{2,1},{3,2},{4,3},{5,4},{6,5},{7,6},{8,7},{9,8},{10,9},{11,1... | collective-permute-start | bytes 786440 | tf_op jit(solution)/shard_map/ppermute | solution.py:453
  108.2 1.6 %copy-done.2 = bf16[64,16384]{1,0:T(8,128)(2,1)S(1)} copy-done((bf16[64,16384]{1,0:T(8,128)(2,1)S(1)}, bf16[64,16384]{1,0:T(8,128)(2,1)}, u32[]{:S(2)}) %copy-start.2) | copy-done | bytes 2097176
  109.8 0.8 copy-done.7
  110.6 0.7 copy-done.12
  111.3 0.7 copy-done.13
  112.0 2.3 %normal_equations.1 = (f32[64,4096]{1,0:T(8,128)S(1)}, f32[40,128]{1,0:T(8,128)S(1)}) custom-call(s32[16]{0:T(128)S(1)} %bitcast.22, s32[16]{0:T(128)S(1)} %bitcast.24, s32[16]{0:T(128)S(1)} %copy-done.15, s32[16]{0:T(128)S(1)} %copy-done.14, f32[16,2,64,256]{3,2,1,0:T(8,128)S(1)} %copy-done.1, f32[16,64,256]{2,1,0:T(8,128)S(1)} %all-to-all-done.2.far, ...), custom_call_target="tpu_custom_call" | custom-call | tf_op jit(solution)/shard_map/normal_equations/pallas_call | solution.py:528
  114.5 1.8 %collective-permute-start.2 = (f32[40,128]{1,0:T(8,128)S(1)}, f32[40,128]{1,0:T(8,128)S(1)}, u32[]{:S(2)}, u32[]{:S(2)}) collective-permute-start(f32[40,128]{1,0:T(8,128)S(1)} %get-tuple-element.28.p0), channel_id=1, source_target_pairs={{0,2},{1,3},{2,0},{3,1},{4,6},{5,7},{6,4},{7,5},{8,10},{9,11},{10,... | collective-permute-start | bytes 61448 | tf_op jit(solution)/shard_map/ppermute | solution.py:543
  116.3 1.4 collective-permute-start.1
  117.7 0.9 collective-permute-done.1.p1
  118.7 9.0 %solve_and_subtract.1 = (f32[64,4096]{1,0:T(8,128)S(1)}, f32[16,4096]{1,0:T(8,128)S(1)}, f32[16,4096]{1,0:T(8,128)S(1)}, f32[32,128]{1,0:T(8,128)S(1)}, f32[8,128]{1,0:T(8,128)S(1)}) custom-call(f32[40,128]{1,0:T(8,128)S(1)} %get-tuple-element.28.p0, f32[40,128]{1,0:T(8,128)S(1)} %collective-permute-done.1.p1, f32[40,128]{1,0:T(8,128)S(1)} %collective-permute-done.2.p2, ...), custom_call_target="tpu_custom_call" | custom-call | tf_op jit(solution)/shard_map/solve_and_subtract/pallas_call | solution.py:551
  128.2 4.2 %collective-permute-start.6 = (f32[16,4096]{1,0:T(8,128)S(1)}, f32[16,4096]{1,0:T(8,128)S(1)}, u32[]{:S(2)}, u32[]{:S(2)}) collective-permute-start(f32[16,4096]{1,0:T(8,128)S(1)} %get-tuple-element.33), channel_id=1, source_target_pairs={{0,1},{1,2},{2,3},{3,4},{4,5},{5,6},{6,7},{7,8},{8,9},{9,10},{10,1... | collective-permute-start | bytes 786440 | tf_op jit(solution)/shard_map/ppermute | solution.py:452
  132.4 1.9 %collective-permute-start.7 = (f32[16,4096]{1,0:T(8,128)S(1)}, f32[16,4096]{1,0:T(8,128)S(1)}, u32[]{:S(2)}, u32[]{:S(2)}) collective-permute-start(f32[16,4096]{1,0:T(8,128)S(1)} %get-tuple-element.35), channel_id=1, source_target_pairs={{1,0},{2,1},{3,2},{4,3},{5,4},{6,5},{7,6},{8,7},{9,8},{10,9},{11,1... | collective-permute-start | bytes 786440 | tf_op jit(solution)/shard_map/ppermute | solution.py:453
  134.3 2.5 %add_multiply_fusion = f32[64,4096]{1,0:T(8,128)} fusion(f32[64,4096]{1,0:T(8,128)S(1)} %copy-done.19, f32[64,4096]{1,0:T(8,128)S(1)} %get-tuple-element.37, f32[]{:T(128)} %bitcast.8, f32[]{:T(128)} %bitcast.7), kind=kLoop, calls=%fused_computation | loop fusion | flops 786432 | bytes 3145736 | tf_op jit(solution)/shard_map/mul | solution.py:567
  136.8 3.3 %collective-permute-done.7.after = f32[16,4096]{1,0:T(8,128)S(1)} collective-permute-done((f32[16,4096]{1,0:T(8,128)S(1)}, f32[16,4096]{1,0:T(8,128)S(1)}, u32[]{:S(2)}, u32[]{:S(2)}) %collective-permute-start.7) | collective-permute-done | bytes 262176 | tf_op jit(solution)/shard_map/ppermute | solution.py:453
  140.1 6.0 %decorrelate.1 = f32[64,4096]{1,0:T(8,128)} custom-call(f32[32,128]{1,0:T(8,128)S(1)} %get-tuple-element.32.filter_t, f32[16,4096]{1,0:T(8,128)S(1)} %collective-permute-done.6.before, f32[64,4096]{1,0:T(8,128)S(1)} %get-tuple-element.34.own, f32[16,4096]{1,0:T(8,128)S(1)} %collective-permute-done.7.after), custom_call_target="tpu_custom_call" | custom-call | tf_op jit(solution)/shard_map/decorrelate/pallas_call | solution.py:568
  (48 shorter events, 0.9 us)
Async XLA Ops:
  5.7 52.6 %all-to-all-start = ((f32[16,2,64,256]{3,2,1,0:T(8,128)}), f32[16,2,64,256]{3,2,1,0:T(8,128)S(1)}, u32[]{:S(2)}, u32[]{:S(2)}) async-start(f32[16,2,64,256]{3,2,1,0:T(8,128)} %pick_blocks.3), calls=%async_computation | async-start | bytes 4194304 | tf_op jit(solution)/shard_map/all_to_all | solution.py:486
  11.0 45.7 %collective-permute-start = (f32[8,2,64,256]{3,2,1,0:T(8,128)}, f32[8,2,64,256]{3,2,1,0:T(8,128)S(1)}, u32[]{:S(2)}, u32[]{:S(2)}) collective-permute-start(f32[8,2,64,256]{3,2,1,0:T(8,128)} %source.1), channel_id=1, source_target_pairs={{0,8},{1,9},{2,10},{3,11},{4,12},{5,13},{6,14},{7,15},{8,0},{9,1},... | collective-permute-start | bytes 3145736 | tf_op jit(solution)/shard_map/ppermute | solution.py:488
  56.7 1.6 %copy-start.18 = (f32[8,2,64,256]{3,2,1,0:T(8,128)}, f32[8,2,64,256]{3,2,1,0:T(8,128)S(1)}, u32[]{:S(2)}) copy-start(f32[8,2,64,256]{3,2,1,0:T(8,128)S(1)} %collective-permute-done.source) | copy-start | bytes 3145732
  58.3 23.7 %copy-start = (f32[16,2,64,256]{3,2,1,0:T(8,128)}, f32[16,2,64,256]{3,2,1,0:T(8,128)S(1)}, u32[]{:S(2)}) copy-start(f32[16,2,64,256]{3,2,1,0:T(8,128)S(1)} %all-to-all-done.near) | copy-start | bytes 6291460
  84.3 23.8 %all-to-all-start.2 = ((f32[16,64,256]{2,1,0:T(8,128)}), f32[16,64,256]{2,1,0:T(8,128)S(1)}, u32[]{:S(2)}, u32[]{:S(2)}) async-start(f32[16,64,256]{2,1,0:T(8,128)} %pick_blocks.5), calls=%async_computation.2 | async-start | bytes 2097152 | tf_op jit(solution)/shard_map/all_to_all | solution.py:486
  90.5 17.7 %copy-start.1 = (f32[16,2,64,256]{3,2,1,0:T(8,128)S(1)}, f32[16,2,64,256]{3,2,1,0:T(8,128)}, u32[]{:S(2)}) copy-start(f32[16,2,64,256]{3,2,1,0:T(8,128)} %copy-done) | copy-start | bytes 6291460
  90.5 17.7 %copy-start.14 = (s32[16]{0:T(128)S(1)}, s32[16]{0:T(128)}, u32[]{:S(2)}) copy-start(s32[16]{0:T(128)} %get-tuple-element.44.is_near) | copy-start | bytes 196
  90.5 17.7 %copy-start.15 = (s32[16]{0:T(128)S(1)}, s32[16]{0:T(128)}, u32[]{:S(2)}) copy-start(s32[16]{0:T(128)} %fusion.1.slots) | copy-start | bytes 196
  90.5 17.7 %copy-start.16 = (s32[1,16]{1,0:T(1,128)S(1)}, s32[1,16]{1,0:T(1,128)}, u32[]{:S(2)}) copy-start(s32[1,16]{1,0:T(1,128)} %param.23) | copy-start | bytes 196
  90.5 17.7 %copy-start.17 = (s32[1,16]{1,0:T(1,128)S(1)}, s32[1,16]{1,0:T(1,128)}, u32[]{:S(2)}) copy-start(s32[1,16]{1,0:T(1,128)} %param.24) | copy-start | bytes 196
  102.6 15.1 %collective-permute-start.4 = (f32[16,4096]{1,0:T(8,128)}, f32[16,4096]{1,0:T(8,128)S(1)}, u32[]{:S(2)}, u32[]{:S(2)}) collective-permute-start(f32[16,4096]{1,0:T(8,128)} %get-tuple-element.29), channel_id=1, source_target_pairs={{0,1},{1,2},{2,3},{3,4},{4,5},{5,6},{6,7},{7,8},{8,9},{9,10},{10,1... | collective-permute-start | bytes 786440 | tf_op jit(solution)/shard_map/ppermute | solution.py:452
  106.2 11.5 %collective-permute-start.5 = (f32[16,4096]{1,0:T(8,128)}, f32[16,4096]{1,0:T(8,128)}, u32[]{:S(2)}, u32[]{:S(2)}) collective-permute-start(f32[16,4096]{1,0:T(8,128)} %get-tuple-element.31), channel_id=1, source_target_pairs={{1,0},{2,1},{3,2},{4,3},{5,4},{6,5},{7,6},{8,7},{9,8},{10,9},{11,1... | collective-permute-start | bytes 786440 | tf_op jit(solution)/shard_map/ppermute | solution.py:453
  108.2 1.6 %copy-start.2 = (bf16[64,16384]{1,0:T(8,128)(2,1)S(1)}, bf16[64,16384]{1,0:T(8,128)(2,1)}, u32[]{:S(2)}) copy-start(bf16[64,16384]{1,0:T(8,128)(2,1)} %get-tuple-element.24.flat_x) | copy-start | bytes 6291460
  109.7 0.8 copy-start.7
  110.6 0.7 copy-start.12
  111.3 0.7 copy-start.13
  112.0 6.6 %copy-start.3 = (f32[64,4096]{1,0:T(8,128)S(1)}, f32[64,4096]{1,0:T(8,128)}, u32[]{:S(2)}) copy-start(f32[64,4096]{1,0:T(8,128)} %science.3) | copy-start | bytes 3145732
  112.0 6.6 %copy-start.4 = (f32[64,4096]{1,0:T(8,128)S(1)}, f32[64,4096]{1,0:T(8,128)}, u32[]{:S(2)}) copy-start(f32[64,4096]{1,0:T(8,128)} %get-tuple-element.30.own) | copy-start | bytes 3145732
  112.0 6.6 %copy-start.5 = (f32[256,256]{1,0:T(8,128)S(1)}, f32[256,256]{1,0:T(8,128)}, u32[]{:S(2)}) copy-start(f32[256,256]{1,0:T(8,128)} %constant.106.clone.right) | copy-start | bytes 786436
  112.0 6.6 %copy-start.6 = (f32[256,128]{1,0:T(8,128)S(1)}, f32[256,128]{1,0:T(8,128)}, u32[]{:S(2)}) copy-start(f32[256,128]{1,0:T(8,128)} %constant.108.clone.back_right) | copy-start | bytes 393220
  112.0 6.6 %copy-start.8 = (f32[64,32]{1,0:T(8,128)S(1)}, f32[64,32]{1,0:T(8,128)}, u32[]{:S(2)}) copy-start(f32[64,32]{1,0:T(8,128)} %constant.107.clone.back_left) | copy-start | bytes 24580
  112.0 6.6 %copy-start.9 = (f32[64,32]{1,0:T(8,128)S(1)}, f32[64,32]{1,0:T(8,128)}, u32[]{:S(2)}) copy-start(f32[64,32]{1,0:T(8,128)} %constant.105.clone.left) | copy-start | bytes 24580
  112.0 6.6 %copy-start.10 = (f32[32,128]{1,0:T(8,128)S(1)}, f32[32,128]{1,0:T(8,128)}, u32[]{:S(2)}) copy-start(f32[32,128]{1,0:T(8,128)} %constant.104.clone.lu) | copy-start | bytes 49156
  112.0 6.6 %copy-start.11 = (f32[32,32]{1,0:T(8,128)S(1)}, f32[32,32]{1,0:T(8,128)}, u32[]{:S(2)}) copy-start(f32[32,32]{1,0:T(8,128)} %constant.103.clone.lv) | copy-start | bytes 12292
  114.4 20.0 %copy-start.19 = (f32[64,4096]{1,0:T(8,128)S(1)}, f32[64,4096]{1,0:T(8,128)}, u32[]{:S(2)}) copy-start(f32[64,4096]{1,0:T(8,128)} %variance.1) | copy-start | bytes 3145732
  114.4 3.3 %collective-permute-start.3 = (f32[40,128]{1,0:T(8,128)S(1)}, f32[40,128]{1,0:T(8,128)S(1)}, u32[]{:S(2)}, u32[]{:S(2)}) collective-permute-start(f32[40,128]{1,0:T(8,128)S(1)} %get-tuple-element.28.p0), channel_id=1, source_target_pairs={{0,3},{1,0},{2,1},{3,2},{4,7},{5,4},{6,5},{7,6},{8,11},{9,8},{10,9... | collective-permute-start | bytes 61448 | tf_op jit(solution)/shard_map/ppermute | solution.py:543
  114.5 3.2 %collective-permute-start.2 = (f32[40,128]{1,0:T(8,128)S(1)}, f32[40,128]{1,0:T(8,128)S(1)}, u32[]{:S(2)}, u32[]{:S(2)}) collective-permute-start(f32[40,128]{1,0:T(8,128)S(1)} %get-tuple-element.28.p0), channel_id=1, source_target_pairs={{0,2},{1,3},{2,0},{3,1},{4,6},{5,7},{6,4},{7,5},{8,10},{9,11},{10,... | collective-permute-start | bytes 61448 | tf_op jit(solution)/shard_map/ppermute | solution.py:543
  116.3 2.3 %collective-permute-start.1 = (f32[40,128]{1,0:T(8,128)S(1)}, f32[40,128]{1,0:T(8,128)S(1)}, u32[]{:S(2)}, u32[]{:S(2)}) collective-permute-start(f32[40,128]{1,0:T(8,128)S(1)} %get-tuple-element.28.p0), channel_id=1, source_target_pairs={{0,1},{1,2},{2,3},{3,0},{4,5},{5,6},{6,7},{7,4},{8,9},{9,10},{10,1... | collective-permute-start | bytes 61448 | tf_op jit(solution)/shard_map/ppermute | solution.py:543
  128.2 8.6 %collective-permute-start.6 = (f32[16,4096]{1,0:T(8,128)S(1)}, f32[16,4096]{1,0:T(8,128)S(1)}, u32[]{:S(2)}, u32[]{:S(2)}) collective-permute-start(f32[16,4096]{1,0:T(8,128)S(1)} %get-tuple-element.33), channel_id=1, source_target_pairs={{0,1},{1,2},{2,3},{3,4},{4,5},{5,6},{6,7},{7,8},{8,9},{9,10},{10,1... | collective-permute-start | bytes 786440 | tf_op jit(solution)/shard_map/ppermute | solution.py:452
  132.4 7.7 %collective-permute-start.7 = (f32[16,4096]{1,0:T(8,128)S(1)}, f32[16,4096]{1,0:T(8,128)S(1)}, u32[]{:S(2)}, u32[]{:S(2)}) collective-permute-start(f32[16,4096]{1,0:T(8,128)S(1)} %get-tuple-element.35), channel_id=1, source_target_pairs={{1,0},{2,1},{3,2},{4,3},{5,4},{6,5},{7,6},{8,7},{9,8},{10,9},{11,1... | collective-permute-start | bytes 786440 | tf_op jit(solution)/shard_map/ppermute | solution.py:453

commit v4 on v3

--- a/solution.py
+++ b/solution.py
@@ -56,6 +56,7 @@
 NB = len(PAIRS)
 NFUN = LINE.shape[0]
 WROWS = 56
+TABLES = 7
 FINE, COARSE = 3, 7
 
 
@@ -194,40 +195,60 @@
     return pltpu.roll(moved, x.shape[0] - row - MARGIN, 0)[:SS]
 
 
-def image_kernel(stamp_rows, stamp_cols, slots, is_near, near, far, science, variance, across_ref,
-                 down_ref, left_ref, right_ref, back_left_ref, back_right_ref, ones_ref,
-                 template, top, bottom, flat_x, variance_stamps, stamp_weights, variance_sum, images, sem):
+def science_kernel(stamp_rows, stamp_cols, science, variance, science_stamps, variance_stamps, variance_sum):
+    _, columns = science.shape
+    narrow = lax.broadcasted_iota(jnp.int32, (1, 128), 1)
+    for g in range(stamp_rows.shape[0] // 4):
+        sci = var = None
+        for k in range(4):
+            row, off, cols = stamp_place(stamp_rows, stamp_cols, g * 4 + k, columns)
+            s = inner_stamp(science[:, cols], row, off, k)
+            v = inner_stamp(variance[:, cols], row, off, k)
+            here = narrow // 32 == k
+            sci, var = (s, v) if k == 0 else (jnp.where(here, s, sci), jnp.where(here, v, var))
+        science_stamps[g * SS : (g + 1) * SS, :] = sci
+        variance_stamps[g * SS : (g + 1) * SS, :] = var
+    variance_sum[...] = jnp.broadcast_to(total_of(variance[...]), (8, 128))
+
+
+def image_kernel(stamp_rows, stamp_cols, slots, is_near, near, far, science_stamps, *refs):
+    tables_in, refs = refs[:TABLES], refs[TABLES:]
+    template, top, bottom, flat_x, stamp_weights, images, sem, table_sem = refs[:8]
+    tables = refs[8:]
+    loads = [
+        pltpu.make_async_copy(source, table, table_sem.at[i])
+        for i, (source, table) in enumerate(zip(tables_in, tables))
+    ]
+    for load in loads:
+        load.start()
+    across_ref, down_ref, left_ref, right_ref, back_left_ref, back_right_ref, ones_ref = tables
     lay_strip(slots, is_near, near, far, 0, template, sem)
+    height, columns = template.shape
     top[...] = template[:HALO, :]
-    bottom[...] = template[template.shape[0] - HALO :, :]
-    height, columns = science.shape
+    bottom[...] = template[height - HALO :, :]
     stamps = stamp_rows.shape[0]
     groups = stamps // 4
     lane = lax.broadcasted_iota(jnp.int32, (1, 256), 1)
 
     windows, sciences, templates = [], [], []
     for g in range(groups):
-        window = sci = tmp = var = None
+        window = tmp = None
         for k in range(4):
             row, off, cols = stamp_place(stamp_rows, stamp_cols, g * 4 + k, columns)
             t = template[:, cols]
             to64 = lax.rem(64 * k - off + 256, 256)
             tw = pltpu.roll(pltpu.roll(t, to64, 1), lax.rem(height - row, height), 0)[:WROWS]
             t = inner_stamp(t, row, off, k)
-            s = inner_stamp(science[:, cols], row, off, k)
-            v = inner_stamp(variance[:, cols], row, off, k)
             if k == 0:
-                window, sci, tmp, var = tw, s, t, v
+                window, tmp = tw, t
             else:
                 window = jnp.where(lane // 64 == k, tw, window)
-                here = lane[:, :128] // 32 == k
-                sci = jnp.where(here, s, sci)
-                tmp = jnp.where(here, t, tmp)
-                var = jnp.where(here, v, var)
+                tmp = jnp.where(lane[:, :128] // 32 == k, t, tmp)
         windows.append(window)
-        sciences.append(sci)
         templates.append(tmp)
-        variance_stamps[g * SS : (g + 1) * SS, :] = var
+        sciences.append(science_stamps[g * SS : (g + 1) * SS, :])
+    for load in loads:
+        load.wait()
 
     across = dot(jnp.concatenate(windows, 0), across_ref[...])
     row = 0
@@ -284,7 +305,6 @@
             )
             best = jnp.maximum(best, partner)
         stamp_weights[g * 8 : (g + 1) * 8, :] = jnp.maximum(best, 0.1)
-    variance_sum[...] = jnp.broadcast_to(total_of(variance[...]), (8, 128))
 
 
 def normal_kernel(stamp_rows, stamp_cols, slots, is_near, near, far, flat_x, variance_stamps,
@@ -488,11 +508,6 @@
     partner_blocks = lax.ppermute(template_blocks, "det", across_halves)
     near = serve(pick(picks_of(device), template_blocks))
     far_picks = picks_of(partner)
-    partner_blocks, near = lax.optimization_barrier((partner_blocks, near))
-    far_image = serve(pick(far_picks, partner_blocks, 0))
-    partner_blocks, far_image = lax.optimization_barrier((partner_blocks, far_image))
-    far_variance = serve(pick(far_picks, partner_blocks, 1))
-
     vmem, smem, anywhere = (pl.BlockSpec(memory_space=m) for m in (VMEM, SMEM, pl.ANY))
     rows, cols = stamp_rows[0], stamp_cols[0]
     stamps = rows.shape[0]
@@ -503,27 +518,44 @@
     tables = [jnp.asarray(t) for t in (across_table(), down_table(), *dft_blocks())]
     params = pltpu.CompilerParams(vmem_limit_bytes=VMEM_LIMIT)
     small = pltpu.CompilerParams(vmem_limit_bytes=VMEM_SMALL)
-    template_image, template_top, template_bottom, flat_x, variance_stamps, stamp_weights, variance_sum = pl.pallas_call(
+    stamp_rows_shape = jax.ShapeDtypeStruct((stamps // 4 * SS, 128), jnp.float32)
+    science_stamps, variance_stamps, variance_sum = pl.pallas_call(
+        science_kernel,
+        out_shape=[stamp_rows_shape, stamp_rows_shape, row],
+        in_specs=[smem] * 2 + [vmem] * 2,
+        out_specs=[vmem] * 3,
+        compiler_params=params,
+        name="science_stamps",
+    )(rows, cols, science, variance)
+    partner_blocks, near, slots, is_near, science_stamps, variance_stamps, variance_sum = (
+        lax.optimization_barrier(
+            (partner_blocks, near, slots, is_near, science_stamps, variance_stamps, variance_sum)
+        )
+    )
+    far_image = serve(pick(far_picks, partner_blocks, 0))
+    partner_blocks, far_image = lax.optimization_barrier((partner_blocks, far_image))
+    far_variance = serve(pick(far_picks, partner_blocks, 1))
+
+    template_image, template_top, template_bottom, flat_x, stamp_weights = pl.pallas_call(
         image_kernel,
         out_shape=[
             strip,
             edge,
             edge,
             jax.ShapeDtypeStruct((64, flat), jnp.bfloat16),
-            jax.ShapeDtypeStruct((stamps // 4 * SS, 128), jnp.float32),
             jax.ShapeDtypeStruct((stamps // 4 * 8, 128), jnp.float32),
-            row,
         ],
-        in_specs=[smem] * 4 + [anywhere] * 2 + [vmem] * 9,
-        out_specs=[vmem] * 7,
+        in_specs=[smem] * 4 + [anywhere] * 2 + [vmem] + [anywhere] * TABLES,
+        out_specs=[vmem] * 5,
         scratch_shapes=[
             pltpu.VMEM((stamps // 4, 32 * SS, 128), jnp.float32),
             pltpu.SemaphoreType.DMA((wanted.shape[0],)),
+            pltpu.SemaphoreType.DMA((TABLES,)),
+            *[pltpu.VMEM(t.shape, t.dtype) for t in tables],
         ],
         compiler_params=params,
-        cost_estimate=pl.CostEstimate(flops=10**10, bytes_accessed=10**7, transcendentals=0),
         name="stamp_images",
-    )(rows, cols, slots, is_near, near, far_image, science, variance, *tables)
+    )(rows, cols, slots, is_near, near, far_image, science_stamps, *tables)
     before, after = edges(template_top, template_bottom, "det")
     template_variance, partial = pl.pallas_call(
         normal_kernel,

time: 147 us -> 142 us (0.966)
  waiting for transfers between devices: 48.5 us -> 43.8 us
  Pallas kernels: 37.5 us -> 39 us
    ppermute x1, waiting for transfers between devices: 42.6 us -> 37.9 us  [per_device(): partner_blocks = lax.ppermute(template_blocks, 'det', across_halves)]
    pallas_call x0 -> x1, Pallas kernels: none -> 2.84 us  [per_device(): pl.pallas_call(science_kernel, out_shape=[stamp_rows_shape, stamp_rows_sh...]
    unnamed x40, local copies, waits for them, and re-layouts: 3.89 us -> 2.39 us
  transfers between devices with their start and end apart: 10 -> 10, of which waited for: 4 -> 4; matrix products, arithmetic and copies ran while one was open for 3% -> 4% of each run, Pallas kernels for 10% -> 11%
where the time goes in v4:
time: 142 us; the launch traced here: 141 us
  waiting for transfers between devices  43.8 us (31%)
  Pallas kernels  39 us (27%)
  starting transfers between devices  26.7 us (19%)
  blocking collectives  19.9 us (14%)
  other arithmetic  5.84 us (4%)
  local copies, waits for them, and re-layouts  4.42 us (3%)
    ppermute x1, waiting for transfers between devices, per_device(): partner_blocks = lax.ppermute(template_blocks, 'det', across_halves)  37.9 us
    all_to_all x1, blocking collectives, serve(): return lax.all_to_all(x, 'det', 0, 0, axis_index_groups=halves, tiled=True)  19.9 us
    pallas_call x1, Pallas kernels, per_device(): pl.pallas_call(image_kernel, out_shape=[strip, edge, edge, jax.ShapeDtype...  10.8 us
    all_to_all x2, starting transfers between devices, serve(): return lax.all_to_all(x, 'det', 0, 0, axis_index_groups=halves, tiled=True)  9.54 us
    pallas_call x1, Pallas kernels, per_device(): pl.pallas_call(functools.partial(first_kernel, pixels), out_shape=[strip,...  8.96 us
    pallas_call x3, Pallas kernels, pick(): pl.pallas_call(functools.partial(pick_kernel, plane), out_shape=jax.Shape...  8.13 us
    ppermute x2, starting transfers between devices, edges(): before = lax.ppermute(bottom, axis, up)  7.75 us
    pallas_call x1, Pallas kernels, per_device(): pl.pallas_call(second_kernel, out_shape=strip, in_specs=[vmem] * 4, out_s...  5.96 us
  transfers between devices with their start and end apart: 10, of which 4 were waited for; matrix products, arithmetic and copies ran while one was open for 4% of the time, Pallas kernels for 11%

profile of v4, /device:TPU:1, one launch (start us, length us, event | category | flops | bytes accessed | tf_op | source)
XLA Modules:
  0.0 140.7 jit_solution(18066252374079169423)
XLA Ops:
  0.7 0.7 compare_and_fusion.1
  1.4 0.9 select_reduce_fusion.1
  2.4 0.6 reshape.10.picks
  3.0 2.7 %pick_blocks.3 = f32[16,2,64,256]{3,2,1,0:T(8,128)} custom-call(s32[16]{0:T(128)} %reshape.10.picks, f32[8,2,64,256]{3,2,1,0:T(8,128)} %source.1), custom_call_target="tpu_custom_call" | custom-call | tf_op jit(solution)/shard_map/pick_blocks/pallas_call | solution.py:145
  5.7 5.3 %all-to-all-start = ((f32[16,2,64,256]{3,2,1,0:T(8,128)}), f32[16,2,64,256]{3,2,1,0:T(8,128)S(1)}, u32[]{:S(2)}, u32[]{:S(2)}) async-start(f32[16,2,64,256]{3,2,1,0:T(8,128)} %pick_blocks.3), calls=%async_computation | async-start | bytes 4194304 | tf_op jit(solution)/shard_map/all_to_all | solution.py:506
  11.0 2.3 %collective-permute-start = (f32[8,2,64,256]{3,2,1,0:T(8,128)}, f32[8,2,64,256]{3,2,1,0:T(8,128)S(1)}, u32[]{:S(2)}, u32[]{:S(2)}) collective-permute-start(f32[8,2,64,256]{3,2,1,0:T(8,128)} %source.1), channel_id=1, source_target_pairs={{0,8},{1,9},{2,10},{3,11},{4,12},{5,13},{6,14},{7,15},{8,0},{9,1},... | collective-permute-start | bytes 3145736 | tf_op jit(solution)/shard_map/ppermute | solution.py:508
  13.4 0.7 reshape.11.picks
  14.1 1.2 compare_convert_fusion
  15.4 2.8 %science_stamps.1 = (f32[128,128]{1,0:T(8,128)}, f32[128,128]{1,0:T(8,128)}, f32[8,128]{1,0:T(8,128)}) custom-call(s32[16]{0:T(128)} %bitcast.21, s32[16]{0:T(128)} %bitcast.24, f32[64,4096]{1,0:T(8,128)} %science.3, f32[64,4096]{1,0:T(8,128)} %variance.1), custom_call_target="tpu_custom_call" | custom-call | tf_op jit(solution)/shard_map/science_stamps/pallas_call | solution.py:522
  18.2 0.6 fusion.1.slots
  18.8 37.9 %collective-permute-done.source = f32[8,2,64,256]{3,2,1,0:T(8,128)S(1)} collective-permute-done((f32[8,2,64,256]{3,2,1,0:T(8,128)}, f32[8,2,64,256]{3,2,1,0:T(8,128)S(1)}, u32[]{:S(2)}, u32[]{:S(2)}) %collective-permute-start) | collective-permute-done | bytes 1048608 | tf_op jit(solution)/shard_map/ppermute | solution.py:508
  56.7 1.6 %all-to-all-done.near = f32[16,2,64,256]{3,2,1,0:T(8,128)S(1)} async-done(((f32[16,2,64,256]{3,2,1,0:T(8,128)}), f32[16,2,64,256]{3,2,1,0:T(8,128)S(1)}, u32[]{:S(2)}, u32[]{:S(2)}) %all-to-all-start) | async-done | bytes 2097184 | tf_op jit(solution)/shard_map/all_to_all | solution.py:506
  58.3 3.1 %pick_blocks.4 = f32[16,64,256]{2,1,0:T(8,128)} custom-call(s32[16]{0:T(128)} %reshape.11.picks, f32[8,2,64,256]{3,2,1,0:T(8,128)} %copy-done.18), custom_call_target="tpu_custom_call" | custom-call | tf_op jit(solution)/shard_map/pick_blocks/pallas_call | solution.py:145
  61.4 19.9 %all_to_all.15.far = f32[16,64,256]{2,1,0:T(8,128)} all-to-all(f32[16,64,256]{2,1,0:T(8,128)} %pick_blocks.4), channel_id=1, replica_groups={{0,1,2,3,4,5,6,7},{8,9,10,11,12,13,14,15},{16,17,18,19,20,21,22,23},{24..., dimensions={0} | all-to-all | bytes 2097152 | tf_op jit(solution)/shard_map/all_to_all | solution.py:506
  81.3 2.3 %pick_blocks.5 = f32[16,64,256]{2,1,0:T(8,128)} custom-call(s32[16]{0:T(128)} %reshape.11.picks, f32[8,2,64,256]{3,2,1,0:T(8,128)} %copy-done.18), custom_call_target="tpu_custom_call" | custom-call | tf_op jit(solution)/shard_map/pick_blocks/pallas_call | solution.py:145
  83.6 4.2 %all-to-all-start.2 = ((f32[16,64,256]{2,1,0:T(8,128)}), f32[16,64,256]{2,1,0:T(8,128)S(1)}, u32[]{:S(2)}, u32[]{:S(2)}) async-start(f32[16,64,256]{2,1,0:T(8,128)} %pick_blocks.5), calls=%async_computation.2 | async-start | bytes 2097152 | tf_op jit(solution)/shard_map/all_to_all | solution.py:506
  87.9 10.8 %stamp_images.1 = (f32[64,4096]{1,0:T(8,128)}, f32[16,4096]{1,0:T(8,128)}, f32[16,4096]{1,0:T(8,128)}, bf16[64,16384]{1,0:T(8,128)(2,1)}, f32[32,128]{1,0:T(8,128)}) custom-call(s32[16]{0:T(128)} %bitcast.22, s32[16]{0:T(128)} %bitcast.25, s32[16]{0:T(128)} %fusion.1.slots, s32[16]{0:T(128)} %get-tuple-element.30.is_near, f32[16,2,64,256]{3,2,1,0:T(8,128)} %copy-done, ...), custom_call_target="tpu_custom_call" | custom-call | tf_op jit(solution)/shard_map/stamp_images/pallas_call | solution.py:539
  98.7 3.5 %collective-permute-start.4 = (f32[16,4096]{1,0:T(8,128)}, f32[16,4096]{1,0:T(8,128)S(1)}, u32[]{:S(2)}, u32[]{:S(2)}) collective-permute-start(f32[16,4096]{1,0:T(8,128)} %get-tuple-element.41), channel_id=1, source_target_pairs={{0,1},{1,2},{2,3},{3,4},{4,5},{5,6},{6,7},{7,8},{8,9},{9,10},{10,1... | collective-permute-start | bytes 786440 | tf_op jit(solution)/shard_map/ppermute | solution.py:472
  102.3 1.9 %collective-permute-start.5 = (f32[16,4096]{1,0:T(8,128)}, f32[16,4096]{1,0:T(8,128)}, u32[]{:S(2)}, u32[]{:S(2)}) collective-permute-start(f32[16,4096]{1,0:T(8,128)} %get-tuple-element.43), channel_id=1, source_target_pairs={{1,0},{2,1},{3,2},{4,3},{5,4},{6,5},{7,6},{8,7},{9,8},{10,9},{11,1... | collective-permute-start | bytes 786440 | tf_op jit(solution)/shard_map/ppermute | solution.py:473
  104.3 1.6 %copy-done.3 = bf16[64,16384]{1,0:T(8,128)(2,1)S(1)} copy-done((bf16[64,16384]{1,0:T(8,128)(2,1)S(1)}, bf16[64,16384]{1,0:T(8,128)(2,1)}, u32[]{:S(2)}) %copy-start.3) | copy-done | bytes 2097176
  105.9 0.7 copy-done.12
  106.7 2.3 %normal_equations.1 = (f32[64,4096]{1,0:T(8,128)S(1)}, f32[40,128]{1,0:T(8,128)S(1)}) custom-call(s32[16]{0:T(128)S(1)} %bitcast.23, s32[16]{0:T(128)S(1)} %bitcast.26, s32[16]{0:T(128)S(1)} %copy-done.14, s32[16]{0:T(128)S(1)} %copy-done.13, f32[16,2,64,256]{3,2,1,0:T(8,128)S(1)} %copy-done.1, f32[16,64,256]{2,1,0:T(8,128)S(1)} %all-to-all-done.2.far, ...), custom_call_target="tpu_custom_call" | custom-call | tf_op jit(solution)/shard_map/normal_equations/pallas_call | solution.py:560
  109.1 1.8 %collective-permute-start.2 = (f32[40,128]{1,0:T(8,128)S(1)}, f32[40,128]{1,0:T(8,128)S(1)}, u32[]{:S(2)}, u32[]{:S(2)}) collective-permute-start(f32[40,128]{1,0:T(8,128)S(1)} %get-tuple-element.40.p0), channel_id=1, source_target_pairs={{0,2},{1,3},{2,0},{3,1},{4,6},{5,7},{6,4},{7,5},{8,10},{9,11},{10,... | collective-permute-start | bytes 61448 | tf_op jit(solution)/shard_map/ppermute | solution.py:575
  110.9 1.4 collective-permute-start.1
  112.3 0.9 collective-permute-done.1.p1
  113.3 9.0 %solve_and_subtract.1 = (f32[64,4096]{1,0:T(8,128)S(1)}, f32[16,4096]{1,0:T(8,128)S(1)}, f32[16,4096]{1,0:T(8,128)S(1)}, f32[32,128]{1,0:T(8,128)S(1)}, f32[8,128]{1,0:T(8,128)S(1)}) custom-call(f32[40,128]{1,0:T(8,128)S(1)} %get-tuple-element.40.p0, f32[40,128]{1,0:T(8,128)S(1)} %collective-permute-done.1.p1, f32[40,128]{1,0:T(8,128)S(1)} %collective-permute-done.2.p2, ...), custom_call_target="tpu_custom_call" | custom-call | tf_op jit(solution)/shard_map/solve_and_subtract/pallas_call | solution.py:583
  122.2 0.6 fusion.2
  122.8 4.2 %collective-permute-start.6 = (f32[16,4096]{1,0:T(8,128)S(1)}, f32[16,4096]{1,0:T(8,128)S(1)}, u32[]{:S(2)}, u32[]{:S(2)}) collective-permute-start(f32[16,4096]{1,0:T(8,128)S(1)} %get-tuple-element.45), channel_id=1, source_target_pairs={{0,1},{1,2},{2,3},{3,4},{4,5},{5,6},{6,7},{7,8},{8,9},{9,10},{10,1... | collective-permute-start | bytes 786440 | tf_op jit(solution)/shard_map/ppermute | solution.py:472
  127.0 1.9 %collective-permute-start.7 = (f32[16,4096]{1,0:T(8,128)S(1)}, f32[16,4096]{1,0:T(8,128)S(1)}, u32[]{:S(2)}, u32[]{:S(2)}) collective-permute-start(f32[16,4096]{1,0:T(8,128)S(1)} %get-tuple-element.47), channel_id=1, source_target_pairs={{1,0},{2,1},{3,2},{4,3},{5,4},{6,5},{7,6},{8,7},{9,8},{10,9},{11,1... | collective-permute-start | bytes 786440 | tf_op jit(solution)/shard_map/ppermute | solution.py:473
  129.0 2.4 %add_multiply_fusion = f32[64,4096]{1,0:T(8,128)} fusion(f32[64,4096]{1,0:T(8,128)S(1)} %copy-done.19, f32[64,4096]{1,0:T(8,128)S(1)} %get-tuple-element.49, f32[]{:T(128)} %bitcast.8, f32[]{:T(128)} %bitcast.7), kind=kLoop, calls=%fused_computation | loop fusion | flops 786432 | bytes 3145736 | tf_op jit(solution)/shard_map/mul | solution.py:599
  131.4 3.3 %collective-permute-done.7.after = f32[16,4096]{1,0:T(8,128)S(1)} collective-permute-done((f32[16,4096]{1,0:T(8,128)S(1)}, f32[16,4096]{1,0:T(8,128)S(1)}, u32[]{:S(2)}, u32[]{:S(2)}) %collective-permute-start.7) | collective-permute-done | bytes 262176 | tf_op jit(solution)/shard_map/ppermute | solution.py:473
  134.7 6.0 %decorrelate.1 = f32[64,4096]{1,0:T(8,128)} custom-call(f32[32,128]{1,0:T(8,128)S(1)} %get-tuple-element.44.filter_t, f32[16,4096]{1,0:T(8,128)S(1)} %collective-permute-done.6.before, f32[64,4096]{1,0:T(8,128)S(1)} %get-tuple-element.46.own, f32[16,4096]{1,0:T(8,128)S(1)} %collective-permute-done.7.after), custom_call_target="tpu_custom_call" | custom-call | tf_op jit(solution)/shard_map/decorrelate/pallas_call | solution.py:600
  (49 shorter events, 0.4 us)
Async XLA Ops:
  5.7 52.6 %all-to-all-start = ((f32[16,2,64,256]{3,2,1,0:T(8,128)}), f32[16,2,64,256]{3,2,1,0:T(8,128)S(1)}, u32[]{:S(2)}, u32[]{:S(2)}) async-start(f32[16,2,64,256]{3,2,1,0:T(8,128)} %pick_blocks.3), calls=%async_computation | async-start | bytes 4194304 | tf_op jit(solution)/shard_map/all_to_all | solution.py:506
  11.0 45.7 %collective-permute-start = (f32[8,2,64,256]{3,2,1,0:T(8,128)}, f32[8,2,64,256]{3,2,1,0:T(8,128)S(1)}, u32[]{:S(2)}, u32[]{:S(2)}) collective-permute-start(f32[8,2,64,256]{3,2,1,0:T(8,128)} %source.1), channel_id=1, source_target_pairs={{0,8},{1,9},{2,10},{3,11},{4,12},{5,13},{6,14},{7,15},{8,0},{9,1},... | collective-permute-start | bytes 3145736 | tf_op jit(solution)/shard_map/ppermute | solution.py:508
  56.7 1.6 %copy-start.18 = (f32[8,2,64,256]{3,2,1,0:T(8,128)}, f32[8,2,64,256]{3,2,1,0:T(8,128)S(1)}, u32[]{:S(2)}) copy-start(f32[8,2,64,256]{3,2,1,0:T(8,128)S(1)} %collective-permute-done.source) | copy-start | bytes 3145732
  58.3 23.0 %copy-start = (f32[16,2,64,256]{3,2,1,0:T(8,128)}, f32[16,2,64,256]{3,2,1,0:T(8,128)S(1)}, u32[]{:S(2)}) copy-start(f32[16,2,64,256]{3,2,1,0:T(8,128)S(1)} %all-to-all-done.near) | copy-start | bytes 6291460
  83.6 20.6 %all-to-all-start.2 = ((f32[16,64,256]{2,1,0:T(8,128)}), f32[16,64,256]{2,1,0:T(8,128)S(1)}, u32[]{:S(2)}, u32[]{:S(2)}) async-start(f32[16,64,256]{2,1,0:T(8,128)} %pick_blocks.5), calls=%async_computation.2 | async-start | bytes 2097152 | tf_op jit(solution)/shard_map/all_to_all | solution.py:506
  87.9 16.4 %copy-start.1 = (f32[16,2,64,256]{3,2,1,0:T(8,128)S(1)}, f32[16,2,64,256]{3,2,1,0:T(8,128)}, u32[]{:S(2)}) copy-start(f32[16,2,64,256]{3,2,1,0:T(8,128)} %copy-done) | copy-start | bytes 6291460
  87.9 16.4 %copy-start.7 = (f32[128,128]{1,0:T(8,128)S(1)}, f32[128,128]{1,0:T(8,128)}, u32[]{:S(2)}) copy-start(f32[128,128]{1,0:T(8,128)} %get-tuple-element.37.variance_stamps) | copy-start | bytes 196612
  87.9 16.4 %copy-start.13 = (s32[16]{0:T(128)S(1)}, s32[16]{0:T(128)}, u32[]{:S(2)}) copy-start(s32[16]{0:T(128)} %get-tuple-element.30.is_near) | copy-start | bytes 196
  87.9 16.4 %copy-start.14 = (s32[16]{0:T(128)S(1)}, s32[16]{0:T(128)}, u32[]{:S(2)}) copy-start(s32[16]{0:T(128)} %fusion.1.slots) | copy-start | bytes 196
  87.9 16.4 %copy-start.15 = (s32[1,16]{1,0:T(1,128)S(1)}, s32[1,16]{1,0:T(1,128)}, u32[]{:S(2)}) copy-start(s32[1,16]{1,0:T(1,128)} %param.23) | copy-start | bytes 196
  87.9 16.4 %copy-start.16 = (s32[1,16]{1,0:T(1,128)S(1)}, s32[1,16]{1,0:T(1,128)}, u32[]{:S(2)}) copy-start(s32[1,16]{1,0:T(1,128)} %param.24) | copy-start | bytes 196
  87.9 16.4 %copy-start.17 = (f32[8,128]{1,0:T(8,128)S(1)}, f32[8,128]{1,0:T(8,128)}, u32[]{:S(2)}) copy-start(f32[8,128]{1,0:T(8,128)} %get-tuple-element.39.variance_sum) | copy-start | bytes 12292
  98.7 13.6 %collective-permute-start.4 = (f32[16,4096]{1,0:T(8,128)}, f32[16,4096]{1,0:T(8,128)S(1)}, u32[]{:S(2)}, u32[]{:S(2)}) collective-permute-start(f32[16,4096]{1,0:T(8,128)} %get-tuple-element.41), channel_id=1, source_target_pairs={{0,1},{1,2},{2,3},{3,4},{4,5},{5,6},{6,7},{7,8},{8,9},{9,10},{10,1... | collective-permute-start | bytes 786440 | tf_op jit(solution)/shard_map/ppermute | solution.py:472
  102.3 10.0 %collective-permute-start.5 = (f32[16,4096]{1,0:T(8,128)}, f32[16,4096]{1,0:T(8,128)}, u32[]{:S(2)}, u32[]{:S(2)}) collective-permute-start(f32[16,4096]{1,0:T(8,128)} %get-tuple-element.43), channel_id=1, source_target_pairs={{1,0},{2,1},{3,2},{4,3},{5,4},{6,5},{7,6},{8,7},{9,8},{10,9},{11,1... | collective-permute-start | bytes 786440 | tf_op jit(solution)/shard_map/ppermute | solution.py:473
  104.3 1.6 %copy-start.3 = (bf16[64,16384]{1,0:T(8,128)(2,1)S(1)}, bf16[64,16384]{1,0:T(8,128)(2,1)}, u32[]{:S(2)}) copy-start(bf16[64,16384]{1,0:T(8,128)(2,1)} %get-tuple-element.36.flat_x) | copy-start | bytes 6291460
  105.9 0.7 copy-start.12
  106.6 6.6 %copy-start.2 = (f32[64,4096]{1,0:T(8,128)S(1)}, f32[64,4096]{1,0:T(8,128)}, u32[]{:S(2)}) copy-start(f32[64,4096]{1,0:T(8,128)} %science.3) | copy-start | bytes 3145732
  106.6 6.6 %copy-start.4 = (f32[64,4096]{1,0:T(8,128)S(1)}, f32[64,4096]{1,0:T(8,128)}, u32[]{:S(2)}) copy-start(f32[64,4096]{1,0:T(8,128)} %get-tuple-element.42.own) | copy-start | bytes 3145732
  106.6 6.6 %copy-start.5 = (f32[256,256]{1,0:T(8,128)S(1)}, f32[256,256]{1,0:T(8,128)}, u32[]{:S(2)}) copy-start(f32[256,256]{1,0:T(8,128)} %constant.106.clone.right) | copy-start | bytes 786436
  106.6 6.6 %copy-start.6 = (f32[256,128]{1,0:T(8,128)S(1)}, f32[256,128]{1,0:T(8,128)}, u32[]{:S(2)}) copy-start(f32[256,128]{1,0:T(8,128)} %constant.108.clone.back_right) | copy-start | bytes 393220
  106.6 6.6 %copy-start.8 = (f32[64,32]{1,0:T(8,128)S(1)}, f32[64,32]{1,0:T(8,128)}, u32[]{:S(2)}) copy-start(f32[64,32]{1,0:T(8,128)} %constant.107.clone.back_left) | copy-start | bytes 24580
  106.6 6.6 %copy-start.9 = (f32[64,32]{1,0:T(8,128)S(1)}, f32[64,32]{1,0:T(8,128)}, u32[]{:S(2)}) copy-start(f32[64,32]{1,0:T(8,128)} %constant.105.clone.left) | copy-start | bytes 24580
  106.7 6.6 %copy-start.10 = (f32[32,128]{1,0:T(8,128)S(1)}, f32[32,128]{1,0:T(8,128)}, u32[]{:S(2)}) copy-start(f32[32,128]{1,0:T(8,128)} %constant.104.clone.lu) | copy-start | bytes 49156
  106.7 6.6 %copy-start.11 = (f32[32,32]{1,0:T(8,128)S(1)}, f32[32,32]{1,0:T(8,128)}, u32[]{:S(2)}) copy-start(f32[32,32]{1,0:T(8,128)} %constant.103.clone.lv) | copy-start | bytes 12292
  109.0 19.9 %copy-start.19 = (f32[64,4096]{1,0:T(8,128)S(1)}, f32[64,4096]{1,0:T(8,128)}, u32[]{:S(2)}) copy-start(f32[64,4096]{1,0:T(8,128)} %variance.1) | copy-start | bytes 3145732
  109.0 3.3 %collective-permute-start.3 = (f32[40,128]{1,0:T(8,128)S(1)}, f32[40,128]{1,0:T(8,128)S(1)}, u32[]{:S(2)}, u32[]{:S(2)}) collective-permute-start(f32[40,128]{1,0:T(8,128)S(1)} %get-tuple-element.40.p0), channel_id=1, source_target_pairs={{0,3},{1,0},{2,1},{3,2},{4,7},{5,4},{6,5},{7,6},{8,11},{9,8},{10,9... | collective-permute-start | bytes 61448 | tf_op jit(solution)/shard_map/ppermute | solution.py:575
  109.1 3.2 %collective-permute-start.2 = (f32[40,128]{1,0:T(8,128)S(1)}, f32[40,128]{1,0:T(8,128)S(1)}, u32[]{:S(2)}, u32[]{:S(2)}) collective-permute-start(f32[40,128]{1,0:T(8,128)S(1)} %get-tuple-element.40.p0), channel_id=1, source_target_pairs={{0,2},{1,3},{2,0},{3,1},{4,6},{5,7},{6,4},{7,5},{8,10},{9,11},{10,... | collective-permute-start | bytes 61448 | tf_op jit(solution)/shard_map/ppermute | solution.py:575
  110.9 2.3 %collective-permute-start.1 = (f32[40,128]{1,0:T(8,128)S(1)}, f32[40,128]{1,0:T(8,128)S(1)}, u32[]{:S(2)}, u32[]{:S(2)}) collective-permute-start(f32[40,128]{1,0:T(8,128)S(1)} %get-tuple-element.40.p0), channel_id=1, source_target_pairs={{0,1},{1,2},{2,3},{3,0},{4,5},{5,6},{6,7},{7,4},{8,9},{9,10},{10,1... | collective-permute-start | bytes 61448 | tf_op jit(solution)/shard_map/ppermute | solution.py:575
  122.8 8.6 %collective-permute-start.6 = (f32[16,4096]{1,0:T(8,128)S(1)}, f32[16,4096]{1,0:T(8,128)S(1)}, u32[]{:S(2)}, u32[]{:S(2)}) collective-permute-start(f32[16,4096]{1,0:T(8,128)S(1)} %get-tuple-element.45), channel_id=1, source_target_pairs={{0,1},{1,2},{2,3},{3,4},{4,5},{5,6},{6,7},{7,8},{8,9},{9,10},{10,1... | collective-permute-start | bytes 786440 | tf_op jit(solution)/shard_map/ppermute | solution.py:472
  127.0 7.7 %collective-permute-start.7 = (f32[16,4096]{1,0:T(8,128)S(1)}, f32[16,4096]{1,0:T(8,128)S(1)}, u32[]{:S(2)}, u32[]{:S(2)}) collective-permute-start(f32[16,4096]{1,0:T(8,128)S(1)} %get-tuple-element.47), channel_id=1, source_target_pairs={{1,0},{2,1},{3,2},{4,3},{5,4},{6,5},{7,6},{8,7},{9,8},{10,9},{11,1... | collective-permute-start | bytes 786440 | tf_op jit(solution)/shard_map/ppermute | solution.py:473

commit v5 on v4

--- a/solution.py
+++ b/solution.py
@@ -55,7 +55,7 @@
 PAIRS = [(a, b) for b, downs in GROUPS for a in downs]
 NB = len(PAIRS)
 NFUN = LINE.shape[0]
-WROWS = 56
+WROWS = 64
 TABLES = 7
 FINE, COARSE = 3, 7
 
@@ -74,7 +74,12 @@
         for k in range(4):
             for c in range(SS):
                 table[64 * k + c : 64 * k + c + KS, b * 128 + 32 * k + c] = LINE[b]
-    return table.astype(np.float32)
+    return np.concatenate(split_host(table), 1)
+
+
+def split_host(table):
+    high = table.astype(np.float32).astype(jnp.bfloat16)
+    return high, (table - high.astype(np.float64)).astype(np.float32).astype(jnp.bfloat16)
 
 
 def down_table():
@@ -82,7 +87,8 @@
     for image, (a, _) in enumerate(PAIRS):
         for r in range(SS):
             table[image * SS + r, r : r + KS] = LINE[a]
-    return table.astype(np.float32)
+    high, low = split_host(table)
+    return np.concatenate([high, high, low], 1)
 
 
 def dft_blocks():
@@ -176,6 +182,10 @@
     return lax.dot_general(
         a, b, (contract, ((), ())), precision=HIGHEST, preferred_element_type=jnp.float32
     )
+
+
+def dot16(a, b):
+    return jnp.dot(a, b, preferred_element_type=jnp.float32)
 
 
 def split(x):
@@ -250,14 +260,18 @@
     for load in loads:
         load.wait()
 
-    across = dot(jnp.concatenate(windows, 0), across_ref[...])
+    high, low = split(jnp.concatenate(windows, 0))
+    table_high, table_low = across_ref[:, : NFUN * 128], across_ref[:, NFUN * 128 :]
+    across = dot16(high, table_high) + (dot16(low, table_high) + dot16(high, table_low))
     row = 0
     for b, downs in GROUPS:
         piece = jnp.concatenate(
             [across[g * WROWS : (g + 1) * WROWS, b * 128 : (b + 1) * 128] for g in range(groups)], 1
         )
         count = len(downs) * SS
-        made = dot(down_ref[row : row + count, :], piece)
+        high = piece.astype(jnp.bfloat16).astype(jnp.float32)
+        stacked = jnp.concatenate([high, piece - high, high], 0).astype(jnp.bfloat16)
+        made = dot16(down_ref[row : row + count, :], stacked)
         for g in range(groups):
             images[g, row : row + count, :] = made[:, g * 128 : (g + 1) * 128]
         row += count
@@ -533,8 +547,10 @@
         )
     )
     far_image = serve(pick(far_picks, partner_blocks, 0))
-    partner_blocks, far_image = lax.optimization_barrier((partner_blocks, far_image))
-    far_variance = serve(pick(far_picks, partner_blocks, 1))
+    picked_variance, far_image = lax.optimization_barrier(
+        (pick(far_picks, partner_blocks, 1), far_image)
+    )
+    far_variance = serve(picked_variance)
 
     template_image, template_top, template_bottom, flat_x, stamp_weights = pl.pallas_call(
         image_kernel,

time: 142 us -> 139 us (0.979)
  blocking collectives: 19.9 us -> 0 us
  waiting for transfers between devices: 43.8 us -> 55 us
  starting transfers between devices: 26.7 us -> 32.8 us
    all_to_all x1 -> x0, blocking collectives: 19.9 us -> none  [serve(): return lax.all_to_all(x, 'det', 0, 0, axis_index_groups=halves, tiled=True)]
    all_to_all x2 -> x3, waiting for transfers between devices: 1.64 us -> 12.9 us  [serve(): return lax.all_to_all(x, 'det', 0, 0, axis_index_groups=halves, tiled=True)]
    all_to_all x2 -> x3, starting transfers between devices: 9.54 us -> 15.6 us  [serve(): return lax.all_to_all(x, 'det', 0, 0, axis_index_groups=halves, tiled=True)]
    unnamed x40 -> x42, local copies, waits for them, and re-layouts: 2.39 us -> 3.36 us
  transfers between devices with their start and end apart: 10 -> 11, of which waited for: 4 -> 5; matrix products, arithmetic and copies ran while one was open for 4% -> 4% of each run, Pallas kernels for 11% -> 12%
where the time goes in v5:
time: 139 us; the launch traced here: 138 us
  waiting for transfers between devices  55 us (40%)
  Pallas kernels  37.8 us (27%)
  starting transfers between devices  32.8 us (24%)
  other arithmetic  5.91 us (4%)
  local copies, waits for them, and re-layouts  5.33 us (4%)
    ppermute x1, waiting for transfers between devices, per_device(): partner_blocks = lax.ppermute(template_blocks, 'det', across_halves)  37.9 us
    all_to_all x3, starting transfers between devices, serve(): return lax.all_to_all(x, 'det', 0, 0, axis_index_groups=halves, tiled=True)  15.6 us
    all_to_all x3, waiting for transfers between devices, serve(): return lax.all_to_all(x, 'det', 0, 0, axis_index_groups=halves, tiled=True)  12.9 us
    pallas_call x1, Pallas kernels, per_device(): pl.pallas_call(image_kernel, out_shape=[strip, edge, edge, jax.ShapeDtype...  9.51 us
    pallas_call x1, Pallas kernels, per_device(): pl.pallas_call(functools.partial(first_kernel, pixels), out_shape=[strip,...  8.96 us
    pallas_call x3, Pallas kernels, pick(): pl.pallas_call(functools.partial(pick_kernel, plane), out_shape=jax.Shape...  8.17 us
    ppermute x2, starting transfers between devices, edges(): before = lax.ppermute(bottom, axis, up)  7.75 us
    pallas_call x1, Pallas kernels, per_device(): pl.pallas_call(second_kernel, out_shape=strip, in_specs=[vmem] * 4, out_s...  5.96 us
  transfers between devices with their start and end apart: 11, of which 5 were waited for; matrix products, arithmetic and copies ran while one was open for 4% of the time, Pallas kernels for 12%

profile of v5, /device:TPU:1, one launch (start us, length us, event | category | flops | bytes accessed | tf_op | source)
XLA Modules:
  0.0 137.8 jit_solution(8641203066019320969)
XLA Ops:
  0.7 0.7 compare_and_fusion.1
  1.4 0.9 select_reduce_fusion.1
  3.0 2.7 %pick_blocks.3 = f32[16,2,64,256]{3,2,1,0:T(8,128)} custom-call(s32[16]{0:T(128)} %reshape.10.picks, f32[8,2,64,256]{3,2,1,0:T(8,128)} %source.1), custom_call_target="tpu_custom_call" | custom-call | tf_op jit(solution)/shard_map/pick_blocks/pallas_call | solution.py:151
  5.7 5.3 %all-to-all-start = ((f32[16,2,64,256]{3,2,1,0:T(8,128)}), f32[16,2,64,256]{3,2,1,0:T(8,128)S(1)}, u32[]{:S(2)}, u32[]{:S(2)}) async-start(f32[16,2,64,256]{3,2,1,0:T(8,128)} %pick_blocks.3), calls=%async_computation | async-start | bytes 4194304 | tf_op jit(solution)/shard_map/all_to_all | solution.py:520
  11.0 2.3 %collective-permute-start = (f32[8,2,64,256]{3,2,1,0:T(8,128)}, f32[8,2,64,256]{3,2,1,0:T(8,128)S(1)}, u32[]{:S(2)}, u32[]{:S(2)}) collective-permute-start(f32[8,2,64,256]{3,2,1,0:T(8,128)} %source.1), channel_id=1, source_target_pairs={{0,8},{1,9},{2,10},{3,11},{4,12},{5,13},{6,14},{7,15},{8,0},{9,1},... | collective-permute-start | bytes 3145736 | tf_op jit(solution)/shard_map/ppermute | solution.py:522
  13.4 0.6 reshape.11.picks
  14.0 1.2 compare_convert_fusion
  15.3 2.8 %science_stamps.1 = (f32[128,128]{1,0:T(8,128)}, f32[128,128]{1,0:T(8,128)}, f32[8,128]{1,0:T(8,128)}) custom-call(s32[16]{0:T(128)} %bitcast.21, s32[16]{0:T(128)} %bitcast.24, f32[64,4096]{1,0:T(8,128)} %science.3, f32[64,4096]{1,0:T(8,128)} %variance.1), custom_call_target="tpu_custom_call" | custom-call | tf_op jit(solution)/shard_map/science_stamps/pallas_call | solution.py:536
  18.1 0.7 fusion.1.slots
  18.8 37.9 %collective-permute-done.source = f32[8,2,64,256]{3,2,1,0:T(8,128)S(1)} collective-permute-done((f32[8,2,64,256]{3,2,1,0:T(8,128)}, f32[8,2,64,256]{3,2,1,0:T(8,128)S(1)}, u32[]{:S(2)}, u32[]{:S(2)}) %collective-permute-start) | collective-permute-done | bytes 1048608 | tf_op jit(solution)/shard_map/ppermute | solution.py:522
  56.7 1.6 %all-to-all-done.near = f32[16,2,64,256]{3,2,1,0:T(8,128)S(1)} async-done(((f32[16,2,64,256]{3,2,1,0:T(8,128)}), f32[16,2,64,256]{3,2,1,0:T(8,128)S(1)}, u32[]{:S(2)}, u32[]{:S(2)}) %all-to-all-start) | async-done | bytes 2097184 | tf_op jit(solution)/shard_map/all_to_all | solution.py:520
  58.3 3.1 %pick_blocks.5 = f32[16,64,256]{2,1,0:T(8,128)} custom-call(s32[16]{0:T(128)} %reshape.11.picks, f32[8,2,64,256]{3,2,1,0:T(8,128)} %copy-done.18), custom_call_target="tpu_custom_call" | custom-call | tf_op jit(solution)/shard_map/pick_blocks/pallas_call | solution.py:151
  61.5 5.9 %all-to-all-start.1 = ((f32[16,64,256]{2,1,0:T(8,128)}), f32[16,64,256]{2,1,0:T(8,128)S(1)}, u32[]{:S(2)}, u32[]{:S(2)}) async-start(f32[16,64,256]{2,1,0:T(8,128)} %pick_blocks.5), calls=%async_computation.1 | async-start | bytes 2097152 | tf_op jit(solution)/shard_map/all_to_all | solution.py:520
  67.4 2.3 %pick_blocks.4 = f32[16,64,256]{2,1,0:T(8,128)} custom-call(s32[16]{0:T(128)} %reshape.11.picks, f32[8,2,64,256]{3,2,1,0:T(8,128)} %copy-done.18), custom_call_target="tpu_custom_call" | custom-call | tf_op jit(solution)/shard_map/pick_blocks/pallas_call | solution.py:151
  69.7 11.3 %all-to-all-done.1.far = f32[16,64,256]{2,1,0:T(8,128)S(1)} async-done(((f32[16,64,256]{2,1,0:T(8,128)}), f32[16,64,256]{2,1,0:T(8,128)S(1)}, u32[]{:S(2)}, u32[]{:S(2)}) %all-to-all-start.1) | async-done | bytes 1048608 | tf_op jit(solution)/shard_map/all_to_all | solution.py:520
  81.0 1.0 copy-done.20
  82.0 4.3 %all-to-all-start.2 = ((f32[16,64,256]{2,1,0:T(8,128)}), f32[16,64,256]{2,1,0:T(8,128)S(1)}, u32[]{:S(2)}, u32[]{:S(2)}) async-start(f32[16,64,256]{2,1,0:T(8,128)} %pick_blocks.4), calls=%async_computation.2 | async-start | bytes 2097152 | tf_op jit(solution)/shard_map/all_to_all | solution.py:520
  86.4 9.5 %stamp_images.1 = (f32[64,4096]{1,0:T(8,128)}, f32[16,4096]{1,0:T(8,128)}, f32[16,4096]{1,0:T(8,128)}, bf16[64,16384]{1,0:T(8,128)(2,1)}, f32[32,128]{1,0:T(8,128)}) custom-call(s32[16]{0:T(128)} %bitcast.22, s32[16]{0:T(128)} %bitcast.25, s32[16]{0:T(128)} %fusion.1.slots, s32[16]{0:T(128)} %get-tuple-element.30.is_near, f32[16,2,64,256]{3,2,1,0:T(8,128)} %copy-done, ...), custom_call_target="tpu_custom_call" | custom-call | tf_op jit(solution)/shard_map/stamp_images/pallas_call | solution.py:555
  95.9 3.5 %collective-permute-start.4 = (f32[16,4096]{1,0:T(8,128)}, f32[16,4096]{1,0:T(8,128)S(1)}, u32[]{:S(2)}, u32[]{:S(2)}) collective-permute-start(f32[16,4096]{1,0:T(8,128)} %get-tuple-element.41), channel_id=1, source_target_pairs={{0,1},{1,2},{2,3},{3,4},{4,5},{5,6},{6,7},{7,8},{8,9},{9,10},{10,1... | collective-permute-start | bytes 786440 | tf_op jit(solution)/shard_map/ppermute | solution.py:486
  99.4 1.9 %collective-permute-start.5 = (f32[16,4096]{1,0:T(8,128)}, f32[16,4096]{1,0:T(8,128)}, u32[]{:S(2)}, u32[]{:S(2)}) collective-permute-start(f32[16,4096]{1,0:T(8,128)} %get-tuple-element.43), channel_id=1, source_target_pairs={{1,0},{2,1},{3,2},{4,3},{5,4},{6,5},{7,6},{8,7},{9,8},{10,9},{11,1... | collective-permute-start | bytes 786440 | tf_op jit(solution)/shard_map/ppermute | solution.py:487
  101.5 1.6 %copy-done.3 = bf16[64,16384]{1,0:T(8,128)(2,1)S(1)} copy-done((bf16[64,16384]{1,0:T(8,128)(2,1)S(1)}, bf16[64,16384]{1,0:T(8,128)(2,1)}, u32[]{:S(2)}) %copy-start.3) | copy-done | bytes 2097176
  103.0 0.7 copy-done.12
  103.8 2.3 %normal_equations.1 = (f32[64,4096]{1,0:T(8,128)S(1)}, f32[40,128]{1,0:T(8,128)S(1)}) custom-call(s32[16]{0:T(128)S(1)} %bitcast.23, s32[16]{0:T(128)S(1)} %bitcast.26, s32[16]{0:T(128)S(1)} %copy-done.14, s32[16]{0:T(128)S(1)} %copy-done.13, f32[16,2,64,256]{3,2,1,0:T(8,128)S(1)} %copy-done.1, f32[16,64,256]{2,1,0:T(8,128)S(1)} %all-to-all-done.2.far, ...), custom_call_target="tpu_custom_call" | custom-call | tf_op jit(solution)/shard_map/normal_equations/pallas_call | solution.py:576
  106.2 1.9 %collective-permute-start.2 = (f32[40,128]{1,0:T(8,128)S(1)}, f32[40,128]{1,0:T(8,128)S(1)}, u32[]{:S(2)}, u32[]{:S(2)}) collective-permute-start(f32[40,128]{1,0:T(8,128)S(1)} %get-tuple-element.40.p0), channel_id=1, source_target_pairs={{0,2},{1,3},{2,0},{3,1},{4,6},{5,7},{6,4},{7,5},{8,10},{9,11},{10,... | collective-permute-start | bytes 61448 | tf_op jit(solution)/shard_map/ppermute | solution.py:591
  108.1 1.4 collective-permute-start.1
  109.5 0.9 collective-permute-done.1.p1
  110.4 9.0 %solve_and_subtract.1 = (f32[64,4096]{1,0:T(8,128)S(1)}, f32[16,4096]{1,0:T(8,128)S(1)}, f32[16,4096]{1,0:T(8,128)S(1)}, f32[32,128]{1,0:T(8,128)S(1)}, f32[8,128]{1,0:T(8,128)S(1)}) custom-call(f32[40,128]{1,0:T(8,128)S(1)} %get-tuple-element.40.p0, f32[40,128]{1,0:T(8,128)S(1)} %collective-permute-done.1.p1, f32[40,128]{1,0:T(8,128)S(1)} %collective-permute-done.2.p2, ...), custom_call_target="tpu_custom_call" | custom-call | tf_op jit(solution)/shard_map/solve_and_subtract/pallas_call | solution.py:599
  120.0 4.2 %collective-permute-start.6 = (f32[16,4096]{1,0:T(8,128)S(1)}, f32[16,4096]{1,0:T(8,128)S(1)}, u32[]{:S(2)}, u32[]{:S(2)}) collective-permute-start(f32[16,4096]{1,0:T(8,128)S(1)} %get-tuple-element.45), channel_id=1, source_target_pairs={{0,1},{1,2},{2,3},{3,4},{4,5},{5,6},{6,7},{7,8},{8,9},{9,10},{10,1... | collective-permute-start | bytes 786440 | tf_op jit(solution)/shard_map/ppermute | solution.py:486
  124.2 1.9 %collective-permute-start.7 = (f32[16,4096]{1,0:T(8,128)S(1)}, f32[16,4096]{1,0:T(8,128)S(1)}, u32[]{:S(2)}, u32[]{:S(2)}) collective-permute-start(f32[16,4096]{1,0:T(8,128)S(1)} %get-tuple-element.47), channel_id=1, source_target_pairs={{1,0},{2,1},{3,2},{4,3},{5,4},{6,5},{7,6},{8,7},{9,8},{10,9},{11,1... | collective-permute-start | bytes 786440 | tf_op jit(solution)/shard_map/ppermute | solution.py:487
  126.1 2.4 %add_multiply_fusion = f32[64,4096]{1,0:T(8,128)} fusion(f32[64,4096]{1,0:T(8,128)S(1)} %copy-done.19, f32[64,4096]{1,0:T(8,128)S(1)} %get-tuple-element.49, f32[]{:T(128)} %bitcast.8, f32[]{:T(128)} %bitcast.7), kind=kLoop, calls=%fused_computation | loop fusion | flops 786432 | bytes 3145736 | tf_op jit(solution)/shard_map/mul | solution.py:615
  128.5 3.3 %collective-permute-done.7.after = f32[16,4096]{1,0:T(8,128)S(1)} collective-permute-done((f32[16,4096]{1,0:T(8,128)S(1)}, f32[16,4096]{1,0:T(8,128)S(1)}, u32[]{:S(2)}, u32[]{:S(2)}) %collective-permute-start.7) | collective-permute-done | bytes 262176 | tf_op jit(solution)/shard_map/ppermute | solution.py:487
  131.9 6.0 %decorrelate.1 = f32[64,4096]{1,0:T(8,128)} custom-call(f32[32,128]{1,0:T(8,128)S(1)} %get-tuple-element.44.filter_t, f32[16,4096]{1,0:T(8,128)S(1)} %collective-permute-done.6.before, f32[64,4096]{1,0:T(8,128)S(1)} %get-tuple-element.46.own, f32[16,4096]{1,0:T(8,128)S(1)} %collective-permute-done.7.after), custom_call_target="tpu_custom_call" | custom-call | tf_op jit(solution)/shard_map/decorrelate/pallas_call | solution.py:616
  (52 shorter events, 1.6 us)
Async XLA Ops:
  5.7 52.6 %all-to-all-start = ((f32[16,2,64,256]{3,2,1,0:T(8,128)}), f32[16,2,64,256]{3,2,1,0:T(8,128)S(1)}, u32[]{:S(2)}, u32[]{:S(2)}) async-start(f32[16,2,64,256]{3,2,1,0:T(8,128)} %pick_blocks.3), calls=%async_computation | async-start | bytes 4194304 | tf_op jit(solution)/shard_map/all_to_all | solution.py:520
  11.0 45.7 %collective-permute-start = (f32[8,2,64,256]{3,2,1,0:T(8,128)}, f32[8,2,64,256]{3,2,1,0:T(8,128)S(1)}, u32[]{:S(2)}, u32[]{:S(2)}) collective-permute-start(f32[8,2,64,256]{3,2,1,0:T(8,128)} %source.1), channel_id=1, source_target_pairs={{0,8},{1,9},{2,10},{3,11},{4,12},{5,13},{6,14},{7,15},{8,0},{9,1},... | collective-permute-start | bytes 3145736 | tf_op jit(solution)/shard_map/ppermute | solution.py:522
  56.7 1.6 %copy-start.18 = (f32[8,2,64,256]{3,2,1,0:T(8,128)}, f32[8,2,64,256]{3,2,1,0:T(8,128)S(1)}, u32[]{:S(2)}) copy-start(f32[8,2,64,256]{3,2,1,0:T(8,128)S(1)} %collective-permute-done.source) | copy-start | bytes 3145732
  58.3 3.1 %copy-start = (f32[16,2,64,256]{3,2,1,0:T(8,128)}, f32[16,2,64,256]{3,2,1,0:T(8,128)S(1)}, u32[]{:S(2)}) copy-start(f32[16,2,64,256]{3,2,1,0:T(8,128)S(1)} %all-to-all-done.near) | copy-start | bytes 6291460
  61.5 19.5 %all-to-all-start.1 = ((f32[16,64,256]{2,1,0:T(8,128)}), f32[16,64,256]{2,1,0:T(8,128)S(1)}, u32[]{:S(2)}, u32[]{:S(2)}) async-start(f32[16,64,256]{2,1,0:T(8,128)} %pick_blocks.5), calls=%async_computation.1 | async-start | bytes 2097152 | tf_op jit(solution)/shard_map/all_to_all | solution.py:520
  81.0 1.0 copy-start.20
  82.0 19.4 %all-to-all-start.2 = ((f32[16,64,256]{2,1,0:T(8,128)}), f32[16,64,256]{2,1,0:T(8,128)S(1)}, u32[]{:S(2)}, u32[]{:S(2)}) async-start(f32[16,64,256]{2,1,0:T(8,128)} %pick_blocks.4), calls=%async_computation.2 | async-start | bytes 2097152 | tf_op jit(solution)/shard_map/all_to_all | solution.py:520
  86.3 15.1 %copy-start.1 = (f32[16,2,64,256]{3,2,1,0:T(8,128)S(1)}, f32[16,2,64,256]{3,2,1,0:T(8,128)}, u32[]{:S(2)}) copy-start(f32[16,2,64,256]{3,2,1,0:T(8,128)} %copy-done) | copy-start | bytes 6291460
  86.3 15.1 %copy-start.7 = (f32[128,128]{1,0:T(8,128)S(1)}, f32[128,128]{1,0:T(8,128)}, u32[]{:S(2)}) copy-start(f32[128,128]{1,0:T(8,128)} %get-tuple-element.37.variance_stamps) | copy-start | bytes 196612
  86.3 15.1 %copy-start.13 = (s32[16]{0:T(128)S(1)}, s32[16]{0:T(128)}, u32[]{:S(2)}) copy-start(s32[16]{0:T(128)} %get-tuple-element.30.is_near) | copy-start | bytes 196
  86.3 15.1 %copy-start.14 = (s32[16]{0:T(128)S(1)}, s32[16]{0:T(128)}, u32[]{:S(2)}) copy-start(s32[16]{0:T(128)} %fusion.1.slots) | copy-start | bytes 196
  86.3 15.1 %copy-start.15 = (s32[1,16]{1,0:T(1,128)S(1)}, s32[1,16]{1,0:T(1,128)}, u32[]{:S(2)}) copy-start(s32[1,16]{1,0:T(1,128)} %param.23) | copy-start | bytes 196
  86.3 15.1 %copy-start.16 = (s32[1,16]{1,0:T(1,128)S(1)}, s32[1,16]{1,0:T(1,128)}, u32[]{:S(2)}) copy-start(s32[1,16]{1,0:T(1,128)} %param.24) | copy-start | bytes 196
  86.3 15.1 %copy-start.17 = (f32[8,128]{1,0:T(8,128)S(1)}, f32[8,128]{1,0:T(8,128)}, u32[]{:S(2)}) copy-start(f32[8,128]{1,0:T(8,128)} %get-tuple-element.39.variance_sum) | copy-start | bytes 12292
  95.9 13.6 %collective-permute-start.4 = (f32[16,4096]{1,0:T(8,128)}, f32[16,4096]{1,0:T(8,128)S(1)}, u32[]{:S(2)}, u32[]{:S(2)}) collective-permute-start(f32[16,4096]{1,0:T(8,128)} %get-tuple-element.41), channel_id=1, source_target_pairs={{0,1},{1,2},{2,3},{3,4},{4,5},{5,6},{6,7},{7,8},{8,9},{9,10},{10,1... | collective-permute-start | bytes 786440 | tf_op jit(solution)/shard_map/ppermute | solution.py:486
  99.4 10.0 %collective-permute-start.5 = (f32[16,4096]{1,0:T(8,128)}, f32[16,4096]{1,0:T(8,128)}, u32[]{:S(2)}, u32[]{:S(2)}) collective-permute-start(f32[16,4096]{1,0:T(8,128)} %get-tuple-element.43), channel_id=1, source_target_pairs={{1,0},{2,1},{3,2},{4,3},{5,4},{6,5},{7,6},{8,7},{9,8},{10,9},{11,1... | collective-permute-start | bytes 786440 | tf_op jit(solution)/shard_map/ppermute | solution.py:487
  101.4 1.6 %copy-start.3 = (bf16[64,16384]{1,0:T(8,128)(2,1)S(1)}, bf16[64,16384]{1,0:T(8,128)(2,1)}, u32[]{:S(2)}) copy-start(bf16[64,16384]{1,0:T(8,128)(2,1)} %get-tuple-element.36.flat_x) | copy-start | bytes 6291460
  103.0 0.7 copy-start.12
  103.8 6.6 %copy-start.2 = (f32[64,4096]{1,0:T(8,128)S(1)}, f32[64,4096]{1,0:T(8,128)}, u32[]{:S(2)}) copy-start(f32[64,4096]{1,0:T(8,128)} %science.3) | copy-start | bytes 3145732
  103.8 6.6 %copy-start.4 = (f32[64,4096]{1,0:T(8,128)S(1)}, f32[64,4096]{1,0:T(8,128)}, u32[]{:S(2)}) copy-start(f32[64,4096]{1,0:T(8,128)} %get-tuple-element.42.own) | copy-start | bytes 3145732
  103.8 6.6 %copy-start.5 = (f32[256,256]{1,0:T(8,128)S(1)}, f32[256,256]{1,0:T(8,128)}, u32[]{:S(2)}) copy-start(f32[256,256]{1,0:T(8,128)} %constant.106.clone.right) | copy-start | bytes 786436
  103.8 6.6 %copy-start.6 = (f32[256,128]{1,0:T(8,128)S(1)}, f32[256,128]{1,0:T(8,128)}, u32[]{:S(2)}) copy-start(f32[256,128]{1,0:T(8,128)} %constant.108.clone.back_right) | copy-start | bytes 393220
  103.8 6.6 %copy-start.8 = (f32[64,32]{1,0:T(8,128)S(1)}, f32[64,32]{1,0:T(8,128)}, u32[]{:S(2)}) copy-start(f32[64,32]{1,0:T(8,128)} %constant.107.clone.back_left) | copy-start | bytes 24580
  103.8 6.6 %copy-start.9 = (f32[64,32]{1,0:T(8,128)S(1)}, f32[64,32]{1,0:T(8,128)}, u32[]{:S(2)}) copy-start(f32[64,32]{1,0:T(8,128)} %constant.105.clone.left) | copy-start | bytes 24580
  103.8 6.6 %copy-start.10 = (f32[32,128]{1,0:T(8,128)S(1)}, f32[32,128]{1,0:T(8,128)}, u32[]{:S(2)}) copy-start(f32[32,128]{1,0:T(8,128)} %constant.104.clone.lu) | copy-start | bytes 49156
  103.8 6.6 %copy-start.11 = (f32[32,32]{1,0:T(8,128)S(1)}, f32[32,32]{1,0:T(8,128)}, u32[]{:S(2)}) copy-start(f32[32,32]{1,0:T(8,128)} %constant.103.clone.lv) | copy-start | bytes 12292
  106.1 20.0 %copy-start.19 = (f32[64,4096]{1,0:T(8,128)S(1)}, f32[64,4096]{1,0:T(8,128)}, u32[]{:S(2)}) copy-start(f32[64,4096]{1,0:T(8,128)} %variance.1) | copy-start | bytes 3145732
  106.2 3.3 %collective-permute-start.3 = (f32[40,128]{1,0:T(8,128)S(1)}, f32[40,128]{1,0:T(8,128)S(1)}, u32[]{:S(2)}, u32[]{:S(2)}) collective-permute-start(f32[40,128]{1,0:T(8,128)S(1)} %get-tuple-element.40.p0), channel_id=1, source_target_pairs={{0,3},{1,0},{2,1},{3,2},{4,7},{5,4},{6,5},{7,6},{8,11},{9,8},{10,9... | collective-permute-start | bytes 61448 | tf_op jit(solution)/shard_map/ppermute | solution.py:591
  106.2 3.2 %collective-permute-start.2 = (f32[40,128]{1,0:T(8,128)S(1)}, f32[40,128]{1,0:T(8,128)S(1)}, u32[]{:S(2)}, u32[]{:S(2)}) collective-permute-start(f32[40,128]{1,0:T(8,128)S(1)} %get-tuple-element.40.p0), channel_id=1, source_target_pairs={{0,2},{1,3},{2,0},{3,1},{4,6},{5,7},{6,4},{7,5},{8,10},{9,11},{10,... | collective-permute-start | bytes 61448 | tf_op jit(solution)/shard_map/ppermute | solution.py:591
  108.1 2.3 %collective-permute-start.1 = (f32[40,128]{1,0:T(8,128)S(1)}, f32[40,128]{1,0:T(8,128)S(1)}, u32[]{:S(2)}, u32[]{:S(2)}) collective-permute-start(f32[40,128]{1,0:T(8,128)S(1)} %get-tuple-element.40.p0), channel_id=1, source_target_pairs={{0,1},{1,2},{2,3},{3,0},{4,5},{5,6},{6,7},{7,4},{8,9},{9,10},{10,1... | collective-permute-start | bytes 61448 | tf_op jit(solution)/shard_map/ppermute | solution.py:591
  120.0 8.6 %collective-permute-start.6 = (f32[16,4096]{1,0:T(8,128)S(1)}, f32[16,4096]{1,0:T(8,128)S(1)}, u32[]{:S(2)}, u32[]{:S(2)}) collective-permute-start(f32[16,4096]{1,0:T(8,128)S(1)} %get-tuple-element.45), channel_id=1, source_target_pairs={{0,1},{1,2},{2,3},{3,4},{4,5},{5,6},{6,7},{7,8},{8,9},{9,10},{10,1... | collective-permute-start | bytes 786440 | tf_op jit(solution)/shard_map/ppermute | solution.py:486
  124.2 7.7 %collective-permute-start.7 = (f32[16,4096]{1,0:T(8,128)S(1)}, f32[16,4096]{1,0:T(8,128)S(1)}, u32[]{:S(2)}, u32[]{:S(2)}) collective-permute-start(f32[16,4096]{1,0:T(8,128)S(1)} %get-tuple-element.47), channel_id=1, source_target_pairs={{1,0},{2,1},{3,2},{4,3},{5,4},{6,5},{7,6},{8,7},{9,8},{10,9},{11,1... | collective-permute-start | bytes 786440 | tf_op jit(solution)/shard_map/ppermute | solution.py:487

commit v6 on v5

--- a/solution.py
+++ b/solution.py
@@ -100,7 +100,7 @@
     right = np.block([[c, -s], [-s, -c]])
     back_left = np.block([[c, -s], [s, c]])
     back_right = np.concatenate([c, -s], 0) / (SS * SS)
-    return [x.astype(np.float32) for x in (left, right, back_left, back_right, ones)]
+    return [np.concatenate(split_host(x), 0) for x in (left, right, back_left, back_right, ones)]
 
 
 def basis_tables():
@@ -159,6 +159,46 @@
     )(picks, source)
 
 
+def pick_near_kernel(axis, half, requests, source, out, sem):
+    owner = lax.axis_index(axis)
+    held = source.shape[0]
+    base = owner // half * half
+
+    def copies(d):
+        first = second = found = jnp.int32(0)
+        for j in range(requests.shape[1]):
+            local = requests[base + d, j] - owner * held
+            mine = (local >= 0) & (local < held)
+            first = jnp.where(mine & (found == 0), local, first)
+            second = jnp.where(mine & (found > 0), local, second)
+            found = jnp.where(mine, 1, found)
+        return [
+            pltpu.make_async_copy(source.at[block], out.at[2 * d + t], sem.at[2 * d + t])
+            for t, block in enumerate((first, second))
+        ]
+
+    started = []
+    for d in range(half):
+        started += copies(d)
+        started[-2].start()
+        started[-1].start()
+    for copy in started:
+        copy.wait()
+
+
+def pick_near(axis, half, requests, source):
+    count = 2 * half
+    return pl.pallas_call(
+        functools.partial(pick_near_kernel, axis, half),
+        out_shape=jax.ShapeDtypeStruct((count,) + source.shape[1:], source.dtype),
+        in_specs=[pl.BlockSpec(memory_space=SMEM), pl.BlockSpec(memory_space=VMEM)],
+        out_specs=pl.BlockSpec(memory_space=pl.ANY),
+        scratch_shapes=[pltpu.SemaphoreType.DMA((count,))],
+        compiler_params=pltpu.CompilerParams(vmem_limit_bytes=VMEM_LIMIT),
+        name="pick_near_blocks",
+    )(requests, source)
+
+
 def lay_strip(slots, is_near, near, far, plane, out, sem):
     needed = slots.shape[0]
     width = near.shape[3]
@@ -191,6 +231,18 @@
 def split(x):
     high = x.astype(jnp.bfloat16)
     return high, (x - high.astype(jnp.float32)).astype(jnp.bfloat16)
+
+
+def dot_left(table, x):
+    half = table.shape[0] // 2
+    high, low = split(x)
+    return dot16(table[:half, :], high) + (dot16(table[half:, :], high) + dot16(table[:half, :], low))
+
+
+def dot_right(x, table):
+    half = table.shape[0] // 2
+    high, low = split(x)
+    return dot16(high, table[:half, :]) + (dot16(low, table[:half, :]) + dot16(high, table[half:, :]))
 
 
 def stamp_place(stamp_rows, stamp_cols, stamp, columns):
@@ -288,7 +340,7 @@
     sci = jnp.concatenate(sciences, 0)
     tmp = jnp.concatenate(templates, 0)
     side = groups * SS
-    first = dot(left_ref[...], jnp.concatenate([sci, tmp], 1))
+    first = dot_left(left_ref, jnp.concatenate([sci, tmp], 1))
     first = jnp.concatenate(
         [
             jnp.concatenate([first[:side, :128], first[side:, :128]], 1),
@@ -296,17 +348,17 @@
         ],
         0,
     )
-    second = dot(first, right_ref[...])
+    second = dot_right(first, right_ref)
     sre, sim = second[:side, :128], second[:side, 128:]
     tre, tim = second[side:, :128], second[side:, 128:]
     cross_re = sre * tre + sim * tim
     cross_im = sim * tre - sre * tim
     magnitude = jnp.sqrt(cross_re * cross_re + cross_im * cross_im)
-    mean = dot(dot(ones_ref[...], magnitude), ones_ref[...]) * (1.0 / (SS * SS))
+    mean = dot_right(dot_left(ones_ref, magnitude), ones_ref) * (1.0 / (SS * SS))
     scaling = 1.0 / jnp.maximum(magnitude, 0.25 * (mean + 1e-06))
     unit = jnp.concatenate([cross_re * scaling, cross_im * scaling], 0)
-    back = dot(back_left_ref[...], unit)
-    surface = dot(jnp.concatenate([back[:side], back[side:]], 1), back_right_ref[...])
+    back = dot_left(back_left_ref, unit)
+    surface = dot_right(jnp.concatenate([back[:side], back[side:]], 1), back_right_ref)
     narrow = lane[:, :128]
     for g in range(groups):
         best = jnp.max(surface[g * SS : (g + 1) * SS], axis=0, keepdims=True)
@@ -322,7 +374,9 @@
 
 
 def normal_kernel(stamp_rows, stamp_cols, slots, is_near, near, far, flat_x, variance_stamps,
-                  stamp_weights, variance_sum, template_variance, out, flat_y, sem):
+                  stamp_weights, variance_sum, template_variance, out, images, flat_y, sem, images_sem):
+    load = pltpu.make_async_copy(flat_x, images, images_sem)
+    load.start()
     lay_strip(slots, is_near, near, far, 1, template_variance, sem)
     _, columns = template_variance.shape
     stamps = stamp_rows.shape[0]
@@ -339,14 +393,15 @@
         pixel_weight.append(stamp_weights[g * 8 : g * 8 + 1, :] / weight)
     pixel_weight = jnp.concatenate(pixel_weight, 1)
     wide = groups * 128
+    load.wait()
     for r in range(SS):
         at = slice(r * wide, (r + 1) * wide)
-        pair = flat_x[:, at].astype(jnp.float32)
+        pair = images[:, at].astype(jnp.float32)
         y = (pair[:32] + pair[32:]) * pixel_weight[r : r + 1, :]
         high = y.astype(jnp.bfloat16).astype(jnp.float32)
         flat_y[:, at] = jnp.concatenate([high, y - high], 0).astype(jnp.bfloat16)
     gram = lax.dot_general(
-        flat_y[...], flat_x[...], (((1,), (1,)), ((), ())), preferred_element_type=jnp.float32
+        flat_y[...], images[...], (((1,), (1,)), ((), ())), preferred_element_type=jnp.float32
     )
     gram = widen(gram[:32] + gram[32:])
     out[:32, :] = gram + pltpu.roll(gram, 96, 1)
@@ -520,7 +575,7 @@
         return lax.all_to_all(x, "det", 0, 0, axis_index_groups=halves, tiled=True)
 
     partner_blocks = lax.ppermute(template_blocks, "det", across_halves)
-    near = serve(pick(picks_of(device), template_blocks))
+    near = serve(pick_near("det", half, requests, template_blocks))
     far_picks = picks_of(partner)
     vmem, smem, anywhere = (pl.BlockSpec(memory_space=m) for m in (VMEM, SMEM, pl.ANY))
     rows, cols = stamp_rows[0], stamp_cols[0]
@@ -576,13 +631,15 @@
     template_variance, partial = pl.pallas_call(
         normal_kernel,
         out_shape=[strip, jax.ShapeDtypeStruct((40, 128), jnp.float32)],
-        in_specs=[smem] * 4 + [anywhere] * 2 + [vmem] * 4,
+        in_specs=[smem] * 4 + [anywhere] * 3 + [vmem] * 3,
         out_specs=[vmem] * 2,
         scratch_shapes=[
             pltpu.VMEM((64, flat), jnp.bfloat16),
+            pltpu.VMEM((64, flat), jnp.bfloat16),
             pltpu.SemaphoreType.DMA((wanted.shape[0],)),
+            pltpu.SemaphoreType.DMA,
         ],
-        compiler_params=small,
+        compiler_params=params,
         name="normal_equations",
     )(rows, cols, slots, is_near, near, far_variance, flat_x, variance_stamps, stamp_weights, variance_sum)
     partials = [partial]

time: 139 us -> 136 us (0.978)
  local copies, waits for them, and re-layouts: 5.33 us -> 3.01 us
  other arithmetic: 5.91 us -> 3.71 us
    pallas_call x0 -> x1, Pallas kernels: none -> 2.83 us  [pick_near(): pl.pallas_call(functools.partial(pick_near_kernel, axis, half), out_shape...]
    pallas_call x3 -> x2, Pallas kernels: 8.17 us -> 5.46 us  [pick(): pl.pallas_call(functools.partial(pick_kernel, plane), out_shape=jax.Shape...]
    pallas_call x1, Pallas kernels: 2.32 us -> 4.79 us  [per_device(): pl.pallas_call(normal_kernel, out_shape=[strip, jax.ShapeDtypeStruct((40,...]
    unnamed x42 -> x32, local copies, waits for them, and re-layouts: 3.36 us -> 1.75 us
  transfers between devices with their start and end apart: 11 -> 11, of which waited for: 5 -> 6; matrix products, arithmetic and copies ran while one was open for 4% -> 3% of each run, Pallas kernels for 12% -> 14%
where the time goes in v6:
time: 136 us; the launch traced here: 135 us
  waiting for transfers between devices  55.9 us (41%)
  Pallas kernels  38.5 us (28%)
  starting transfers between devices  32.6 us (24%)
  other arithmetic  3.71 us (3%)
  local copies, waits for them, and re-layouts  3.01 us (2%)
    ppermute x1, waiting for transfers between devices, per_device(): partner_blocks = lax.ppermute(template_blocks, 'det', across_halves)  38.5 us
    all_to_all x3, starting transfers between devices, serve(): return lax.all_to_all(x, 'det', 0, 0, axis_index_groups=halves, tiled=True)  15.6 us
    all_to_all x3, waiting for transfers between devices, serve(): return lax.all_to_all(x, 'det', 0, 0, axis_index_groups=halves, tiled=True)  12.9 us
    pallas_call x1, Pallas kernels, per_device(): pl.pallas_call(image_kernel, out_shape=[strip, edge, edge, jax.ShapeDtype...  8.63 us
    pallas_call x1, Pallas kernels, per_device(): pl.pallas_call(functools.partial(first_kernel, pixels), out_shape=[strip,...  8 us
    ppermute x2, starting transfers between devices, edges(): before = lax.ppermute(bottom, axis, up)  7.74 us
    pallas_call x1, Pallas kernels, per_device(): pl.pallas_call(second_kernel, out_shape=strip, in_specs=[vmem] * 4, out_s...  5.96 us
    pallas_call x2, Pallas kernels, pick(): pl.pallas_call(functools.partial(pick_kernel, plane), out_shape=jax.Shape...  5.46 us
  transfers between devices with their start and end apart: 11, of which 6 were waited for; matrix products, arithmetic and copies ran while one was open for 3% of the time, Pallas kernels for 14%

profile of v6, /device:TPU:1, one launch (start us, length us, event | category | flops | bytes accessed | tf_op | source)
XLA Modules:
  0.0 134.6 jit_solution(4583909529798829939)
XLA Ops:
  0.6 2.8 %pick_near_blocks.1 = f32[16,2,64,256]{3,2,1,0:T(8,128)} custom-call(s32[16,16]{1,0:T(8,128)} %requests.1, f32[8,2,64,256]{3,2,1,0:T(8,128)} %source.1), custom_call_target="tpu_custom_call" | custom-call | tf_op jit(solution)/shard_map/pick_near_blocks/pallas_call | solution.py:191
  3.5 5.3 %all-to-all-start = ((f32[16,2,64,256]{3,2,1,0:T(8,128)}), f32[16,2,64,256]{3,2,1,0:T(8,128)S(1)}, u32[]{:S(2)}, u32[]{:S(2)}) async-start(f32[16,2,64,256]{3,2,1,0:T(8,128)} %pick_near_blocks.1), calls=%async_computation | async-start | bytes 4194304 | tf_op jit(solution)/shard_map/all_to_all | solution.py:575
  8.8 2.3 %collective-permute-start = (f32[8,2,64,256]{3,2,1,0:T(8,128)}, f32[8,2,64,256]{3,2,1,0:T(8,128)S(1)}, u32[]{:S(2)}, u32[]{:S(2)}) collective-permute-start(f32[8,2,64,256]{3,2,1,0:T(8,128)} %source.1), channel_id=1, source_target_pairs={{0,8},{1,9},{2,10},{3,11},{4,12},{5,13},{6,14},{7,15},{8,0},{9,1},... | collective-permute-start | bytes 3145736 | tf_op jit(solution)/shard_map/ppermute | solution.py:577
  11.4 0.6 reshape.7.picks
  12.0 0.6 compare_convert_fusion
  12.6 2.8 %science_stamps.1 = (f32[128,128]{1,0:T(8,128)}, f32[128,128]{1,0:T(8,128)}, f32[8,128]{1,0:T(8,128)}) custom-call(s32[16]{0:T(128)} %bitcast.20, s32[16]{0:T(128)} %bitcast.23, f32[64,4096]{1,0:T(8,128)} %science.3, f32[64,4096]{1,0:T(8,128)} %variance.1), custom_call_target="tpu_custom_call" | custom-call | tf_op jit(solution)/shard_map/science_stamps/pallas_call | solution.py:591
  15.4 0.6 fusion.1.slots
  16.0 38.5 %collective-permute-done.source = f32[8,2,64,256]{3,2,1,0:T(8,128)S(1)} collective-permute-done((f32[8,2,64,256]{3,2,1,0:T(8,128)}, f32[8,2,64,256]{3,2,1,0:T(8,128)S(1)}, u32[]{:S(2)}, u32[]{:S(2)}) %collective-permute-start) | collective-permute-done | bytes 1048608 | tf_op jit(solution)/shard_map/ppermute | solution.py:577
  54.5 1.6 %all-to-all-done.near = f32[16,2,64,256]{3,2,1,0:T(8,128)S(1)} async-done(((f32[16,2,64,256]{3,2,1,0:T(8,128)}), f32[16,2,64,256]{3,2,1,0:T(8,128)S(1)}, u32[]{:S(2)}, u32[]{:S(2)}) %all-to-all-start) | async-done | bytes 2097184 | tf_op jit(solution)/shard_map/all_to_all | solution.py:575
  56.1 3.1 %pick_blocks.3 = f32[16,64,256]{2,1,0:T(8,128)} custom-call(s32[16]{0:T(128)} %reshape.7.picks, f32[8,2,64,256]{3,2,1,0:T(8,128)} %copy-done.10), custom_call_target="tpu_custom_call" | custom-call | tf_op jit(solution)/shard_map/pick_blocks/pallas_call | solution.py:151
  59.3 5.9 %all-to-all-start.1 = ((f32[16,64,256]{2,1,0:T(8,128)}), f32[16,64,256]{2,1,0:T(8,128)S(1)}, u32[]{:S(2)}, u32[]{:S(2)}) async-start(f32[16,64,256]{2,1,0:T(8,128)} %pick_blocks.3), calls=%async_computation.1 | async-start | bytes 2097152 | tf_op jit(solution)/shard_map/all_to_all | solution.py:575
  65.2 2.3 %pick_blocks.2 = f32[16,64,256]{2,1,0:T(8,128)} custom-call(s32[16]{0:T(128)} %reshape.7.picks, f32[8,2,64,256]{3,2,1,0:T(8,128)} %copy-done.10), custom_call_target="tpu_custom_call" | custom-call | tf_op jit(solution)/shard_map/pick_blocks/pallas_call | solution.py:151
  67.5 11.3 %all-to-all-done.1.far = f32[16,64,256]{2,1,0:T(8,128)S(1)} async-done(((f32[16,64,256]{2,1,0:T(8,128)}), f32[16,64,256]{2,1,0:T(8,128)S(1)}, u32[]{:S(2)}, u32[]{:S(2)}) %all-to-all-start.1) | async-done | bytes 1048608 | tf_op jit(solution)/shard_map/all_to_all | solution.py:575
  78.8 4.3 %all-to-all-start.2 = ((f32[16,64,256]{2,1,0:T(8,128)}), f32[16,64,256]{2,1,0:T(8,128)S(1)}, u32[]{:S(2)}, u32[]{:S(2)}) async-start(f32[16,64,256]{2,1,0:T(8,128)} %pick_blocks.2), calls=%async_computation.2 | async-start | bytes 2097152 | tf_op jit(solution)/shard_map/all_to_all | solution.py:575
  83.1 8.6 %stamp_images.1 = (f32[64,4096]{1,0:T(8,128)}, f32[16,4096]{1,0:T(8,128)}, f32[16,4096]{1,0:T(8,128)}, bf16[64,16384]{1,0:T(8,128)(2,1)}, f32[32,128]{1,0:T(8,128)}) custom-call(s32[16]{0:T(128)} %bitcast.21, s32[16]{0:T(128)} %bitcast.24, s32[16]{0:T(128)} %fusion.1.slots, s32[16]{0:T(128)} %get-tuple-element.30.is_near, f32[16,2,64,256]{3,2,1,0:T(8,128)} %copy-done.9, ...), custom_call_target="tpu_custom_call" | custom-call | tf_op jit(solution)/shard_map/stamp_images/pallas_call | solution.py:610
  91.8 3.5 %collective-permute-start.4 = (f32[16,4096]{1,0:T(8,128)}, f32[16,4096]{1,0:T(8,128)S(1)}, u32[]{:S(2)}, u32[]{:S(2)}) collective-permute-start(f32[16,4096]{1,0:T(8,128)} %get-tuple-element.41), channel_id=1, source_target_pairs={{0,1},{1,2},{2,3},{3,4},{4,5},{5,6},{6,7},{7,8},{8,9},{9,10},{10,1... | collective-permute-start | bytes 786440 | tf_op jit(solution)/shard_map/ppermute | solution.py:541
  95.3 1.9 %collective-permute-start.5 = (f32[16,4096]{1,0:T(8,128)}, f32[16,4096]{1,0:T(8,128)S(1)}, u32[]{:S(2)}, u32[]{:S(2)}) collective-permute-start(f32[16,4096]{1,0:T(8,128)} %get-tuple-element.43), channel_id=1, source_target_pairs={{1,0},{2,1},{3,2},{4,3},{5,4},{6,5},{7,6},{8,7},{9,8},{10,9},{11,1... | collective-permute-start | bytes 786440 | tf_op jit(solution)/shard_map/ppermute | solution.py:542
  97.3 1.0 copy-done.12
  98.3 4.8 %normal_equations.1 = (f32[64,4096]{1,0:T(8,128)}, f32[40,128]{1,0:T(8,128)}) custom-call(s32[16]{0:T(128)} %bitcast.22, s32[16]{0:T(128)} %bitcast.25, s32[16]{0:T(128)} %fusion.1.slots, s32[16]{0:T(128)} %get-tuple-element.30.is_near, f32[16,2,64,256]{3,2,1,0:T(8,128)} %copy-done.9, f32[16,64,256]{2,1,0:T(8,128)} %copy-done.12, ...), custom_call_target="tpu_custom_call" | custom-call | tf_op jit(solution)/shard_map/normal_equations/pallas_call | solution.py:631
  103.1 0.4 collective-permute-start.3
  103.5 1.5 %collective-permute-start.2 = (f32[40,128]{1,0:T(8,128)}, f32[40,128]{1,0:T(8,128)S(1)}, u32[]{:S(2)}, u32[]{:S(2)}) collective-permute-start(f32[40,128]{1,0:T(8,128)} %get-tuple-element.40.p0), channel_id=1, source_target_pairs={{0,2},{1,3},{2,0},{3,1},{4,6},{5,7},{6,4},{7,5},{8,10},{9,11},{10,... | collective-permute-start | bytes 61448 | tf_op jit(solution)/shard_map/ppermute | solution.py:648
  105.0 1.2 collective-permute-start.1
  106.2 0.4 collective-permute-done.3.p3
  106.6 0.7 collective-permute-done.1.p1
  107.4 0.7 copy-done.6
  108.1 8.0 %solve_and_subtract.1 = (f32[64,4096]{1,0:T(8,128)S(1)}, f32[16,4096]{1,0:T(8,128)S(1)}, f32[16,4096]{1,0:T(8,128)S(1)}, f32[32,128]{1,0:T(8,128)S(1)}, f32[8,128]{1,0:T(8,128)S(1)}) custom-call(f32[40,128]{1,0:T(8,128)S(1)} %copy-done.6, f32[40,128]{1,0:T(8,128)S(1)} %collective-permute-done.1.p1, f32[40,128]{1,0:T(8,128)S(1)} %collective-permute-done.2.p2, ...), custom_call_target="tpu_custom_call" | custom-call | tf_op jit(solution)/shard_map/solve_and_subtract/pallas_call | solution.py:656
  116.1 0.6 fusion.2
  116.7 4.2 %collective-permute-start.6 = (f32[16,4096]{1,0:T(8,128)S(1)}, f32[16,4096]{1,0:T(8,128)S(1)}, u32[]{:S(2)}, u32[]{:S(2)}) collective-permute-start(f32[16,4096]{1,0:T(8,128)S(1)} %get-tuple-element.45), channel_id=1, source_target_pairs={{0,1},{1,2},{2,3},{3,4},{4,5},{5,6},{6,7},{7,8},{8,9},{9,10},{10,1... | collective-permute-start | bytes 786440 | tf_op jit(solution)/shard_map/ppermute | solution.py:541
  120.9 1.9 %collective-permute-start.7 = (f32[16,4096]{1,0:T(8,128)S(1)}, f32[16,4096]{1,0:T(8,128)S(1)}, u32[]{:S(2)}, u32[]{:S(2)}) collective-permute-start(f32[16,4096]{1,0:T(8,128)S(1)} %get-tuple-element.47), channel_id=1, source_target_pairs={{1,0},{2,1},{3,2},{4,3},{5,4},{6,5},{7,6},{8,7},{9,8},{10,9},{11,1... | collective-permute-start | bytes 786440 | tf_op jit(solution)/shard_map/ppermute | solution.py:542
  122.9 2.3 %add_multiply_fusion = f32[64,4096]{1,0:T(8,128)} fusion(f32[64,4096]{1,0:T(8,128)S(1)} %copy-done.11, f32[64,4096]{1,0:T(8,128)S(1)} %copy-done.14, f32[]{:T(128)} %bitcast.6, f32[]{:T(128)} %bitcast.5), kind=kLoop, calls=%fused_computation | loop fusion | flops 786432 | bytes 3145736 | tf_op jit(solution)/shard_map/mul | solution.py:672
  125.2 3.4 %collective-permute-done.7.after = f32[16,4096]{1,0:T(8,128)S(1)} collective-permute-done((f32[16,4096]{1,0:T(8,128)S(1)}, f32[16,4096]{1,0:T(8,128)S(1)}, u32[]{:S(2)}, u32[]{:S(2)}) %collective-permute-start.7) | collective-permute-done | bytes 262176 | tf_op jit(solution)/shard_map/ppermute | solution.py:542
  128.6 6.0 %decorrelate.1 = f32[64,4096]{1,0:T(8,128)} custom-call(f32[32,128]{1,0:T(8,128)S(1)} %get-tuple-element.44.filter_t, f32[16,4096]{1,0:T(8,128)S(1)} %collective-permute-done.6.before, f32[64,4096]{1,0:T(8,128)S(1)} %get-tuple-element.46.own, f32[16,4096]{1,0:T(8,128)S(1)} %collective-permute-done.7.after), custom_call_target="tpu_custom_call" | custom-call | tf_op jit(solution)/shard_map/decorrelate/pallas_call | solution.py:673
  (39 shorter events, 0.4 us)
Async XLA Ops:
  3.5 7.6 %copy-start.15 = (s32[16,16]{1,0:T(8,128)S(1)}, s32[16,16]{1,0:T(8,128)}, u32[]{:S(2)}) copy-start(s32[16,16]{1,0:T(8,128)} %requests.1) | copy-start | bytes 3076
  3.5 52.6 %all-to-all-start = ((f32[16,2,64,256]{3,2,1,0:T(8,128)}), f32[16,2,64,256]{3,2,1,0:T(8,128)S(1)}, u32[]{:S(2)}, u32[]{:S(2)}) async-start(f32[16,2,64,256]{3,2,1,0:T(8,128)} %pick_near_blocks.1), calls=%async_computation | async-start | bytes 4194304 | tf_op jit(solution)/shard_map/all_to_all | solution.py:575
  8.8 45.7 %collective-permute-start = (f32[8,2,64,256]{3,2,1,0:T(8,128)}, f32[8,2,64,256]{3,2,1,0:T(8,128)S(1)}, u32[]{:S(2)}, u32[]{:S(2)}) collective-permute-start(f32[8,2,64,256]{3,2,1,0:T(8,128)} %source.1), channel_id=1, source_target_pairs={{0,8},{1,9},{2,10},{3,11},{4,12},{5,13},{6,14},{7,15},{8,0},{9,1},... | collective-permute-start | bytes 3145736 | tf_op jit(solution)/shard_map/ppermute | solution.py:577
  54.5 1.6 %copy-start.10 = (f32[8,2,64,256]{3,2,1,0:T(8,128)}, f32[8,2,64,256]{3,2,1,0:T(8,128)S(1)}, u32[]{:S(2)}) copy-start(f32[8,2,64,256]{3,2,1,0:T(8,128)S(1)} %collective-permute-done.source) | copy-start | bytes 3145732
  56.1 3.1 %copy-start.9 = (f32[16,2,64,256]{3,2,1,0:T(8,128)}, f32[16,2,64,256]{3,2,1,0:T(8,128)S(1)}, u32[]{:S(2)}) copy-start(f32[16,2,64,256]{3,2,1,0:T(8,128)S(1)} %all-to-all-done.near) | copy-start | bytes 6291460
  59.3 19.5 %all-to-all-start.1 = ((f32[16,64,256]{2,1,0:T(8,128)}), f32[16,64,256]{2,1,0:T(8,128)S(1)}, u32[]{:S(2)}, u32[]{:S(2)}) async-start(f32[16,64,256]{2,1,0:T(8,128)} %pick_blocks.3), calls=%async_computation.1 | async-start | bytes 2097152 | tf_op jit(solution)/shard_map/all_to_all | solution.py:575
  78.8 4.3 %copy-start.13 = (f32[16,64,256]{2,1,0:T(8,128)}, f32[16,64,256]{2,1,0:T(8,128)S(1)}, u32[]{:S(2)}) copy-start(f32[16,64,256]{2,1,0:T(8,128)S(1)} %all-to-all-done.1.far) | copy-start | bytes 3145732
  78.8 18.4 %all-to-all-start.2 = ((f32[16,64,256]{2,1,0:T(8,128)}), f32[16,64,256]{2,1,0:T(8,128)S(1)}, u32[]{:S(2)}, u32[]{:S(2)}) async-start(f32[16,64,256]{2,1,0:T(8,128)} %pick_blocks.2), calls=%async_computation.2 | async-start | bytes 2097152 | tf_op jit(solution)/shard_map/all_to_all | solution.py:575
  91.8 14.4 %collective-permute-start.4 = (f32[16,4096]{1,0:T(8,128)}, f32[16,4096]{1,0:T(8,128)S(1)}, u32[]{:S(2)}, u32[]{:S(2)}) collective-permute-start(f32[16,4096]{1,0:T(8,128)} %get-tuple-element.41), channel_id=1, source_target_pairs={{0,1},{1,2},{2,3},{3,4},{4,5},{5,6},{6,7},{7,8},{8,9},{9,10},{10,1... | collective-permute-start | bytes 786440 | tf_op jit(solution)/shard_map/ppermute | solution.py:541
  95.3 10.9 %collective-permute-start.5 = (f32[16,4096]{1,0:T(8,128)}, f32[16,4096]{1,0:T(8,128)S(1)}, u32[]{:S(2)}, u32[]{:S(2)}) collective-permute-start(f32[16,4096]{1,0:T(8,128)} %get-tuple-element.43), channel_id=1, source_target_pairs={{1,0},{2,1},{3,2},{4,3},{5,4},{6,5},{7,6},{8,7},{9,8},{10,9},{11,1... | collective-permute-start | bytes 786440 | tf_op jit(solution)/shard_map/ppermute | solution.py:542
  97.2 1.0 copy-start.12
  98.2 9.1 %copy-start = (f32[64,4096]{1,0:T(8,128)S(1)}, f32[64,4096]{1,0:T(8,128)}, u32[]{:S(2)}) copy-start(f32[64,4096]{1,0:T(8,128)} %science.3) | copy-start | bytes 3145732
  98.2 9.1 %copy-start.1 = (f32[64,4096]{1,0:T(8,128)S(1)}, f32[64,4096]{1,0:T(8,128)}, u32[]{:S(2)}) copy-start(f32[64,4096]{1,0:T(8,128)} %get-tuple-element.42.own) | copy-start | bytes 3145732
  98.2 9.1 %copy-start.2 = (f32[256,256]{1,0:T(8,128)S(1)}, f32[256,256]{1,0:T(8,128)}, u32[]{:S(2)}) copy-start(f32[256,256]{1,0:T(8,128)} %constant.105.clone.right) | copy-start | bytes 786436
  98.2 9.1 %copy-start.3 = (f32[256,128]{1,0:T(8,128)S(1)}, f32[256,128]{1,0:T(8,128)}, u32[]{:S(2)}) copy-start(f32[256,128]{1,0:T(8,128)} %constant.107.clone.back_right) | copy-start | bytes 393220
  98.2 9.1 %copy-start.4 = (f32[64,32]{1,0:T(8,128)S(1)}, f32[64,32]{1,0:T(8,128)}, u32[]{:S(2)}) copy-start(f32[64,32]{1,0:T(8,128)} %constant.106.clone.back_left) | copy-start | bytes 24580
  98.2 9.1 %copy-start.5 = (f32[64,32]{1,0:T(8,128)S(1)}, f32[64,32]{1,0:T(8,128)}, u32[]{:S(2)}) copy-start(f32[64,32]{1,0:T(8,128)} %constant.104.clone.left) | copy-start | bytes 24580
  98.3 9.1 %copy-start.7 = (f32[32,128]{1,0:T(8,128)S(1)}, f32[32,128]{1,0:T(8,128)}, u32[]{:S(2)}) copy-start(f32[32,128]{1,0:T(8,128)} %constant.103.clone.lu) | copy-start | bytes 49156
  98.3 9.1 %copy-start.8 = (f32[32,32]{1,0:T(8,128)S(1)}, f32[32,32]{1,0:T(8,128)}, u32[]{:S(2)}) copy-start(f32[32,32]{1,0:T(8,128)} %constant.102.clone.lv) | copy-start | bytes 12292
  103.1 3.5 %collective-permute-start.3 = (f32[40,128]{1,0:T(8,128)}, f32[40,128]{1,0:T(8,128)S(1)}, u32[]{:S(2)}, u32[]{:S(2)}) collective-permute-start(f32[40,128]{1,0:T(8,128)} %get-tuple-element.40.p0), channel_id=1, source_target_pairs={{0,3},{1,0},{2,1},{3,2},{4,7},{5,4},{6,5},{7,6},{8,11},{9,8},{10,9... | collective-permute-start | bytes 61448 | tf_op jit(solution)/shard_map/ppermute | solution.py:648
  103.5 3.1 %collective-permute-start.2 = (f32[40,128]{1,0:T(8,128)}, f32[40,128]{1,0:T(8,128)S(1)}, u32[]{:S(2)}, u32[]{:S(2)}) collective-permute-start(f32[40,128]{1,0:T(8,128)} %get-tuple-element.40.p0), channel_id=1, source_target_pairs={{0,2},{1,3},{2,0},{3,1},{4,6},{5,7},{6,4},{7,5},{8,10},{9,11},{10,... | collective-permute-start | bytes 61448 | tf_op jit(solution)/shard_map/ppermute | solution.py:648
  105.0 2.3 %collective-permute-start.1 = (f32[40,128]{1,0:T(8,128)}, f32[40,128]{1,0:T(8,128)S(1)}, u32[]{:S(2)}, u32[]{:S(2)}) collective-permute-start(f32[40,128]{1,0:T(8,128)} %get-tuple-element.40.p0), channel_id=1, source_target_pairs={{0,1},{1,2},{2,3},{3,0},{4,5},{5,6},{6,7},{7,4},{8,9},{9,10},{10,1... | collective-permute-start | bytes 61448 | tf_op jit(solution)/shard_map/ppermute | solution.py:648
  107.4 0.7 copy-start.6
  108.1 14.8 %copy-start.11 = (f32[64,4096]{1,0:T(8,128)S(1)}, f32[64,4096]{1,0:T(8,128)}, u32[]{:S(2)}) copy-start(f32[64,4096]{1,0:T(8,128)} %variance.1) | copy-start | bytes 3145732
  108.1 14.8 %copy-start.14 = (f32[64,4096]{1,0:T(8,128)S(1)}, f32[64,4096]{1,0:T(8,128)}, u32[]{:S(2)}) copy-start(f32[64,4096]{1,0:T(8,128)} %get-tuple-element.49) | copy-start | bytes 3145732
  116.7 8.5 %collective-permute-start.6 = (f32[16,4096]{1,0:T(8,128)S(1)}, f32[16,4096]{1,0:T(8,128)S(1)}, u32[]{:S(2)}, u32[]{:S(2)}) collective-permute-start(f32[16,4096]{1,0:T(8,128)S(1)} %get-tuple-element.45), channel_id=1, source_target_pairs={{0,1},{1,2},{2,3},{3,4},{4,5},{5,6},{6,7},{7,8},{8,9},{9,10},{10,1... | collective-permute-start | bytes 786440 | tf_op jit(solution)/shard_map/ppermute | solution.py:541
  120.9 7.7 %collective-permute-start.7 = (f32[16,4096]{1,0:T(8,128)S(1)}, f32[16,4096]{1,0:T(8,128)S(1)}, u32[]{:S(2)}, u32[]{:S(2)}) collective-permute-start(f32[16,4096]{1,0:T(8,128)S(1)} %get-tuple-element.47), channel_id=1, source_target_pairs={{1,0},{2,1},{3,2},{4,3},{5,4},{6,5},{7,6},{8,7},{9,8},{10,9},{11,1... | collective-permute-start | bytes 786440 | tf_op jit(solution)/shard_map/ppermute | solution.py:542

commit v7 on v6

--- a/solution.py
+++ b/solution.py
@@ -108,7 +108,7 @@
     for image, (a, b) in enumerate(PAIRS):
         lv[:KS, image] = LINE[b]
         lu[image, :KS] = LINE[a]
-    return lv.astype(np.float32), lu.astype(np.float32)
+    return np.concatenate(split_host(lv), 0), lu.astype(np.float32)
 
 
 def filter_tables():
@@ -123,7 +123,7 @@
     back_c, back_s = np.zeros((128, 128)), np.zeros((128, 128))
     back_c[:PD, :32], back_s[:PD, :32] = c, s
     back_right = np.concatenate([back_c, -back_s], 0)
-    return [x.astype(np.float32) for x in (left, right, back_left, back_right)]
+    return [np.concatenate(split_host(x), 0) for x in (left, right, back_left, back_right)]
 
 
 def pick_kernel(plane, picks, source, out, sem):
@@ -501,18 +501,18 @@
     coefficients = eliminate(sums[:32, :])
     mean_science = sums[32:33, 0:1] * (1.0 / pixels)
     mean_template = sums[32:33, 1:2] * (1.0 / pixels)
-    kernel_t = dot(lv[...], coefficients * lu[...])
+    kernel_t = dot_left(lv, coefficients * lu[...])
     v_index = lax.broadcasted_iota(jnp.int32, (32, 128), 0)
     u_index = lax.broadcasted_iota(jnp.int32, (32, 128), 1)
     kernel_t = kernel_t + ((v_index == MARGIN) & (u_index == MARGIN)).astype(jnp.float32)
-    step = dot(left[...], kernel_t)
-    both = dot(jnp.concatenate([step[:PD], step[PD:]], 1), right[...])
+    step = dot_left(left, kernel_t)
+    both = dot_right(jnp.concatenate([step[:PD], step[PD:]], 1), right)
     re, im = both[:, :128], both[:, 128:]
     response = jnp.sqrt(
         (mean_science + mean_template) / (mean_science + mean_template * (re * re + im * im))
     )
-    step = dot(back_left[...], response)
-    filter_t = dot(jnp.concatenate([step[:32], step[32:]], 1), back_right[...])
+    step = dot_left(back_left, response)
+    filter_t = dot_right(jnp.concatenate([step[:32], step[32:]], 1), back_right)
     filter_out[...] = filter_t
     powers[0:1, :] = jnp.broadcast_to(total_of(kernel_t * kernel_t), (1, 128))
     powers[1:2, :] = jnp.broadcast_to(total_of(filter_t * filter_t), (1, 128))
@@ -669,7 +669,7 @@
         name="solve_and_subtract",
     )(*partials, science, before, template_image, after, *tables)
     before, after = edges(top, bottom, "det")
-    decorrelated_variance = powers[1, 0] * (variance + template_variance * powers[0, 0])
+    decorrelated_variance = powers[1:2, :1] * (variance + template_variance * powers[:1, :1])
     decorrelated = pl.pallas_call(
         second_kernel,
         out_shape=strip,

time: 136 us -> 136 us (level)
  no operation moved by 1% of the time
where the time goes in v7:
time: 136 us; the launch traced here: 134 us
  waiting for transfers between devices  55.9 us (41%)
  Pallas kernels  38 us (28%)
  starting transfers between devices  32.8 us (24%)
  other arithmetic  3.71 us (3%)
  local copies, waits for them, and re-layouts  3.01 us (2%)
    ppermute x1, waiting for transfers between devices, per_device(): partner_blocks = lax.ppermute(template_blocks, 'det', across_halves)  38.5 us
    all_to_all x3, starting transfers between devices, serve(): return lax.all_to_all(x, 'det', 0, 0, axis_index_groups=halves, tiled=True)  15.6 us
    all_to_all x3, waiting for transfers between devices, serve(): return lax.all_to_all(x, 'det', 0, 0, axis_index_groups=halves, tiled=True)  12.9 us
    pallas_call x1, Pallas kernels, per_device(): pl.pallas_call(image_kernel, out_shape=[strip, edge, edge, jax.ShapeDtype...  8.62 us
    ppermute x2, starting transfers between devices, edges(): before = lax.ppermute(bottom, axis, up)  7.76 us
    pallas_call x1, Pallas kernels, per_device(): pl.pallas_call(functools.partial(first_kernel, pixels), out_shape=[strip,...  7.66 us
    pallas_call x1, Pallas kernels, per_device(): pl.pallas_call(second_kernel, out_shape=strip, in_specs=[vmem] * 4, out_s...  5.97 us
    pallas_call x2, Pallas kernels, pick(): pl.pallas_call(functools.partial(pick_kernel, plane), out_shape=jax.Shape...  5.46 us
  transfers between devices with their start and end apart: 11, of which 6 were waited for; matrix products, arithmetic and copies ran while one was open for 3% of the time, Pallas kernels for 14%

profile of v7, /device:TPU:1, one launch (start us, length us, event | category | flops | bytes accessed | tf_op | source)
XLA Modules:
  0.0 134.2 jit_solution(2040606220311466561)
XLA Ops:
  0.6 2.8 %pick_near_blocks.1 = f32[16,2,64,256]{3,2,1,0:T(8,128)} custom-call(s32[16,16]{1,0:T(8,128)} %requests.1, f32[8,2,64,256]{3,2,1,0:T(8,128)} %source.1), custom_call_target="tpu_custom_call" | custom-call | tf_op jit(solution)/shard_map/pick_near_blocks/pallas_call | solution.py:191
  3.5 5.3 %all-to-all-start = ((f32[16,2,64,256]{3,2,1,0:T(8,128)}), f32[16,2,64,256]{3,2,1,0:T(8,128)S(1)}, u32[]{:S(2)}, u32[]{:S(2)}) async-start(f32[16,2,64,256]{3,2,1,0:T(8,128)} %pick_near_blocks.1), calls=%async_computation | async-start | bytes 4194304 | tf_op jit(solution)/shard_map/all_to_all | solution.py:575
  8.8 2.3 %collective-permute-start = (f32[8,2,64,256]{3,2,1,0:T(8,128)}, f32[8,2,64,256]{3,2,1,0:T(8,128)S(1)}, u32[]{:S(2)}, u32[]{:S(2)}) collective-permute-start(f32[8,2,64,256]{3,2,1,0:T(8,128)} %source.1), channel_id=1, source_target_pairs={{0,8},{1,9},{2,10},{3,11},{4,12},{5,13},{6,14},{7,15},{8,0},{9,1},... | collective-permute-start | bytes 3145736 | tf_op jit(solution)/shard_map/ppermute | solution.py:577
  11.4 0.6 reshape.7.picks
  12.0 0.6 compare_convert_fusion
  12.6 2.8 %science_stamps.1 = (f32[128,128]{1,0:T(8,128)}, f32[128,128]{1,0:T(8,128)}, f32[8,128]{1,0:T(8,128)}) custom-call(s32[16]{0:T(128)} %bitcast.20, s32[16]{0:T(128)} %bitcast.23, f32[64,4096]{1,0:T(8,128)} %science.3, f32[64,4096]{1,0:T(8,128)} %variance.1), custom_call_target="tpu_custom_call" | custom-call | tf_op jit(solution)/shard_map/science_stamps/pallas_call | solution.py:591
  15.4 0.6 fusion.1.slots
  16.0 38.5 %collective-permute-done.source = f32[8,2,64,256]{3,2,1,0:T(8,128)S(1)} collective-permute-done((f32[8,2,64,256]{3,2,1,0:T(8,128)}, f32[8,2,64,256]{3,2,1,0:T(8,128)S(1)}, u32[]{:S(2)}, u32[]{:S(2)}) %collective-permute-start) | collective-permute-done | bytes 1048608 | tf_op jit(solution)/shard_map/ppermute | solution.py:577
  54.5 1.6 %all-to-all-done.near = f32[16,2,64,256]{3,2,1,0:T(8,128)S(1)} async-done(((f32[16,2,64,256]{3,2,1,0:T(8,128)}), f32[16,2,64,256]{3,2,1,0:T(8,128)S(1)}, u32[]{:S(2)}, u32[]{:S(2)}) %all-to-all-start) | async-done | bytes 2097184 | tf_op jit(solution)/shard_map/all_to_all | solution.py:575
  56.1 3.1 %pick_blocks.3 = f32[16,64,256]{2,1,0:T(8,128)} custom-call(s32[16]{0:T(128)} %reshape.7.picks, f32[8,2,64,256]{3,2,1,0:T(8,128)} %copy-done.10), custom_call_target="tpu_custom_call" | custom-call | tf_op jit(solution)/shard_map/pick_blocks/pallas_call | solution.py:151
  59.3 5.9 %all-to-all-start.1 = ((f32[16,64,256]{2,1,0:T(8,128)}), f32[16,64,256]{2,1,0:T(8,128)S(1)}, u32[]{:S(2)}, u32[]{:S(2)}) async-start(f32[16,64,256]{2,1,0:T(8,128)} %pick_blocks.3), calls=%async_computation.1 | async-start | bytes 2097152 | tf_op jit(solution)/shard_map/all_to_all | solution.py:575
  65.2 2.3 %pick_blocks.2 = f32[16,64,256]{2,1,0:T(8,128)} custom-call(s32[16]{0:T(128)} %reshape.7.picks, f32[8,2,64,256]{3,2,1,0:T(8,128)} %copy-done.10), custom_call_target="tpu_custom_call" | custom-call | tf_op jit(solution)/shard_map/pick_blocks/pallas_call | solution.py:151
  67.5 11.3 %all-to-all-done.1.far = f32[16,64,256]{2,1,0:T(8,128)S(1)} async-done(((f32[16,64,256]{2,1,0:T(8,128)}), f32[16,64,256]{2,1,0:T(8,128)S(1)}, u32[]{:S(2)}, u32[]{:S(2)}) %all-to-all-start.1) | async-done | bytes 1048608 | tf_op jit(solution)/shard_map/all_to_all | solution.py:575
  78.8 4.3 %all-to-all-start.2 = ((f32[16,64,256]{2,1,0:T(8,128)}), f32[16,64,256]{2,1,0:T(8,128)S(1)}, u32[]{:S(2)}, u32[]{:S(2)}) async-start(f32[16,64,256]{2,1,0:T(8,128)} %pick_blocks.2), calls=%async_computation.2 | async-start | bytes 2097152 | tf_op jit(solution)/shard_map/all_to_all | solution.py:575
  83.1 8.6 %stamp_images.1 = (f32[64,4096]{1,0:T(8,128)}, f32[16,4096]{1,0:T(8,128)}, f32[16,4096]{1,0:T(8,128)}, bf16[64,16384]{1,0:T(8,128)(2,1)}, f32[32,128]{1,0:T(8,128)}) custom-call(s32[16]{0:T(128)} %bitcast.21, s32[16]{0:T(128)} %bitcast.24, s32[16]{0:T(128)} %fusion.1.slots, s32[16]{0:T(128)} %get-tuple-element.30.is_near, f32[16,2,64,256]{3,2,1,0:T(8,128)} %copy-done.9, ...), custom_call_target="tpu_custom_call" | custom-call | tf_op jit(solution)/shard_map/stamp_images/pallas_call | solution.py:610
  91.8 3.6 %collective-permute-start.4 = (f32[16,4096]{1,0:T(8,128)}, f32[16,4096]{1,0:T(8,128)S(1)}, u32[]{:S(2)}, u32[]{:S(2)}) collective-permute-start(f32[16,4096]{1,0:T(8,128)} %get-tuple-element.41), channel_id=1, source_target_pairs={{0,1},{1,2},{2,3},{3,4},{4,5},{5,6},{6,7},{7,8},{8,9},{9,10},{10,1... | collective-permute-start | bytes 786440 | tf_op jit(solution)/shard_map/ppermute | solution.py:541
  95.3 1.9 %collective-permute-start.5 = (f32[16,4096]{1,0:T(8,128)}, f32[16,4096]{1,0:T(8,128)S(1)}, u32[]{:S(2)}, u32[]{:S(2)}) collective-permute-start(f32[16,4096]{1,0:T(8,128)} %get-tuple-element.43), channel_id=1, source_target_pairs={{1,0},{2,1},{3,2},{4,3},{5,4},{6,5},{7,6},{8,7},{9,8},{10,9},{11,1... | collective-permute-start | bytes 786440 | tf_op jit(solution)/shard_map/ppermute | solution.py:542
  97.3 1.0 copy-done.12
  98.3 4.6 %normal_equations.1 = (f32[64,4096]{1,0:T(8,128)}, f32[40,128]{1,0:T(8,128)}) custom-call(s32[16]{0:T(128)} %bitcast.22, s32[16]{0:T(128)} %bitcast.25, s32[16]{0:T(128)} %fusion.1.slots, s32[16]{0:T(128)} %get-tuple-element.30.is_near, f32[16,2,64,256]{3,2,1,0:T(8,128)} %copy-done.9, f32[16,64,256]{2,1,0:T(8,128)} %copy-done.12, ...), custom_call_target="tpu_custom_call" | custom-call | tf_op jit(solution)/shard_map/normal_equations/pallas_call | solution.py:631
  102.9 0.6 collective-permute-start.3
  103.5 1.3 collective-permute-start.2
  104.8 1.4 %collective-permute-start.1 = (f32[40,128]{1,0:T(8,128)}, f32[40,128]{1,0:T(8,128)S(1)}, u32[]{:S(2)}, u32[]{:S(2)}) collective-permute-start(f32[40,128]{1,0:T(8,128)} %get-tuple-element.40.p0), channel_id=1, source_target_pairs={{0,1},{1,2},{2,3},{3,0},{4,5},{5,6},{6,7},{7,4},{8,9},{9,10},{10,1... | collective-permute-start | bytes 61448 | tf_op jit(solution)/shard_map/ppermute | solution.py:648
  106.2 0.4 collective-permute-done.3.p3
  106.6 0.7 collective-permute-done.1.p1
  107.4 0.7 copy-done.6
  108.1 7.7 %solve_and_subtract.1 = (f32[64,4096]{1,0:T(8,128)S(1)}, f32[16,4096]{1,0:T(8,128)S(1)}, f32[16,4096]{1,0:T(8,128)S(1)}, f32[32,128]{1,0:T(8,128)S(1)}, f32[8,128]{1,0:T(8,128)S(1)}) custom-call(f32[40,128]{1,0:T(8,128)S(1)} %copy-done.6, f32[40,128]{1,0:T(8,128)S(1)} %collective-permute-done.1.p1, f32[40,128]{1,0:T(8,128)S(1)} %collective-permute-done.2.p2, ...), custom_call_target="tpu_custom_call" | custom-call | tf_op jit(solution)/shard_map/solve_and_subtract/pallas_call | solution.py:656
  115.8 0.6 fusion.2
  116.4 4.2 %collective-permute-start.6 = (f32[16,4096]{1,0:T(8,128)S(1)}, f32[16,4096]{1,0:T(8,128)S(1)}, u32[]{:S(2)}, u32[]{:S(2)}) collective-permute-start(f32[16,4096]{1,0:T(8,128)S(1)} %get-tuple-element.45), channel_id=1, source_target_pairs={{0,1},{1,2},{2,3},{3,4},{4,5},{5,6},{6,7},{7,8},{8,9},{9,10},{10,1... | collective-permute-start | bytes 786440 | tf_op jit(solution)/shard_map/ppermute | solution.py:541
  120.6 1.9 %collective-permute-start.7 = (f32[16,4096]{1,0:T(8,128)S(1)}, f32[16,4096]{1,0:T(8,128)S(1)}, u32[]{:S(2)}, u32[]{:S(2)}) collective-permute-start(f32[16,4096]{1,0:T(8,128)S(1)} %get-tuple-element.47), channel_id=1, source_target_pairs={{1,0},{2,1},{3,2},{4,3},{5,4},{6,5},{7,6},{8,7},{9,8},{10,9},{11,1... | collective-permute-start | bytes 786440 | tf_op jit(solution)/shard_map/ppermute | solution.py:542
  122.5 2.3 %add_multiply_fusion = f32[64,4096]{1,0:T(8,128)} fusion(f32[64,4096]{1,0:T(8,128)S(1)} %copy-done.11, f32[64,4096]{1,0:T(8,128)S(1)} %copy-done.14, f32[]{:T(128)} %bitcast.6, f32[]{:T(128)} %bitcast.5), kind=kLoop, calls=%fused_computation | loop fusion | flops 786432 | bytes 3145736 | tf_op jit(solution)/shard_map/mul | solution.py:672
  124.9 3.4 %collective-permute-done.7.after = f32[16,4096]{1,0:T(8,128)S(1)} collective-permute-done((f32[16,4096]{1,0:T(8,128)S(1)}, f32[16,4096]{1,0:T(8,128)S(1)}, u32[]{:S(2)}, u32[]{:S(2)}) %collective-permute-start.7) | collective-permute-done | bytes 262176 | tf_op jit(solution)/shard_map/ppermute | solution.py:542
  128.3 6.0 %decorrelate.1 = f32[64,4096]{1,0:T(8,128)} custom-call(f32[32,128]{1,0:T(8,128)S(1)} %get-tuple-element.44.filter_t, f32[16,4096]{1,0:T(8,128)S(1)} %collective-permute-done.6.before, f32[64,4096]{1,0:T(8,128)S(1)} %get-tuple-element.46.own, f32[16,4096]{1,0:T(8,128)S(1)} %collective-permute-done.7.after), custom_call_target="tpu_custom_call" | custom-call | tf_op jit(solution)/shard_map/decorrelate/pallas_call | solution.py:673
  (39 shorter events, 0.4 us)
Async XLA Ops:
  3.5 7.6 %copy-start.15 = (s32[16,16]{1,0:T(8,128)S(1)}, s32[16,16]{1,0:T(8,128)}, u32[]{:S(2)}) copy-start(s32[16,16]{1,0:T(8,128)} %requests.1) | copy-start | bytes 3076
  3.5 52.6 %all-to-all-start = ((f32[16,2,64,256]{3,2,1,0:T(8,128)}), f32[16,2,64,256]{3,2,1,0:T(8,128)S(1)}, u32[]{:S(2)}, u32[]{:S(2)}) async-start(f32[16,2,64,256]{3,2,1,0:T(8,128)} %pick_near_blocks.1), calls=%async_computation | async-start | bytes 4194304 | tf_op jit(solution)/shard_map/all_to_all | solution.py:575
  8.8 45.7 %collective-permute-start = (f32[8,2,64,256]{3,2,1,0:T(8,128)}, f32[8,2,64,256]{3,2,1,0:T(8,128)S(1)}, u32[]{:S(2)}, u32[]{:S(2)}) collective-permute-start(f32[8,2,64,256]{3,2,1,0:T(8,128)} %source.1), channel_id=1, source_target_pairs={{0,8},{1,9},{2,10},{3,11},{4,12},{5,13},{6,14},{7,15},{8,0},{9,1},... | collective-permute-start | bytes 3145736 | tf_op jit(solution)/shard_map/ppermute | solution.py:577
  54.5 1.6 %copy-start.10 = (f32[8,2,64,256]{3,2,1,0:T(8,128)}, f32[8,2,64,256]{3,2,1,0:T(8,128)S(1)}, u32[]{:S(2)}) copy-start(f32[8,2,64,256]{3,2,1,0:T(8,128)S(1)} %collective-permute-done.source) | copy-start | bytes 3145732
  56.1 3.1 %copy-start.9 = (f32[16,2,64,256]{3,2,1,0:T(8,128)}, f32[16,2,64,256]{3,2,1,0:T(8,128)S(1)}, u32[]{:S(2)}) copy-start(f32[16,2,64,256]{3,2,1,0:T(8,128)S(1)} %all-to-all-done.near) | copy-start | bytes 6291460
  59.3 19.5 %all-to-all-start.1 = ((f32[16,64,256]{2,1,0:T(8,128)}), f32[16,64,256]{2,1,0:T(8,128)S(1)}, u32[]{:S(2)}, u32[]{:S(2)}) async-start(f32[16,64,256]{2,1,0:T(8,128)} %pick_blocks.3), calls=%async_computation.1 | async-start | bytes 2097152 | tf_op jit(solution)/shard_map/all_to_all | solution.py:575
  78.8 4.3 %copy-start.13 = (f32[16,64,256]{2,1,0:T(8,128)}, f32[16,64,256]{2,1,0:T(8,128)S(1)}, u32[]{:S(2)}) copy-start(f32[16,64,256]{2,1,0:T(8,128)S(1)} %all-to-all-done.1.far) | copy-start | bytes 3145732
  78.8 18.5 %all-to-all-start.2 = ((f32[16,64,256]{2,1,0:T(8,128)}), f32[16,64,256]{2,1,0:T(8,128)S(1)}, u32[]{:S(2)}, u32[]{:S(2)}) async-start(f32[16,64,256]{2,1,0:T(8,128)} %pick_blocks.2), calls=%async_computation.2 | async-start | bytes 2097152 | tf_op jit(solution)/shard_map/all_to_all | solution.py:575
  91.8 14.4 %collective-permute-start.4 = (f32[16,4096]{1,0:T(8,128)}, f32[16,4096]{1,0:T(8,128)S(1)}, u32[]{:S(2)}, u32[]{:S(2)}) collective-permute-start(f32[16,4096]{1,0:T(8,128)} %get-tuple-element.41), channel_id=1, source_target_pairs={{0,1},{1,2},{2,3},{3,4},{4,5},{5,6},{6,7},{7,8},{8,9},{9,10},{10,1... | collective-permute-start | bytes 786440 | tf_op jit(solution)/shard_map/ppermute | solution.py:541
  95.3 10.9 %collective-permute-start.5 = (f32[16,4096]{1,0:T(8,128)}, f32[16,4096]{1,0:T(8,128)S(1)}, u32[]{:S(2)}, u32[]{:S(2)}) collective-permute-start(f32[16,4096]{1,0:T(8,128)} %get-tuple-element.43), channel_id=1, source_target_pairs={{1,0},{2,1},{3,2},{4,3},{5,4},{6,5},{7,6},{8,7},{9,8},{10,9},{11,1... | collective-permute-start | bytes 786440 | tf_op jit(solution)/shard_map/ppermute | solution.py:542
  97.3 1.0 copy-start.12
  98.2 9.1 %copy-start = (f32[64,4096]{1,0:T(8,128)S(1)}, f32[64,4096]{1,0:T(8,128)}, u32[]{:S(2)}) copy-start(f32[64,4096]{1,0:T(8,128)} %science.3) | copy-start | bytes 3145732
  98.2 9.1 %copy-start.1 = (f32[64,4096]{1,0:T(8,128)S(1)}, f32[64,4096]{1,0:T(8,128)}, u32[]{:S(2)}) copy-start(f32[64,4096]{1,0:T(8,128)} %get-tuple-element.42.own) | copy-start | bytes 3145732
  98.2 9.1 %copy-start.2 = (bf16[512,256]{1,0:T(8,128)(2,1)S(1)}, bf16[512,256]{1,0:T(8,128)(2,1)}, u32[]{:S(2)}) copy-start(bf16[512,256]{1,0:T(8,128)(2,1)} %constant.105.clone.right) | copy-start | bytes 786436
  98.2 9.1 %copy-start.3 = (bf16[512,128]{1,0:T(8,128)(2,1)S(1)}, bf16[512,128]{1,0:T(8,128)(2,1)}, u32[]{:S(2)}) copy-start(bf16[512,128]{1,0:T(8,128)(2,1)} %constant.107.clone.back_right) | copy-start | bytes 393220
  98.2 9.1 %copy-start.4 = (bf16[128,32]{1,0:T(8,128)(2,1)S(1)}, bf16[128,32]{1,0:T(8,128)(2,1)}, u32[]{:S(2)}) copy-start(bf16[128,32]{1,0:T(8,128)(2,1)} %constant.106.clone.back_left) | copy-start | bytes 24580
  98.3 9.1 %copy-start.5 = (bf16[128,32]{1,0:T(8,128)(2,1)S(1)}, bf16[128,32]{1,0:T(8,128)(2,1)}, u32[]{:S(2)}) copy-start(bf16[128,32]{1,0:T(8,128)(2,1)} %constant.104.clone.left) | copy-start | bytes 24580
  98.3 9.1 %copy-start.7 = (f32[32,128]{1,0:T(8,128)S(1)}, f32[32,128]{1,0:T(8,128)}, u32[]{:S(2)}) copy-start(f32[32,128]{1,0:T(8,128)} %constant.103.clone.lu) | copy-start | bytes 49156
  98.3 9.1 %copy-start.8 = (bf16[64,32]{1,0:T(8,128)(2,1)S(1)}, bf16[64,32]{1,0:T(8,128)(2,1)}, u32[]{:S(2)}) copy-start(bf16[64,32]{1,0:T(8,128)(2,1)} %constant.102.clone.lv) | copy-start | bytes 12292
  102.9 3.6 %collective-permute-start.3 = (f32[40,128]{1,0:T(8,128)}, f32[40,128]{1,0:T(8,128)S(1)}, u32[]{:S(2)}, u32[]{:S(2)}) collective-permute-start(f32[40,128]{1,0:T(8,128)} %get-tuple-element.40.p0), channel_id=1, source_target_pairs={{0,3},{1,0},{2,1},{3,2},{4,7},{5,4},{6,5},{7,6},{8,11},{9,8},{10,9... | collective-permute-start | bytes 61448 | tf_op jit(solution)/shard_map/ppermute | solution.py:648
  103.5 3.1 %collective-permute-start.2 = (f32[40,128]{1,0:T(8,128)}, f32[40,128]{1,0:T(8,128)S(1)}, u32[]{:S(2)}, u32[]{:S(2)}) collective-permute-start(f32[40,128]{1,0:T(8,128)} %get-tuple-element.40.p0), channel_id=1, source_target_pairs={{0,2},{1,3},{2,0},{3,1},{4,6},{5,7},{6,4},{7,5},{8,10},{9,11},{10,... | collective-permute-start | bytes 61448 | tf_op jit(solution)/shard_map/ppermute | solution.py:648
  104.8 2.5 %collective-permute-start.1 = (f32[40,128]{1,0:T(8,128)}, f32[40,128]{1,0:T(8,128)S(1)}, u32[]{:S(2)}, u32[]{:S(2)}) collective-permute-start(f32[40,128]{1,0:T(8,128)} %get-tuple-element.40.p0), channel_id=1, source_target_pairs={{0,1},{1,2},{2,3},{3,0},{4,5},{5,6},{6,7},{7,4},{8,9},{9,10},{10,1... | collective-permute-start | bytes 61448 | tf_op jit(solution)/shard_map/ppermute | solution.py:648
  107.4 0.7 copy-start.6
  108.1 14.4 %copy-start.11 = (f32[64,4096]{1,0:T(8,128)S(1)}, f32[64,4096]{1,0:T(8,128)}, u32[]{:S(2)}) copy-start(f32[64,4096]{1,0:T(8,128)} %variance.1) | copy-start | bytes 3145732
  108.1 14.4 %copy-start.14 = (f32[64,4096]{1,0:T(8,128)S(1)}, f32[64,4096]{1,0:T(8,128)}, u32[]{:S(2)}) copy-start(f32[64,4096]{1,0:T(8,128)} %get-tuple-element.49) | copy-start | bytes 3145732
  116.4 8.5 %collective-permute-start.6 = (f32[16,4096]{1,0:T(8,128)S(1)}, f32[16,4096]{1,0:T(8,128)S(1)}, u32[]{:S(2)}, u32[]{:S(2)}) collective-permute-start(f32[16,4096]{1,0:T(8,128)S(1)} %get-tuple-element.45), channel_id=1, source_target_pairs={{0,1},{1,2},{2,3},{3,4},{4,5},{5,6},{6,7},{7,8},{8,9},{9,10},{10,1... | collective-permute-start | bytes 786440 | tf_op jit(solution)/shard_map/ppermute | solution.py:541
  120.6 7.7 %collective-permute-start.7 = (f32[16,4096]{1,0:T(8,128)S(1)}, f32[16,4096]{1,0:T(8,128)S(1)}, u32[]{:S(2)}, u32[]{:S(2)}) collective-permute-start(f32[16,4096]{1,0:T(8,128)S(1)} %get-tuple-element.47), channel_id=1, source_target_pairs={{1,0},{2,1},{3,2},{4,3},{5,4},{6,5},{7,6},{8,7},{9,8},{10,9},{11,1... | collective-permute-start | bytes 786440 | tf_op jit(solution)/shard_map/ppermute | solution.py:542

commit v8 on v7

--- a/solution.py
+++ b/solution.py
@@ -471,7 +471,7 @@
                 [high, x - high, high, rest], 0
             ).astype(jnp.bfloat16)
         left_last, here, here_last, here_next = here_last, right, right_last, right_next
-    chunk = 384 if tiles % 3 == 0 else 128
+    chunk = 1408 if tiles % 11 == 0 else 128
     for c in range(0, tiles * 128, chunk):
         at = slice(c, c + chunk)
         products[:, at] = jnp.dot(bands[...], stack[:, at], preferred_element_type=jnp.float32)

time: 136 us -> 134 us (0.985)
  no operation moved by 1% of the time
where the time goes in v8:
time: 134 us; the launch traced here: 133 us
  waiting for transfers between devices  55.9 us (42%)
  Pallas kernels  36.7 us (27%)
  starting transfers between devices  32.8 us (24%)
  other arithmetic  3.71 us (3%)
  local copies, waits for them, and re-layouts  3.01 us (2%)
    ppermute x1, waiting for transfers between devices, per_device(): partner_blocks = lax.ppermute(template_blocks, 'det', across_halves)  38.5 us
    all_to_all x3, starting transfers between devices, serve(): return lax.all_to_all(x, 'det', 0, 0, axis_index_groups=halves, tiled=True)  15.6 us
    all_to_all x3, waiting for transfers between devices, serve(): return lax.all_to_all(x, 'det', 0, 0, axis_index_groups=halves, tiled=True)  12.9 us
    pallas_call x1, Pallas kernels, per_device(): pl.pallas_call(image_kernel, out_shape=[strip, edge, edge, jax.ShapeDtype...  8.63 us
    ppermute x2, starting transfers between devices, edges(): before = lax.ppermute(bottom, axis, up)  7.75 us
    pallas_call x1, Pallas kernels, per_device(): pl.pallas_call(functools.partial(first_kernel, pixels), out_shape=[strip,...  6.94 us
    pallas_call x2, Pallas kernels, pick(): pl.pallas_call(functools.partial(pick_kernel, plane), out_shape=jax.Shape...  5.46 us
    pallas_call x1, Pallas kernels, per_device(): pl.pallas_call(second_kernel, out_shape=strip, in_specs=[vmem] * 4, out_s...  5.23 us
  transfers between devices with their start and end apart: 11, of which 6 were waited for; matrix products, arithmetic and copies ran while one was open for 3% of the time, Pallas kernels for 14%

profile of v8, /device:TPU:1, one launch (start us, length us, event | category | flops | bytes accessed | tf_op | source)
XLA Modules:
  0.0 132.9 jit_solution(9756471415945079138)
XLA Ops:
  0.6 2.8 %pick_near_blocks.1 = f32[16,2,64,256]{3,2,1,0:T(8,128)} custom-call(s32[16,16]{1,0:T(8,128)} %requests.1, f32[8,2,64,256]{3,2,1,0:T(8,128)} %source.1), custom_call_target="tpu_custom_call" | custom-call | tf_op jit(solution)/shard_map/pick_near_blocks/pallas_call | solution.py:191
  3.5 5.3 %all-to-all-start = ((f32[16,2,64,256]{3,2,1,0:T(8,128)}), f32[16,2,64,256]{3,2,1,0:T(8,128)S(1)}, u32[]{:S(2)}, u32[]{:S(2)}) async-start(f32[16,2,64,256]{3,2,1,0:T(8,128)} %pick_near_blocks.1), calls=%async_computation | async-start | bytes 4194304 | tf_op jit(solution)/shard_map/all_to_all | solution.py:575
  8.8 2.3 %collective-permute-start = (f32[8,2,64,256]{3,2,1,0:T(8,128)}, f32[8,2,64,256]{3,2,1,0:T(8,128)S(1)}, u32[]{:S(2)}, u32[]{:S(2)}) collective-permute-start(f32[8,2,64,256]{3,2,1,0:T(8,128)} %source.1), channel_id=1, source_target_pairs={{0,8},{1,9},{2,10},{3,11},{4,12},{5,13},{6,14},{7,15},{8,0},{9,1},... | collective-permute-start | bytes 3145736 | tf_op jit(solution)/shard_map/ppermute | solution.py:577
  11.4 0.6 reshape.7.picks
  12.0 0.6 compare_convert_fusion
  12.6 2.8 %science_stamps.1 = (f32[128,128]{1,0:T(8,128)}, f32[128,128]{1,0:T(8,128)}, f32[8,128]{1,0:T(8,128)}) custom-call(s32[16]{0:T(128)} %bitcast.20, s32[16]{0:T(128)} %bitcast.23, f32[64,4096]{1,0:T(8,128)} %science.3, f32[64,4096]{1,0:T(8,128)} %variance.1), custom_call_target="tpu_custom_call" | custom-call | tf_op jit(solution)/shard_map/science_stamps/pallas_call | solution.py:591
  15.4 0.6 fusion.1.slots
  16.0 38.5 %collective-permute-done.source = f32[8,2,64,256]{3,2,1,0:T(8,128)S(1)} collective-permute-done((f32[8,2,64,256]{3,2,1,0:T(8,128)}, f32[8,2,64,256]{3,2,1,0:T(8,128)S(1)}, u32[]{:S(2)}, u32[]{:S(2)}) %collective-permute-start) | collective-permute-done | bytes 1048608 | tf_op jit(solution)/shard_map/ppermute | solution.py:577
  54.5 1.6 %all-to-all-done.near = f32[16,2,64,256]{3,2,1,0:T(8,128)S(1)} async-done(((f32[16,2,64,256]{3,2,1,0:T(8,128)}), f32[16,2,64,256]{3,2,1,0:T(8,128)S(1)}, u32[]{:S(2)}, u32[]{:S(2)}) %all-to-all-start) | async-done | bytes 2097184 | tf_op jit(solution)/shard_map/all_to_all | solution.py:575
  56.1 3.1 %pick_blocks.3 = f32[16,64,256]{2,1,0:T(8,128)} custom-call(s32[16]{0:T(128)} %reshape.7.picks, f32[8,2,64,256]{3,2,1,0:T(8,128)} %copy-done.10), custom_call_target="tpu_custom_call" | custom-call | tf_op jit(solution)/shard_map/pick_blocks/pallas_call | solution.py:151
  59.3 5.9 %all-to-all-start.1 = ((f32[16,64,256]{2,1,0:T(8,128)}), f32[16,64,256]{2,1,0:T(8,128)S(1)}, u32[]{:S(2)}, u32[]{:S(2)}) async-start(f32[16,64,256]{2,1,0:T(8,128)} %pick_blocks.3), calls=%async_computation.1 | async-start | bytes 2097152 | tf_op jit(solution)/shard_map/all_to_all | solution.py:575
  65.2 2.3 %pick_blocks.2 = f32[16,64,256]{2,1,0:T(8,128)} custom-call(s32[16]{0:T(128)} %reshape.7.picks, f32[8,2,64,256]{3,2,1,0:T(8,128)} %copy-done.10), custom_call_target="tpu_custom_call" | custom-call | tf_op jit(solution)/shard_map/pick_blocks/pallas_call | solution.py:151
  67.5 11.3 %all-to-all-done.1.far = f32[16,64,256]{2,1,0:T(8,128)S(1)} async-done(((f32[16,64,256]{2,1,0:T(8,128)}), f32[16,64,256]{2,1,0:T(8,128)S(1)}, u32[]{:S(2)}, u32[]{:S(2)}) %all-to-all-start.1) | async-done | bytes 1048608 | tf_op jit(solution)/shard_map/all_to_all | solution.py:575
  78.8 4.3 %all-to-all-start.2 = ((f32[16,64,256]{2,1,0:T(8,128)}), f32[16,64,256]{2,1,0:T(8,128)S(1)}, u32[]{:S(2)}, u32[]{:S(2)}) async-start(f32[16,64,256]{2,1,0:T(8,128)} %pick_blocks.2), calls=%async_computation.2 | async-start | bytes 2097152 | tf_op jit(solution)/shard_map/all_to_all | solution.py:575
  83.1 8.6 %stamp_images.1 = (f32[64,4096]{1,0:T(8,128)}, f32[16,4096]{1,0:T(8,128)}, f32[16,4096]{1,0:T(8,128)}, bf16[64,16384]{1,0:T(8,128)(2,1)}, f32[32,128]{1,0:T(8,128)}) custom-call(s32[16]{0:T(128)} %bitcast.21, s32[16]{0:T(128)} %bitcast.24, s32[16]{0:T(128)} %fusion.1.slots, s32[16]{0:T(128)} %get-tuple-element.30.is_near, f32[16,2,64,256]{3,2,1,0:T(8,128)} %copy-done.9, ...), custom_call_target="tpu_custom_call" | custom-call | tf_op jit(solution)/shard_map/stamp_images/pallas_call | solution.py:610
  91.8 3.5 %collective-permute-start.4 = (f32[16,4096]{1,0:T(8,128)}, f32[16,4096]{1,0:T(8,128)S(1)}, u32[]{:S(2)}, u32[]{:S(2)}) collective-permute-start(f32[16,4096]{1,0:T(8,128)} %get-tuple-element.41), channel_id=1, source_target_pairs={{0,1},{1,2},{2,3},{3,4},{4,5},{5,6},{6,7},{7,8},{8,9},{9,10},{10,1... | collective-permute-start | bytes 786440 | tf_op jit(solution)/shard_map/ppermute | solution.py:541
  95.3 1.9 %collective-permute-start.5 = (f32[16,4096]{1,0:T(8,128)}, f32[16,4096]{1,0:T(8,128)S(1)}, u32[]{:S(2)}, u32[]{:S(2)}) collective-permute-start(f32[16,4096]{1,0:T(8,128)} %get-tuple-element.43), channel_id=1, source_target_pairs={{1,0},{2,1},{3,2},{4,3},{5,4},{6,5},{7,6},{8,7},{9,8},{10,9},{11,1... | collective-permute-start | bytes 786440 | tf_op jit(solution)/shard_map/ppermute | solution.py:542
  97.3 1.0 copy-done.12
  98.3 4.8 %normal_equations.1 = (f32[64,4096]{1,0:T(8,128)}, f32[40,128]{1,0:T(8,128)}) custom-call(s32[16]{0:T(128)} %bitcast.22, s32[16]{0:T(128)} %bitcast.25, s32[16]{0:T(128)} %fusion.1.slots, s32[16]{0:T(128)} %get-tuple-element.30.is_near, f32[16,2,64,256]{3,2,1,0:T(8,128)} %copy-done.9, f32[16,64,256]{2,1,0:T(8,128)} %copy-done.12, ...), custom_call_target="tpu_custom_call" | custom-call | tf_op jit(solution)/shard_map/normal_equations/pallas_call | solution.py:631
  103.1 0.4 collective-permute-start.3
  103.5 1.5 %collective-permute-start.2 = (f32[40,128]{1,0:T(8,128)}, f32[40,128]{1,0:T(8,128)S(1)}, u32[]{:S(2)}, u32[]{:S(2)}) collective-permute-start(f32[40,128]{1,0:T(8,128)} %get-tuple-element.40.p0), channel_id=1, source_target_pairs={{0,2},{1,3},{2,0},{3,1},{4,6},{5,7},{6,4},{7,5},{8,10},{9,11},{10,... | collective-permute-start | bytes 61448 | tf_op jit(solution)/shard_map/ppermute | solution.py:648
  105.0 1.4 %collective-permute-start.1 = (f32[40,128]{1,0:T(8,128)}, f32[40,128]{1,0:T(8,128)S(1)}, u32[]{:S(2)}, u32[]{:S(2)}) collective-permute-start(f32[40,128]{1,0:T(8,128)} %get-tuple-element.40.p0), channel_id=1, source_target_pairs={{0,1},{1,2},{2,3},{3,0},{4,5},{5,6},{6,7},{7,4},{8,9},{9,10},{10,1... | collective-permute-start | bytes 61448 | tf_op jit(solution)/shard_map/ppermute | solution.py:648
  106.4 0.2 collective-permute-done.3.p3
  106.6 0.9 collective-permute-done.1.p1
  107.5 0.7 copy-done.6
  108.3 6.9 %solve_and_subtract.1 = (f32[64,4096]{1,0:T(8,128)S(1)}, f32[16,4096]{1,0:T(8,128)S(1)}, f32[16,4096]{1,0:T(8,128)S(1)}, f32[32,128]{1,0:T(8,128)S(1)}, f32[8,128]{1,0:T(8,128)S(1)}) custom-call(f32[40,128]{1,0:T(8,128)S(1)} %copy-done.6, f32[40,128]{1,0:T(8,128)S(1)} %collective-permute-done.1.p1, f32[40,128]{1,0:T(8,128)S(1)} %collective-permute-done.2.p2, ...), custom_call_target="tpu_custom_call" | custom-call | tf_op jit(solution)/shard_map/solve_and_subtract/pallas_call | solution.py:656
  115.2 0.6 fusion.2
  115.8 4.2 %collective-permute-start.6 = (f32[16,4096]{1,0:T(8,128)S(1)}, f32[16,4096]{1,0:T(8,128)S(1)}, u32[]{:S(2)}, u32[]{:S(2)}) collective-permute-start(f32[16,4096]{1,0:T(8,128)S(1)} %get-tuple-element.45), channel_id=1, source_target_pairs={{0,1},{1,2},{2,3},{3,4},{4,5},{5,6},{6,7},{7,8},{8,9},{9,10},{10,1... | collective-permute-start | bytes 786440 | tf_op jit(solution)/shard_map/ppermute | solution.py:541
  120.0 1.9 %collective-permute-start.7 = (f32[16,4096]{1,0:T(8,128)S(1)}, f32[16,4096]{1,0:T(8,128)S(1)}, u32[]{:S(2)}, u32[]{:S(2)}) collective-permute-start(f32[16,4096]{1,0:T(8,128)S(1)} %get-tuple-element.47), channel_id=1, source_target_pairs={{1,0},{2,1},{3,2},{4,3},{5,4},{6,5},{7,6},{8,7},{9,8},{10,9},{11,1... | collective-permute-start | bytes 786440 | tf_op jit(solution)/shard_map/ppermute | solution.py:542
  122.0 2.3 %add_multiply_fusion = f32[64,4096]{1,0:T(8,128)} fusion(f32[64,4096]{1,0:T(8,128)S(1)} %copy-done.11, f32[64,4096]{1,0:T(8,128)S(1)} %copy-done.14, f32[]{:T(128)} %bitcast.6, f32[]{:T(128)} %bitcast.5), kind=kLoop, calls=%fused_computation | loop fusion | flops 786432 | bytes 3145736 | tf_op jit(solution)/shard_map/mul | solution.py:672
  124.3 3.4 %collective-permute-done.7.after = f32[16,4096]{1,0:T(8,128)S(1)} collective-permute-done((f32[16,4096]{1,0:T(8,128)S(1)}, f32[16,4096]{1,0:T(8,128)S(1)}, u32[]{:S(2)}, u32[]{:S(2)}) %collective-permute-start.7) | collective-permute-done | bytes 262176 | tf_op jit(solution)/shard_map/ppermute | solution.py:542
  127.7 5.2 %decorrelate.1 = f32[64,4096]{1,0:T(8,128)} custom-call(f32[32,128]{1,0:T(8,128)S(1)} %get-tuple-element.44.filter_t, f32[16,4096]{1,0:T(8,128)S(1)} %collective-permute-done.6.before, f32[64,4096]{1,0:T(8,128)S(1)} %get-tuple-element.46.own, f32[16,4096]{1,0:T(8,128)S(1)} %collective-permute-done.7.after), custom_call_target="tpu_custom_call" | custom-call | tf_op jit(solution)/shard_map/decorrelate/pallas_call | solution.py:673
  (39 shorter events, 0.4 us)
Async XLA Ops:
  3.5 7.6 %copy-start.15 = (s32[16,16]{1,0:T(8,128)S(1)}, s32[16,16]{1,0:T(8,128)}, u32[]{:S(2)}) copy-start(s32[16,16]{1,0:T(8,128)} %requests.1) | copy-start | bytes 3076
  3.5 52.6 %all-to-all-start = ((f32[16,2,64,256]{3,2,1,0:T(8,128)}), f32[16,2,64,256]{3,2,1,0:T(8,128)S(1)}, u32[]{:S(2)}, u32[]{:S(2)}) async-start(f32[16,2,64,256]{3,2,1,0:T(8,128)} %pick_near_blocks.1), calls=%async_computation | async-start | bytes 4194304 | tf_op jit(solution)/shard_map/all_to_all | solution.py:575
  8.8 45.7 %collective-permute-start = (f32[8,2,64,256]{3,2,1,0:T(8,128)}, f32[8,2,64,256]{3,2,1,0:T(8,128)S(1)}, u32[]{:S(2)}, u32[]{:S(2)}) collective-permute-start(f32[8,2,64,256]{3,2,1,0:T(8,128)} %source.1), channel_id=1, source_target_pairs={{0,8},{1,9},{2,10},{3,11},{4,12},{5,13},{6,14},{7,15},{8,0},{9,1},... | collective-permute-start | bytes 3145736 | tf_op jit(solution)/shard_map/ppermute | solution.py:577
  54.5 1.6 %copy-start.10 = (f32[8,2,64,256]{3,2,1,0:T(8,128)}, f32[8,2,64,256]{3,2,1,0:T(8,128)S(1)}, u32[]{:S(2)}) copy-start(f32[8,2,64,256]{3,2,1,0:T(8,128)S(1)} %collective-permute-done.source) | copy-start | bytes 3145732
  56.1 3.1 %copy-start.9 = (f32[16,2,64,256]{3,2,1,0:T(8,128)}, f32[16,2,64,256]{3,2,1,0:T(8,128)S(1)}, u32[]{:S(2)}) copy-start(f32[16,2,64,256]{3,2,1,0:T(8,128)S(1)} %all-to-all-done.near) | copy-start | bytes 6291460
  59.3 19.5 %all-to-all-start.1 = ((f32[16,64,256]{2,1,0:T(8,128)}), f32[16,64,256]{2,1,0:T(8,128)S(1)}, u32[]{:S(2)}, u32[]{:S(2)}) async-start(f32[16,64,256]{2,1,0:T(8,128)} %pick_blocks.3), calls=%async_computation.1 | async-start | bytes 2097152 | tf_op jit(solution)/shard_map/all_to_all | solution.py:575
  78.8 4.3 %copy-start.13 = (f32[16,64,256]{2,1,0:T(8,128)}, f32[16,64,256]{2,1,0:T(8,128)S(1)}, u32[]{:S(2)}) copy-start(f32[16,64,256]{2,1,0:T(8,128)S(1)} %all-to-all-done.1.far) | copy-start | bytes 3145732
  78.8 18.5 %all-to-all-start.2 = ((f32[16,64,256]{2,1,0:T(8,128)}), f32[16,64,256]{2,1,0:T(8,128)S(1)}, u32[]{:S(2)}, u32[]{:S(2)}) async-start(f32[16,64,256]{2,1,0:T(8,128)} %pick_blocks.2), calls=%async_computation.2 | async-start | bytes 2097152 | tf_op jit(solution)/shard_map/all_to_all | solution.py:575
  91.8 14.6 %collective-permute-start.4 = (f32[16,4096]{1,0:T(8,128)}, f32[16,4096]{1,0:T(8,128)S(1)}, u32[]{:S(2)}, u32[]{:S(2)}) collective-permute-start(f32[16,4096]{1,0:T(8,128)} %get-tuple-element.41), channel_id=1, source_target_pairs={{0,1},{1,2},{2,3},{3,4},{4,5},{5,6},{6,7},{7,8},{8,9},{9,10},{10,1... | collective-permute-start | bytes 786440 | tf_op jit(solution)/shard_map/ppermute | solution.py:541
  95.3 11.0 %collective-permute-start.5 = (f32[16,4096]{1,0:T(8,128)}, f32[16,4096]{1,0:T(8,128)S(1)}, u32[]{:S(2)}, u32[]{:S(2)}) collective-permute-start(f32[16,4096]{1,0:T(8,128)} %get-tuple-element.43), channel_id=1, source_target_pairs={{1,0},{2,1},{3,2},{4,3},{5,4},{6,5},{7,6},{8,7},{9,8},{10,9},{11,1... | collective-permute-start | bytes 786440 | tf_op jit(solution)/shard_map/ppermute | solution.py:542
  97.3 1.0 copy-start.12
  98.2 9.2 %copy-start = (f32[64,4096]{1,0:T(8,128)S(1)}, f32[64,4096]{1,0:T(8,128)}, u32[]{:S(2)}) copy-start(f32[64,4096]{1,0:T(8,128)} %science.3) | copy-start | bytes 3145732
  98.2 9.2 %copy-start.1 = (f32[64,4096]{1,0:T(8,128)S(1)}, f32[64,4096]{1,0:T(8,128)}, u32[]{:S(2)}) copy-start(f32[64,4096]{1,0:T(8,128)} %get-tuple-element.42.own) | copy-start | bytes 3145732
  98.2 9.2 %copy-start.2 = (bf16[512,256]{1,0:T(8,128)(2,1)S(1)}, bf16[512,256]{1,0:T(8,128)(2,1)}, u32[]{:S(2)}) copy-start(bf16[512,256]{1,0:T(8,128)(2,1)} %constant.105.clone.right) | copy-start | bytes 786436
  98.2 9.2 %copy-start.3 = (bf16[512,128]{1,0:T(8,128)(2,1)S(1)}, bf16[512,128]{1,0:T(8,128)(2,1)}, u32[]{:S(2)}) copy-start(bf16[512,128]{1,0:T(8,128)(2,1)} %constant.107.clone.back_right) | copy-start | bytes 393220
  98.2 9.2 %copy-start.4 = (bf16[128,32]{1,0:T(8,128)(2,1)S(1)}, bf16[128,32]{1,0:T(8,128)(2,1)}, u32[]{:S(2)}) copy-start(bf16[128,32]{1,0:T(8,128)(2,1)} %constant.106.clone.back_left) | copy-start | bytes 24580
  98.3 9.2 %copy-start.5 = (bf16[128,32]{1,0:T(8,128)(2,1)S(1)}, bf16[128,32]{1,0:T(8,128)(2,1)}, u32[]{:S(2)}) copy-start(bf16[128,32]{1,0:T(8,128)(2,1)} %constant.104.clone.left) | copy-start | bytes 24580
  98.3 9.2 %copy-start.7 = (f32[32,128]{1,0:T(8,128)S(1)}, f32[32,128]{1,0:T(8,128)}, u32[]{:S(2)}) copy-start(f32[32,128]{1,0:T(8,128)} %constant.103.clone.lu) | copy-start | bytes 49156
  98.3 9.2 %copy-start.8 = (bf16[64,32]{1,0:T(8,128)(2,1)S(1)}, bf16[64,32]{1,0:T(8,128)(2,1)}, u32[]{:S(2)}) copy-start(bf16[64,32]{1,0:T(8,128)(2,1)} %constant.102.clone.lv) | copy-start | bytes 12292
  103.1 3.5 %collective-permute-start.3 = (f32[40,128]{1,0:T(8,128)}, f32[40,128]{1,0:T(8,128)S(1)}, u32[]{:S(2)}, u32[]{:S(2)}) collective-permute-start(f32[40,128]{1,0:T(8,128)} %get-tuple-element.40.p0), channel_id=1, source_target_pairs={{0,3},{1,0},{2,1},{3,2},{4,7},{5,4},{6,5},{7,6},{8,11},{9,8},{10,9... | collective-permute-start | bytes 61448 | tf_op jit(solution)/shard_map/ppermute | solution.py:648
  103.5 3.1 %collective-permute-start.2 = (f32[40,128]{1,0:T(8,128)}, f32[40,128]{1,0:T(8,128)S(1)}, u32[]{:S(2)}, u32[]{:S(2)}) collective-permute-start(f32[40,128]{1,0:T(8,128)} %get-tuple-element.40.p0), channel_id=1, source_target_pairs={{0,2},{1,3},{2,0},{3,1},{4,6},{5,7},{6,4},{7,5},{8,10},{9,11},{10,... | collective-permute-start | bytes 61448 | tf_op jit(solution)/shard_map/ppermute | solution.py:648
  105.0 2.5 %collective-permute-start.1 = (f32[40,128]{1,0:T(8,128)}, f32[40,128]{1,0:T(8,128)S(1)}, u32[]{:S(2)}, u32[]{:S(2)}) collective-permute-start(f32[40,128]{1,0:T(8,128)} %get-tuple-element.40.p0), channel_id=1, source_target_pairs={{0,1},{1,2},{2,3},{3,0},{4,5},{5,6},{6,7},{7,4},{8,9},{9,10},{10,1... | collective-permute-start | bytes 61448 | tf_op jit(solution)/shard_map/ppermute | solution.py:648
  107.5 0.7 copy-start.6
  108.3 13.7 %copy-start.11 = (f32[64,4096]{1,0:T(8,128)S(1)}, f32[64,4096]{1,0:T(8,128)}, u32[]{:S(2)}) copy-start(f32[64,4096]{1,0:T(8,128)} %variance.1) | copy-start | bytes 3145732
  108.3 13.7 %copy-start.14 = (f32[64,4096]{1,0:T(8,128)S(1)}, f32[64,4096]{1,0:T(8,128)}, u32[]{:S(2)}) copy-start(f32[64,4096]{1,0:T(8,128)} %get-tuple-element.49) | copy-start | bytes 3145732
  115.8 8.5 %collective-permute-start.6 = (f32[16,4096]{1,0:T(8,128)S(1)}, f32[16,4096]{1,0:T(8,128)S(1)}, u32[]{:S(2)}, u32[]{:S(2)}) collective-permute-start(f32[16,4096]{1,0:T(8,128)S(1)} %get-tuple-element.45), channel_id=1, source_target_pairs={{0,1},{1,2},{2,3},{3,4},{4,5},{5,6},{6,7},{7,8},{8,9},{9,10},{10,1... | collective-permute-start | bytes 786440 | tf_op jit(solution)/shard_map/ppermute | solution.py:541
  120.0 7.7 %collective-permute-start.7 = (f32[16,4096]{1,0:T(8,128)S(1)}, f32[16,4096]{1,0:T(8,128)S(1)}, u32[]{:S(2)}, u32[]{:S(2)}) collective-permute-start(f32[16,4096]{1,0:T(8,128)S(1)} %get-tuple-element.47), channel_id=1, source_target_pairs={{1,0},{2,1},{3,2},{4,3},{5,4},{6,5},{7,6},{8,7},{9,8},{10,9},{11,1... | collective-permute-start | bytes 786440 | tf_op jit(solution)/shard_map/ppermute | solution.py:542
